TPU v7x, 32 devices: a whole 2x2x4 slice. The times are simulated.
32 devices in a mesh: dp: 2 (over y), seq: 4 (over z), head: 4 (over x, core).
Axes of the slice: x: 2, y: 2, z: 4, core: 2. Of those that a mesh axis runs over, the one named last changes fastest.
Arguments:
- tokens: bfloat16 [2, 2048, 1536], P('dp', 'seq'), may hold values from -6 to 6
- cotangent: bfloat16 [2, 2048, 1536], P('dp', 'seq'), may hold values from -6 to 6
- doc_lengths: int32 [2, 2], P('dp'), may hold values from 0 to 2048, as said below
- queries_master: float32 [1536, 1536], P(('dp', 'seq'), 'head'), may hold values from -0.15625 to 0.15625
- queries_moment: float32 [1536, 1536], P(('dp', 'seq'), 'head'), may hold values from -512 to 512
- queries_square: float32 [1536, 1536], P(('dp', 'seq'), 'head'), may hold values from 9216 to 36864
- keyvalue_master: float32 [1536, 512], P(('dp', 'seq')), may hold values from -0.15625 to 0.15625
- keyvalue_moment: float32 [1536, 512], P(('dp', 'seq')), may hold values from -1024 to 1024
- keyvalue_square: float32 [1536, 512], P(('dp', 'seq')), may hold values from 36864 to 147456
- mixing_master: float32 [1536, 1536], P('head', ('dp', 'seq')), may hold values from -2.5 to 2.5
- mixing_moment: float32 [1536, 1536], P('head', ('dp', 'seq')), may hold values from -24 to 24
- mixing_square: float32 [1536, 1536], P('head', ('dp', 'seq')), may hold values from 16 to 64
- expand_master: float32 [1536, 2, 8960], P(('dp', 'seq'), None, 'head'), may hold values from -0.15625 to 0.15625
- expand_moment: float32 [1536, 2, 8960], P(('dp', 'seq'), None, 'head'), may hold values from -96 to 96
- expand_square: float32 [1536, 2, 8960], P(('dp', 'seq'), None, 'head'), may hold values from 256 to 1024
- shrink_master: float32 [8960, 1536], P('head', ('dp', 'seq')), may hold values from -0.0625 to 0.0625
- shrink_moment: float32 [8960, 1536], P('head', ('dp', 'seq')), may hold values from -192 to 192
- shrink_square: float32 [8960, 1536], P('head', ('dp', 'seq')), may hold values from 1024 to 4096
- scalars_master: float32 [5120], P(('dp', 'seq')), as said below
- scalars_moment: float32 [5120], P(('dp', 'seq')), may hold values from -384 to 384
- scalars_square: float32 [5120], P(('dp', 'seq')), may hold values from 4096 to 201326592
Outputs:
- layer_out: bfloat16 [2, 2048, 1536], P('dp', 'seq')
- input_grad: bfloat16 [2, 2048, 1536], P('dp', 'seq')
- queries_grad: float32 [1536, 1536], P(('dp', 'seq'), 'head')
- queries_first: float32 [1536, 1536], P(('dp', 'seq'), 'head')
- queries_second: float32 [1536, 1536], P(('dp', 'seq'), 'head')
- queries_weight: float32 [1536, 1536], P(('dp', 'seq'), 'head')
- queries_copy: bfloat16 [1536, 1536], P(('dp', 'seq'), 'head')
- keyvalue_grad: float32 [1536, 512], P(('dp', 'seq'))
- keyvalue_first: float32 [1536, 512], P(('dp', 'seq'))
- keyvalue_second: float32 [1536, 512], P(('dp', 'seq'))
- keyvalue_weight: float32 [1536, 512], P(('dp', 'seq'))
- keyvalue_copy: bfloat16 [1536, 512], P(('dp', 'seq'))
- mixing_grad: float32 [1536, 1536], P('head', ('dp', 'seq'))
- mixing_first: float32 [1536, 1536], P('head', ('dp', 'seq'))
- mixing_second: float32 [1536, 1536], P('head', ('dp', 'seq'))
- mixing_weight: float32 [1536, 1536], P('head', ('dp', 'seq'))
- mixing_copy: bfloat16 [1536, 1536], P('head', ('dp', 'seq'))
- expand_grad: float32 [1536, 2, 8960], P(('dp', 'seq'), None, 'head')
- expand_first: float32 [1536, 2, 8960], P(('dp', 'seq'), None, 'head')
- expand_second: float32 [1536, 2, 8960], P(('dp', 'seq'), None, 'head')
- expand_weight: float32 [1536, 2, 8960], P(('dp', 'seq'), None, 'head')
- expand_copy: bfloat16 [1536, 2, 8960], P(('dp', 'seq'), None, 'head')
- shrink_grad: float32 [8960, 1536], P('head', ('dp', 'seq'))
- shrink_first: float32 [8960, 1536], P('head', ('dp', 'seq'))
- shrink_second: float32 [8960, 1536], P('head', ('dp', 'seq'))
- shrink_weight: float32 [8960, 1536], P('head', ('dp', 'seq'))
- shrink_copy: bfloat16 [8960, 1536], P('head', ('dp', 'seq'))
- scalars_grad: float32 [5120], P(('dp', 'seq'))
- scalars_first: float32 [5120], P(('dp', 'seq'))
- scalars_second: float32 [5120], P(('dp', 'seq'))
- scalars_weight: float32 [5120], P(('dp', 'seq'))
- scalars_copy: bfloat16 [5120], P(('dp', 'seq'))
Inputs may be any that keep to these rules, and one draw needn't show every extreme that they name: `doc_lengths`: row b lists the lengths of batch b's packed sequences in order: multiples of 1024 that sum to 2048, followed by zeros; the first is longer than half of 2048; in one batch, picked from the seed, a single sequence fills all 2048 rows. `scalars_master`: the gains come first, each within 0.7 to 1.3; the biases follow.
All inputs are finite; a program needn't handle non-finite values.
Results may differ from a plain program's by a relative error of at most 0.025.
Values may be sent and summed in bfloat16 or wider, within the bound.
A program may use at most 256 MiB of HBM per device.

v0:
```python
import math

import jax
import jax.numpy as jnp
from jax import lax
from jax.sharding import PartitionSpec as P

D = 1536
H = 12
KV = 2
HD = 128
STEP = 5


norm_eps = 1e-06
rope_base = 1000000.0
beta_first = 0.5
beta_second = 0.5
adam_eps = 1e-08
masked_low = -1e30
learn_rates = (0.02, 0.02, 0.3, 0.02, 0.01, 0.2)
decay_rates = (0.1, 0.1, 0.1, 0.1, 0.1, 0.0)


def folded_places(row_ids, shard_rows, seq_count):
    owner_index = row_ids // shard_rows
    inside = row_ids % shard_rows
    halves = shard_rows // 2
    block_index = jnp.where(inside < halves, owner_index, 2 * seq_count - 1 - owner_index)
    return block_index * halves + inside % halves


def doc_starts(places, lengths):
    endings = jnp.cumsum(lengths)
    taken_lengths = jnp.where(endings[None, :] <= places[:, None], lengths[None, :], 0)
    return jnp.sum(taken_lengths, axis=1)


def rotate(values, places):
    halves = values.shape[-1] // 2
    powers = jnp.arange(halves, dtype=jnp.float32) * (-2.0 / values.shape[-1])
    frequency = jnp.power(jnp.float32(rope_base), powers)
    angles = places.astype(jnp.float32)[:, None] * frequency[None, :]
    cosine = jnp.cos(angles)[:, None, :]
    sine_term = jnp.sin(angles)[:, None, :]
    first_half = values[..., :halves]
    second_half = values[..., halves:]
    return jnp.concatenate(
        [
            first_half * cosine - second_half * sine_term,
            second_half * cosine + first_half * sine_term,
        ],
        axis=-1,
    )


def visibility(places, starts, key_places):
    return (key_places[None, :] <= places[:, None]) & (key_places[None, :] >= starts[:, None])


def attend_block(running, queries, places, starts, key_block, score_scale):
    running_max, running_sum, running_out = running
    block_keys, block_values, key_places = key_block
    visible = visibility(places, starts, key_places)[:, None, :]
    scores = (
        jnp.einsum("thd,kd->thk", queries, block_keys, preferred_element_type=jnp.float32)
        * score_scale
    )
    scores = jnp.where(visible, scores, masked_low)
    new_max = jnp.maximum(running_max, jnp.max(scores, axis=-1))
    attn_probs = jnp.where(visible, jnp.exp(scores - new_max[..., None]), 0.0)
    fade_factor = jnp.exp(running_max - new_max)
    running_sum = running_sum * fade_factor + jnp.sum(attn_probs, axis=-1)
    added = jnp.einsum(
        "thk,kd->thd",
        attn_probs.astype(jnp.bfloat16),
        block_values,
        preferred_element_type=jnp.float32,
    )
    running_out = running_out * fade_factor[..., None] + added
    return (new_max, running_sum, running_out)


def norm_back(grad_rows, values, scale_rows, gain_vector):
    unit_rows = values * scale_rows
    scaled = grad_rows * gain_vector
    mean_term = jnp.mean(scaled * unit_rows, axis=-1, keepdims=True)
    return (scale_rows * (scaled - unit_rows * mean_term), jnp.sum(grad_rows * unit_rows, axis=0))


def adamw(master, moment, square, grad_rows, rate_value, decay_value):
    first_new = beta_first * moment + (1.0 - beta_first) * grad_rows
    second_new = beta_second * square + (1.0 - beta_second) * grad_rows * grad_rows
    fix_first = 1.0 - beta_first**STEP
    fix_second = 1.0 - beta_second**STEP
    weight = master - rate_value * (
        first_new / fix_first / (jnp.sqrt(second_new / fix_second) + adam_eps)
        + decay_value * master
    )
    return (grad_rows, first_new, second_new, weight, weight.astype(jnp.bfloat16))


def local(
    tokens,
    cotangent,
    doc_lengths,
    queries_master,
    queries_moment,
    queries_square,
    keyvalue_master,
    keyvalue_moment,
    keyvalue_square,
    mixing_master,
    mixing_moment,
    mixing_square,
    expand_master,
    expand_moment,
    expand_square,
    shrink_master,
    shrink_moment,
    shrink_square,
    scalars_master,
    scalars_moment,
    scalars_square,
):
    local_rows = tokens.shape[1]
    seq_count = lax.axis_size("seq")
    head_count = lax.axis_size("head")
    head_index = lax.axis_index("head")
    seq_index = lax.axis_index("seq")
    local_heads = H // head_count
    wide_heads = local_heads * HD
    kv_head = head_index * local_heads // (H // KV)
    kv_cols = 2 * KV * HD // head_count
    kv_begin = head_index * kv_cols
    score_scale = 1.0 / math.sqrt(HD)
    query_low = queries_master.astype(jnp.bfloat16)
    keyvalue_low = keyvalue_master.astype(jnp.bfloat16)
    mixing_low = mixing_master.astype(jnp.bfloat16)
    expand_low = expand_master.astype(jnp.bfloat16)
    shrink_low = shrink_master.astype(jnp.bfloat16)
    scalars_low = scalars_master.astype(jnp.bfloat16)
    gathered = (
        lax.all_gather(query_low, ("dp", "seq"), axis=0, tiled=True),
        lax.all_gather(keyvalue_low, ("dp", "seq"), axis=0, tiled=True),
        lax.all_gather(mixing_low, ("dp", "seq"), axis=1, tiled=True),
        lax.all_gather(expand_low, ("dp", "seq"), axis=0, tiled=True),
        lax.all_gather(shrink_low, ("dp", "seq"), axis=1, tiled=True),
        lax.all_gather(scalars_low, ("dp", "seq"), axis=0, tiled=True),
    )
    query_weight, keyvalue_weight, mixing_weight, expand_weight, shrink_weight, scalars_all = (
        gathered
    )
    scalar_values = scalars_all.astype(jnp.float32)
    gain_one = scalar_values[:D]
    gain_two = scalar_values[D : 2 * D]
    bias_query = lax.dynamic_slice_in_dim(
        scalar_values, 2 * D + head_index * wide_heads, wide_heads
    )
    bias_keyvalue = scalar_values[2 * D + H * HD :]
    key_bias = lax.dynamic_slice_in_dim(bias_keyvalue, kv_head * HD, HD)
    value_bias = lax.dynamic_slice_in_dim(bias_keyvalue, KV * HD + kv_head * HD, HD)
    x_rows = tokens[0].astype(jnp.float32)
    lengths = doc_lengths[0]
    places = folded_places(
        seq_index * local_rows + jnp.arange(local_rows, dtype=jnp.int32), local_rows, seq_count
    )
    starts = doc_starts(places, lengths)
    within = places - starts
    scale_one = lax.rsqrt(jnp.mean(x_rows * x_rows, axis=-1, keepdims=True) + norm_eps)
    normed = (x_rows * scale_one * gain_one).astype(jnp.bfloat16)
    query_pre = jnp.dot(normed, query_weight, preferred_element_type=jnp.float32) + bias_query
    queries = rotate(query_pre.reshape(local_rows, local_heads, HD), within).astype(jnp.bfloat16)
    key_weight = lax.dynamic_slice_in_dim(keyvalue_weight, kv_head * HD, HD, 1)
    value_weight = lax.dynamic_slice_in_dim(keyvalue_weight, KV * HD + kv_head * HD, HD, 1)
    key_pre = jnp.dot(normed, key_weight, preferred_element_type=jnp.float32) + key_bias
    key_rows = rotate(key_pre[:, None, :], within)[:, 0, :].astype(jnp.bfloat16)
    value_rows = (
        jnp.dot(normed, value_weight, preferred_element_type=jnp.float32) + value_bias
    ).astype(jnp.bfloat16)
    initial = (
        jnp.full((local_rows, local_heads), masked_low, jnp.float32),
        jnp.zeros((local_rows, local_heads), jnp.float32),
        jnp.zeros((local_rows, local_heads, HD), jnp.float32),
    )
    running = initial
    piece_keys = lax.all_gather(key_rows, "seq", axis=0, tiled=True)
    piece_values = lax.all_gather(value_rows, "seq", axis=0, tiled=True)
    piece_count = piece_keys.shape[0]
    block_width = 512
    block_count = piece_count // block_width
    key_places = folded_places(jnp.arange(piece_count, dtype=jnp.int32), local_rows, seq_count)

    def fold_step(carried, key_block):
        return (attend_block(carried, queries, places, starts, key_block, score_scale), None)

    blocks = (
        piece_keys.reshape(block_count, block_width, HD),
        piece_values.reshape(block_count, block_width, HD),
        key_places.reshape(block_count, block_width),
    )
    running, unused = lax.scan(fold_step, running, blocks)
    running_max, running_sum, running_out = running
    attended = running_out / running_sum[..., None]
    log_total = running_max + jnp.log(running_sum)
    attended_low = attended.reshape(local_rows, wide_heads).astype(jnp.bfloat16)
    branch = lax.psum(
        jnp.dot(attended_low, mixing_weight, preferred_element_type=jnp.float32).astype(
            jnp.bfloat16
        ),
        "head",
    ).astype(jnp.float32)
    hidden = x_rows + branch
    scale_two = lax.rsqrt(jnp.mean(hidden * hidden, axis=-1, keepdims=True) + norm_eps)
    normed_two = (hidden * scale_two * gain_two).astype(jnp.bfloat16)
    gate_weight = expand_weight[:, 0, :]
    up_weight = expand_weight[:, 1, :]
    gate_value = jnp.dot(normed_two, gate_weight, preferred_element_type=jnp.float32)
    up_value = jnp.dot(normed_two, up_weight, preferred_element_type=jnp.float32)
    gate_sigmoid = jax.nn.sigmoid(gate_value)
    activation = (gate_value * gate_sigmoid * up_value).astype(jnp.bfloat16)
    feedforward = lax.psum(
        jnp.dot(activation, shrink_weight, preferred_element_type=jnp.float32).astype(jnp.bfloat16),
        "head",
    ).astype(jnp.float32)
    layer_out = (hidden + feedforward).astype(jnp.bfloat16)
    cot_low = cotangent[0]
    act_grad = jnp.dot(cot_low, shrink_weight.T, preferred_element_type=jnp.float32).astype(
        jnp.bfloat16
    )
    act_float = act_grad.astype(jnp.float32)
    gate_grad = (
        act_float * up_value * gate_sigmoid * (1.0 + gate_value * (1.0 - gate_sigmoid))
    ).astype(jnp.bfloat16)
    upper_grad = (act_float * gate_value * gate_sigmoid).astype(jnp.bfloat16)
    shrink_grad = jnp.dot(activation.T, cot_low, preferred_element_type=jnp.float32)
    expand_grad = jnp.stack(
        [
            jnp.dot(normed_two.T, gate_grad, preferred_element_type=jnp.float32),
            jnp.dot(normed_two.T, upper_grad, preferred_element_type=jnp.float32),
        ],
        axis=1,
    )
    norm_two_part = jnp.dot(gate_grad, gate_weight.T, preferred_element_type=jnp.float32) + jnp.dot(
        upper_grad, up_weight.T, preferred_element_type=jnp.float32
    )
    norm_two_grad = lax.psum(norm_two_part.astype(jnp.bfloat16), "head").astype(jnp.float32)
    back_two, gain_two_grad = norm_back(norm_two_grad, hidden, scale_two, gain_two)
    hidden_grad = cot_low.astype(jnp.float32) + back_two
    branch_grad = hidden_grad.astype(jnp.bfloat16)
    mixing_grad = jnp.dot(attended_low.T, branch_grad, preferred_element_type=jnp.float32)
    attended_grad = (
        jnp.dot(branch_grad, mixing_weight.T, preferred_element_type=jnp.float32)
        .astype(jnp.bfloat16)
        .reshape(local_rows, local_heads, HD)
    )
    attended_float = attended_grad.astype(jnp.float32)
    row_delta = jnp.sum(attended_float * attended, axis=-1)
    all_keys, all_values = (
        lax.all_gather(key_rows, "seq", axis=0, tiled=True),
        lax.all_gather(value_rows, "seq", axis=0, tiled=True),
    )
    stream_rows = local_rows * seq_count
    block_width = 512
    block_count = stream_rows // block_width
    stream_places = folded_places(jnp.arange(stream_rows, dtype=jnp.int32), local_rows, seq_count)

    def back_step(query_sum, key_block):
        block_keys, block_values, key_places = key_block
        visible = visibility(places, starts, key_places)[:, None, :]
        scores = (
            jnp.einsum("thd,kd->thk", queries, block_keys, preferred_element_type=jnp.float32)
            * score_scale
        )
        attn_probs = jnp.where(visible, jnp.exp(scores - log_total[..., None]), 0.0)
        probs_low = attn_probs.astype(jnp.bfloat16)
        prob_grad = jnp.einsum(
            "thd,kd->thk", attended_grad, block_values, preferred_element_type=jnp.float32
        )
        score_grad = (attn_probs * (prob_grad - row_delta[..., None])).astype(jnp.bfloat16)
        query_sum = query_sum + jnp.einsum(
            "thk,kd->thd", score_grad, block_keys, preferred_element_type=jnp.float32
        )
        key_part = (
            jnp.einsum("thk,thd->kd", score_grad, queries, preferred_element_type=jnp.float32)
            * score_scale
        )
        value_part = jnp.einsum(
            "thk,thd->kd", probs_low, attended_grad, preferred_element_type=jnp.float32
        )
        return (query_sum, (key_part, value_part))

    blocks = (
        all_keys.reshape(block_count, block_width, HD),
        all_values.reshape(block_count, block_width, HD),
        stream_places.reshape(block_count, block_width),
    )
    query_sum, (key_parts, value_parts) = lax.scan(
        back_step, jnp.zeros((local_rows, local_heads, HD), jnp.float32), blocks
    )
    key_sums, value_sums = (
        lax.psum_scatter(
            key_parts.reshape(stream_rows, HD).astype(jnp.bfloat16),
            "seq",
            scatter_dimension=0,
            tiled=True,
        ).astype(jnp.float32),
        lax.psum_scatter(
            value_parts.reshape(stream_rows, HD).astype(jnp.bfloat16),
            "seq",
            scatter_dimension=0,
            tiled=True,
        ).astype(jnp.float32),
    )
    placed = jnp.zeros((local_rows, 2, KV, HD), jnp.float32)
    placed = lax.dynamic_update_slice(
        placed, jnp.stack([key_sums, value_sums], axis=1)[:, :, None, :], (0, 0, kv_head, 0)
    )
    placed = lax.psum(placed.astype(jnp.bfloat16), "head").astype(jnp.float32)
    key_back = rotate(placed[:, 0], -within).astype(jnp.bfloat16)
    value_back = placed[:, 1].astype(jnp.bfloat16)
    keyvalue_rows = jnp.concatenate(
        [key_back.reshape(local_rows, KV * HD), value_back.reshape(local_rows, KV * HD)], axis=1
    )
    query_grad = (
        rotate(query_sum * score_scale, -within)
        .reshape(local_rows, wide_heads)
        .astype(jnp.bfloat16)
    )
    keyvalue_slice = lax.dynamic_slice_in_dim(keyvalue_rows, kv_begin, kv_cols, 1)
    weight_slice = lax.dynamic_slice_in_dim(keyvalue_weight, kv_begin, kv_cols, 1)
    norm_one_part = jnp.dot(
        query_grad, query_weight.T, preferred_element_type=jnp.float32
    ) + jnp.dot(keyvalue_slice, weight_slice.T, preferred_element_type=jnp.float32)
    norm_one_grad = lax.psum(norm_one_part.astype(jnp.bfloat16), "head").astype(jnp.float32)
    back_one, gain_one_grad = norm_back(norm_one_grad, x_rows, scale_one, gain_one)
    input_grad = (hidden_grad + back_one).astype(jnp.bfloat16)
    queries_grad = jnp.dot(normed.T, query_grad, preferred_element_type=jnp.float32)
    keyvalue_grad = lax.dynamic_update_slice(
        jnp.zeros((normed.shape[1], 2 * KV * HD), jnp.float32),
        jnp.dot(normed.T, keyvalue_slice, preferred_element_type=jnp.float32),
        (0, kv_begin),
    )
    leading = (head_index == 0).astype(jnp.float32)
    small_total = scalar_values.shape[0]
    scalars_grad = jnp.zeros((small_total,), jnp.float32)
    scalars_grad = lax.dynamic_update_slice(
        scalars_grad, jnp.concatenate([gain_one_grad, gain_two_grad]) * leading, (0,)
    )
    scalars_grad = lax.dynamic_update_slice(
        scalars_grad,
        jnp.sum(query_grad.astype(jnp.float32), axis=0),
        (2 * D + head_index * wide_heads,),
    )
    scalars_grad = lax.dynamic_update_slice(
        scalars_grad,
        jnp.sum(keyvalue_slice.astype(jnp.float32), axis=0),
        (2 * D + H * HD + kv_begin,),
    )
    reduced = (
        lax.psum_scatter(
            queries_grad.astype(jnp.bfloat16), ("dp", "seq"), scatter_dimension=0, tiled=True
        ).astype(jnp.float32),
        lax.psum_scatter(
            keyvalue_grad.astype(jnp.bfloat16), ("dp", "seq"), scatter_dimension=0, tiled=True
        ).astype(jnp.float32),
        lax.psum_scatter(
            mixing_grad.astype(jnp.bfloat16), ("dp", "seq"), scatter_dimension=1, tiled=True
        ).astype(jnp.float32),
        lax.psum_scatter(
            expand_grad.astype(jnp.bfloat16), ("dp", "seq"), scatter_dimension=0, tiled=True
        ).astype(jnp.float32),
        lax.psum_scatter(
            shrink_grad.astype(jnp.bfloat16), ("dp", "seq"), scatter_dimension=1, tiled=True
        ).astype(jnp.float32),
        lax.psum_scatter(
            scalars_grad.astype(jnp.bfloat16), ("dp", "seq"), scatter_dimension=0, tiled=True
        ).astype(jnp.float32),
    )
    shared_keyvalue, shared_scalars = (
        lax.psum(reduced[1].astype(jnp.bfloat16), "head").astype(jnp.float32),
        lax.psum(reduced[5].astype(jnp.bfloat16), "head").astype(jnp.float32),
    )
    query_out = adamw(
        queries_master, queries_moment, queries_square, reduced[0], learn_rates[0], decay_rates[0]
    )
    keyvalue_out = adamw(
        keyvalue_master,
        keyvalue_moment,
        keyvalue_square,
        shared_keyvalue,
        learn_rates[1],
        decay_rates[1],
    )
    mixing_out = adamw(
        mixing_master, mixing_moment, mixing_square, reduced[2], learn_rates[2], decay_rates[2]
    )
    expand_out = adamw(
        expand_master, expand_moment, expand_square, reduced[3], learn_rates[3], decay_rates[3]
    )
    shrink_out = adamw(
        shrink_master, shrink_moment, shrink_square, reduced[4], learn_rates[4], decay_rates[4]
    )
    scalars_out = adamw(
        scalars_master,
        scalars_moment,
        scalars_square,
        shared_scalars,
        learn_rates[5],
        decay_rates[5],
    )
    return (
        layer_out[None],
        input_grad[None],
        query_out[0],
        query_out[1],
        query_out[2],
        query_out[3],
        query_out[4],
        keyvalue_out[0],
        keyvalue_out[1],
        keyvalue_out[2],
        keyvalue_out[3],
        keyvalue_out[4],
        mixing_out[0],
        mixing_out[1],
        mixing_out[2],
        mixing_out[3],
        mixing_out[4],
        expand_out[0],
        expand_out[1],
        expand_out[2],
        expand_out[3],
        expand_out[4],
        shrink_out[0],
        shrink_out[1],
        shrink_out[2],
        shrink_out[3],
        shrink_out[4],
        scalars_out[0],
        scalars_out[1],
        scalars_out[2],
        scalars_out[3],
        scalars_out[4],
    )


def solution(mesh):
    placed = (
        P("dp", "seq", None),
        P("dp", "seq", None),
        P("dp", None),
        P(("dp", "seq"), "head"),
        P(("dp", "seq"), "head"),
        P(("dp", "seq"), "head"),
        P(("dp", "seq"), None),
        P(("dp", "seq"), None),
        P(("dp", "seq"), None),
        P("head", ("dp", "seq")),
        P("head", ("dp", "seq")),
        P("head", ("dp", "seq")),
        P(("dp", "seq"), None, "head"),
        P(("dp", "seq"), None, "head"),
        P(("dp", "seq"), None, "head"),
        P("head", ("dp", "seq")),
        P("head", ("dp", "seq")),
        P("head", ("dp", "seq")),
        P(("dp", "seq")),
        P(("dp", "seq")),
        P(("dp", "seq")),
    )
    return jax.shard_map(
        local,
        mesh=mesh,
        in_specs=placed,
        out_specs=(
            P("dp", "seq", None),
            P("dp", "seq", None),
            P(("dp", "seq"), "head"),
            P(("dp", "seq"), "head"),
            P(("dp", "seq"), "head"),
            P(("dp", "seq"), "head"),
            P(("dp", "seq"), "head"),
            P(("dp", "seq"), None),
            P(("dp", "seq"), None),
            P(("dp", "seq"), None),
            P(("dp", "seq"), None),
            P(("dp", "seq"), None),
            P("head", ("dp", "seq")),
            P("head", ("dp", "seq")),
            P("head", ("dp", "seq")),
            P("head", ("dp", "seq")),
            P("head", ("dp", "seq")),
            P(("dp", "seq"), None, "head"),
            P(("dp", "seq"), None, "head"),
            P(("dp", "seq"), None, "head"),
            P(("dp", "seq"), None, "head"),
            P(("dp", "seq"), None, "head"),
            P("head", ("dp", "seq")),
            P("head", ("dp", "seq")),
            P("head", ("dp", "seq")),
            P("head", ("dp", "seq")),
            P("head", ("dp", "seq")),
            P(("dp", "seq")),
            P(("dp", "seq")),
            P(("dp", "seq")),
            P(("dp", "seq")),
            P(("dp", "seq")),
        ),
        check_vma=False,
    )
```

profile of v0, /device:TPU:0, one launch (start us, length us, event | category | flops | bytes accessed | tf_op | source)
XLA Modules:
  0.0 1685.2 jit_solution(9911382698328730269)
XLA Ops:
  13.9 32.2 %all-gather.1 = bf16[8,1,640]{2,1,0:T(2,128)(2,1)S(1)} all-gather(bf16[1,1,640]{2,1,0:T(2,128)(2,1)S(1)} %reshape.496), channel_id=1, replica_groups=mesh['dp'=2,'seq'=4,'head'=4] {'dp','seq'}, dimensions={0}, use_global_device_ids=true | all-gather | bytes 11520 | tf_op jit(solution)/shard_map/all_gather | solution.py:149
  58.9 41.3 %all-gather.8.cloned.1.call-done = bf16[1536,512]{1,0:T(8,128)(2,1)} async-done(((bf16[192,512]{1,0:T(8,128)(2,1)}), bf16[1536,512]{1,0:T(8,128)(2,1)}) %all-gather.8.cloned.1.call-update) | async-done | bytes 1572880 | tf_op jit(solution)/shard_map/all_gather | solution.py:145
  102.6 17.8 %all-gather = bf16[2048,1,128]{0,2,1:T(8,128)(2,1)S(1)} all-gather(bf16[512,1,128]{0,2,1:T(8,128)(2,1)S(1)} %pad_maximum_fusion.3), channel_id=2, replica_groups=mesh['dp'=2,'seq'=4,'head'=4] {'seq'}, dimensions={0}, use_global_device_ids=true | all-gather | bytes 655360 | tf_op jit(solution)/shard_map/all_gather | solution.py:187
  123.1 19.2 %all_gather.30 = bf16[2048,128]{1,0:T(8,128)(2,1)} all-gather(bf16[512,128]{1,0:T(8,128)(2,1)S(1)} %fusion.117), channel_id=1, replica_groups=mesh['dp'=2,'seq'=4,'head'=4] {'seq'}, dimensions={0}, use_global_device_ids=true | all-gather | bytes 655360 | tf_op jit(solution)/shard_map/all_gather | solution.py:188
  142.3 34.3 %while.30 = (s32[]{:T(128)}, f32[512,3]{0,1:T(4,128)S(1)}, f32[512,3]{0,1:T(4,128)}, f32[512,3,128]{2,0,1:T(8,128)}, s32[4,512]{1,0:T(4,128)}, /*index=5*/s32[51...) while((s32[]{:T(128)}, f32[512,3]{0,1:T(4,128)S(1)}, ...), condition=%wide.region_6.7_spmd.clone, body=%wide.region_3.6_spmd.clone.sunk | while | flops 414279168 | bytes 19181888 | solution.py:202
  188.3 10.7 all-reduce.12.cloned.1.call-start
  199.1 25.1 %all-reduce.10.cloned.1.call-done = bf16[512,1536]{1,0:T(8,128)(2,1)} async-done(((bf16[512,1536]{1,0:T(8,128)(2,1)}), bf16[512,1536]{1,0:T(8,128)(2,1)}) %all-reduce.10.cloned.1.call-update) | async-done | bytes 1572880 | tf_op jit(solution)/shard_map/psum | solution.py:207
  228.6 107.0 %all-gather.16.cloned.1.call-done = bf16[2240,1536]{0,1:T(8,128)(2,1)} async-done(((bf16[2240,192]{0,1:T(8,128)(2,1)}), bf16[2240,1536]{0,1:T(8,128)(2,1)}) %all-gather.16.cloned.1.call-update) | async-done | bytes 6881296 | tf_op jit(solution)/shard_map/all_gather | solution.py:148
  335.6 8.6 convolution_convert_fusion.3
  344.2 187.7 %all-gather.14.cloned.1.call-done = bf16[1536,2,2240]{2,1,0:T(2,128)(2,1)} async-done(((bf16[192,2,2240]{2,1,0:T(2,128)(2,1)}), bf16[1536,2,2240]{2,1,0:T(2,128)(2,1)}) %all-gather.14.cloned.1.call-update) | async-done | bytes 13762576 | tf_op jit(solution)/shard_map/all_gather | solution.py:147
  532.0 28.2 %fusion.171 = (bf16[1536,1,2240]{2,1,0:T(2,128)(2,1)}, bf16[1536,1,2240]{2,1,0:T(2,128)(2,1)}) fusion(bf16[1536,2,2240]{2,1,0:T(2,128)(2,1)} %all-gather.14.cloned.1.call-done), kind=kLoop, calls=%fused_computation.287 | loop fusion | bytes 27525120 | tf_op jit(solution)/shard_map/slice | solution.py:216
  560.2 30.6 %copy.159 = bf16[1536,1,2240]{0,2,1:T(8,128)(2,1)} copy(bf16[1536,1,2240]{2,1,0:T(2,128)(2,1)} %get-tuple-element.544) | data formatting | bytes 13762560
  590.8 30.8 %copy.158 = bf16[1536,1,2240]{0,2,1:T(8,128)(2,1)} copy(bf16[1536,1,2240]{2,1,0:T(2,128)(2,1)} %get-tuple-element.543) | data formatting | bytes 13762560
  621.6 6.6 fusion.68
  632.3 8.1 fusion.72
  648.0 40.1 %all-reduce.12.cloned.1.call-done = bf16[512,1536]{1,0:T(8,128)(2,1)} async-done(((bf16[512,1536]{1,0:T(8,128)(2,1)}), bf16[512,1536]{1,0:T(8,128)(2,1)}) %all-reduce.12.cloned.1.call-update) | async-done | bytes 1572880 | tf_op jit(solution)/shard_map/psum | solution.py:247
  697.0 42.2 %while.31 = (s32[]{:T(128)}, f32[512,3,128]{2,0,1:T(8,128)}, bf16[4,512,128]{2,1,0:T(8,128)(2,1)}, bf16[4,512,128]{2,1,0:T(8,128)(2,1)}, s32[4,512]{1,0:T(4,128)...) while((s32[]{:T(128)}, f32[512,3,128]{2,0,1:T(8,128)}, ...), condition=%wide.region_14.15_spmd.clone, body=%wide.region_13.14_spmd.clone.sunk | while | flops 1015760896 | bytes 53715436 | solution.py:298
  743.5 19.7 %reduce-scatter.9.cloned.1.call-done = bf16[512,128]{0,1:T(8,128)(2,1)} async-done(((bf16[2048,128]{0,1:T(8,128)(2,1)}), bf16[512,128]{0,1:T(8,128)(2,1)}) %reduce-scatter.9.cloned.1.call-update) | async-done | bytes 131088 | tf_op jit(solution)/shard_map/reduce_scatter | solution.py:308
  763.1 22.8 %reduce-scatter.7.cloned.1.call-done = bf16[512,128]{0,1:T(8,128)(2,1)} async-done(((bf16[2048,128]{0,1:T(8,128)(2,1)}), bf16[512,128]{0,1:T(8,128)(2,1)}) %reduce-scatter.7.cloned.1.call-update) | async-done | bytes 131088 | tf_op jit(solution)/shard_map/reduce_scatter | solution.py:302
  787.9 32.3 %all-reduce.14.cloned.1.call-done = bf16[512,2,2,128]{0,3,2,1:T(8,128)(2,1)} async-done(((bf16[512,2,2,128]{0,3,2,1:T(8,128)(2,1)}), bf16[512,2,2,128]{0,3,2,1:T(8,128)(2,1)}) %all-reduce.14.cloned.1.call-update) | async-done | bytes 524304 | tf_op jit(solution)/shard_map/psum | solution.py:319
  832.8 8.9 convolution_convert_fusion.4
  841.7 9.7 fusion.61
  855.3 34.7 %reduce-scatter.13.cloned.1.call-done = bf16[192,512]{1,0:T(8,128)(2,1)} async-done(((bf16[1536,512]{1,0:T(8,128)(2,1)}), bf16[192,512]{1,0:T(8,128)(2,1)}) %reduce-scatter.13.cloned.1.call-update) | async-done | bytes 196624 | tf_op jit(solution)/shard_map/reduce_scatter | solution.py:364
  895.6 9.1 pad_maximum_fusion
  904.8 35.3 %copy.140 = bf16[1536,2,2240]{2,1,0:T(2,128)(2,1)} copy(bf16[1536,2,2240]{0,2,1:T(8,128)(2,1)} %pad_maximum_fusion) | data formatting | bytes 27525120 | tf_op jit(solution)/shard_map/stack | solution.py:237
  941.4 7.5 convolution_convert_fusion.2
  959.2 65.3 %reduce-scatter.15.cloned.1.call-done = bf16[384,192]{0,1:T(8,128)(2,1)} async-done(((bf16[384,1536]{0,1:T(8,128)(2,1)}), bf16[384,192]{0,1:T(8,128)(2,1)}) %reduce-scatter.15.cloned.1.call-update) | async-done | bytes 147472 | tf_op jit(solution)/shard_map/reduce_scatter | solution.py:367
  1026.7 72.6 %all-reduce.18.cloned.1.call-done = (bf16[512,1536]{1,0:T(8,128)(2,1)}, bf16[512,1536]{1,0:T(8,128)(2,1)}, bf16[192,512]{1,0:T(8,128)(2,1)}) async-done(((bf16[512,1536]{1,0:T(8,128)(2,1)}, bf16[512,1536]{1,0:T(8,128)(2,1)}, bf16[192,512]{1,0:T(8,128)(2,1)}), (bf16[512,1536]{1,0:T(8,128)(2,1)}, bf16[512,1536]{1,0:T(8,128)(2,1)}, bf16[192,512]{1,0:T(8,128)(2,1)})) %all-reduce.18.cloned.1.call-update) | async-done | bytes 3342352 | tf_op jit(solution)/shard_map/psum | solution.py:222
  1107.1 39.4 %all-reduce.2 = bf16[5120]{0:T(1024)(128)(2,1)} all-reduce(bf16[5120]{0:T(1024)(128)(2,1)} %convert_element_type.310), channel_id=10, replica_groups=mesh['dp'=2,'seq'=4,'head'=4] {'dp','seq'}, use_global_device_ids=true, to_apply=%region_30.31.clone | all-reduce | flops 5120 | bytes 20480
  1147.3 6.4 psum.55
  1163.6 377.8 %all-reduce.16.cloned.1.call-done = bf16[1536,2,2240]{2,1,0:T(2,128)(2,1)} async-done(((bf16[1536,2,2240]{2,1,0:T(2,128)(2,1)}), bf16[1536,2,2240]{2,1,0:T(2,128)(2,1)}) %all-reduce.16.cloned.1.call-update) | async-done | bytes 13762576
  1568.3 104.7 %reduce-scatter.17.cloned.1.call-done = bf16[2240,192]{0,1:T(8,128)(2,1)} async-done(((bf16[2240,1536]{0,1:T(8,128)(2,1)}), bf16[2240,192]{0,1:T(8,128)(2,1)}) %reduce-scatter.17.cloned.1.call-update) | async-done | bytes 860176 | tf_op jit(solution)/shard_map/reduce_scatter | solution.py:373
  (458 shorter events, 227.7 us)
Async XLA Ops:
  7.2 40.9 %copy-start.69 = (s32[1,2]{1,0:T(1,128)S(1)}, s32[1,2]{1,0:T(1,128)}, u32[]{:S(2)}) copy-start(s32[1,2]{1,0:T(1,128)} %param.27) | copy-start | bytes 28
  7.2 47.3 %all-gather.10.cloned.1.call-start = ((), (), s32[]{:S(2)}) async-start(), calls=%async_computation.7 | async-start | bytes 1327104 | tf_op jit(solution)/shard_map/all_gather | solution.py:144
  9.1 91.2 %all-gather.8.cloned.1.call-start = ((), (), s32[]{:S(2)}) async-start(), calls=%async_computation.6 | async-start | bytes 1769472 | tf_op jit(solution)/shard_map/all_gather | solution.py:145
  10.8 168.2 %all-gather.12.cloned.1.call-start = ((), (), s32[]{:S(2)}) async-start(), calls=%async_computation.8 | async-start | bytes 1327104 | tf_op jit(solution)/shard_map/all_gather | solution.py:146
  12.5 211.6 %all-reduce.10.cloned.1.call-start = ((), (), s32[]{:S(2)}) async-start(), calls=%async_computation.9 | async-start | bytes 3145728 | tf_op jit(solution)/shard_map/psum | solution.py:207
  48.0 73.4 %copy-start.60 = (f32[512]{0:T(512)}, f32[512]{0:T(512)S(1)}, u32[]{:S(2)}) copy-start(f32[512]{0:T(512)S(1)} %add_rsqrt_fusion.1) | copy-start | bytes 6148
  58.7 43.3 %copy-start.63 = (f32[512]{0:T(512)S(1)}, f32[512]{0:T(512)}, u32[]{:S(2)}) copy-start(f32[512]{0:T(512)} %copy-done.62) | copy-start | bytes 6148
  58.7 43.3 %copy-start.68 = (f32[64]{0:T(128)S(1)}, f32[64]{0:T(128)}, u32[]{:S(2)}) copy-start(f32[64]{0:T(128)} %copy-done.67) | copy-start | bytes 772
  58.7 62.7 %copy-start.55 = (f32[1536]{0:T(1024)S(1)}, f32[1536]{0:T(1024)}, u32[]{:S(2)}) copy-start(f32[1536]{0:T(1024)} %copy-done.54) | copy-start | bytes 18436
  58.7 62.7 %copy-start.70 = (f32[128]{0:T(128)S(1)}, f32[128]{0:T(128)}, u32[]{:S(2)}) copy-start(f32[128]{0:T(128)} %get-tuple-element.569) | copy-start | bytes 1540
  182.6 152.9 %all-gather.16.cloned.1.call-start = ((), (), s32[]{:S(2)}) async-start(), calls=%async_computation.11 | async-start | bytes 7962624 | tf_op jit(solution)/shard_map/all_gather | solution.py:148
  183.7 348.2 %all-gather.14.cloned.1.call-start = ((), (), s32[]{:S(2)}) async-start(), calls=%async_computation.10 | async-start | bytes 15925248 | tf_op jit(solution)/shard_map/all_gather | solution.py:147
  188.3 499.8 %all-reduce.12.cloned.1.call-start = ((), (), s32[]{:S(2)}) async-start(), calls=%async_computation.12 | async-start | bytes 3145728 | tf_op jit(solution)/shard_map/psum | solution.py:247
  646.9 116.2 %reduce-scatter.9.cloned.1.call-start = ((), (), s32[]{:S(2)}) async-start(), calls=%async_computation.14 | async-start | bytes 655360 | tf_op jit(solution)/shard_map/reduce_scatter | solution.py:308
  648.0 43.5 %copy-start.53 = (f32[1536]{0:T(1024)S(1)}, f32[1536]{0:T(1024)}, u32[]{:S(2)}) copy-start(f32[1536]{0:T(1024)} %get-tuple-element.561) | copy-start | bytes 18436
  739.2 82.1 %copy-start.34 = (f32[512,64]{0,1:T(8,128)S(1)}, f32[512,64]{0,1:T(8,128)}, u32[]{:S(2)}) copy-start(f32[512,64]{0,1:T(8,128)} %get-tuple-element.563) | copy-start | bytes 393220
  739.2 82.1 %copy-start.35 = (f32[512,64]{0,1:T(8,128)S(1)}, f32[512,64]{0,1:T(8,128)}, u32[]{:S(2)}) copy-start(f32[512,64]{0,1:T(8,128)} %get-tuple-element.564) | copy-start | bytes 393220
  741.3 44.7 %reduce-scatter.7.cloned.1.call-start = ((), (), s32[]{:S(2)}) async-start(), calls=%async_computation.13 | async-start | bytes 655360 | tf_op jit(solution)/shard_map/reduce_scatter | solution.py:302
  743.4 76.8 %all-reduce.14.cloned.1.call-start = ((), (), s32[]{:S(2)}) async-start(), calls=%async_computation.15 | async-start | bytes 1048576 | tf_op jit(solution)/shard_map/psum | solution.py:319
  787.8 102.1 %reduce-scatter.13.cloned.1.call-start = ((), (), s32[]{:S(2)}) async-start(), calls=%async_computation.17 | async-start | bytes 1769472 | tf_op jit(solution)/shard_map/reduce_scatter | solution.py:364
  825.0 132.2 %reduce-scatter.11.cloned.1.call-start = ((), (), s32[]{:S(2)}) async-start(), calls=%async_computation.16 | async-start | bytes 1327104 | tf_op jit(solution)/shard_map/reduce_scatter | solution.py:361
  828.5 196.1 %reduce-scatter.15.cloned.1.call-start = ((), (), s32[]{:S(2)}) async-start(), calls=%async_computation.18 | async-start | bytes 1327104 | tf_op jit(solution)/shard_map/reduce_scatter | solution.py:367
  832.7 266.5 %all-reduce.18.cloned.1.call-start = ((), (), s32[]{:S(2)}) async-start(), calls=%async_computation.21 | async-start | bytes 6684672 | tf_op jit(solution)/shard_map/psum | solution.py:222
  890.0 651.4 %all-reduce.16.cloned.1.call-start = ((), (), s32[]{:S(2)}) async-start(), calls=%async_computation.20 | async-start | bytes 28311552
  940.1 732.9 %reduce-scatter.17.cloned.1.call-start = ((), (), s32[]{:S(2)}) async-start(), calls=%async_computation.19 | async-start | bytes 7962624 | tf_op jit(solution)/shard_map/reduce_scatter | solution.py:373
  949.0 75.6 %copy-start.32 = (f32[384,192]{0,1:T(8,128)S(1)}, f32[384,192]{0,1:T(8,128)}, u32[]{:S(2)}) copy-start(f32[384,192]{0,1:T(8,128)} %param.34) | copy-start | bytes 884740
  949.0 75.6 %copy-start.51 = (f32[384,192]{0,1:T(8,128)S(1)}, f32[384,192]{0,1:T(8,128)}, u32[]{:S(2)}) copy-start(f32[384,192]{0,1:T(8,128)} %param.36) | copy-start | bytes 884740
  959.2 143.2 %copy-start.59 = (f32[1536]{0:T(1024)S(1)}, f32[1536]{0:T(1024)}, u32[]{:S(2)}) copy-start(f32[1536]{0:T(1024)} %get-tuple-element.453) | copy-start | bytes 18436
  959.2 196.8 %copy-start.27 = (f32[192,512]{1,0:T(8,128)S(1)}, f32[192,512]{1,0:T(8,128)}, u32[]{:S(2)}) copy-start(f32[192,512]{1,0:T(8,128)} %param.31) | copy-start | bytes 1179652
  1099.3 59.3 %copy-start.7 = (bf16[512,1536]{1,0:T(8,128)(2,1)S(1)}, bf16[512,1536]{1,0:T(8,128)(2,1)}, u32[]{:S(2)}) copy-start(bf16[512,1536]{1,0:T(8,128)(2,1)} %all-reduce.10.cloned.1.call-done) | copy-start | bytes 4718596
  1565.3 107.7 %copy-start.13 = (f32[2240,192]{0,1:T(8,128)S(1)}, f32[2240,192]{0,1:T(8,128)}, u32[]{:S(2)}) copy-start(f32[2240,192]{0,1:T(8,128)} %param.40) | copy-start | bytes 5160964
  1565.3 107.7 %copy-start.24 = (f32[2240,192]{0,1:T(8,128)S(1)}, f32[2240,192]{0,1:T(8,128)}, u32[]{:S(2)}) copy-start(f32[2240,192]{0,1:T(8,128)} %param.42) | copy-start | bytes 5160964
  (113 other events, 615.2 us)
Sparse Core Ops, SparseCore 0:
  10.7 43.7 all-gather.9
  57.2 42.9 all-gather.7
  102.9 41.9 all-gather.11
  182.7 41.3 all-reduce.9
  226.7 108.8 all-gather.15
  338.1 193.7 all-gather.13
  647.1 41.0 all-reduce.11
  741.4 21.6 reduce-scatter.8
  766.0 19.9 reduce-scatter.6
  788.7 31.4 all-reduce.13
  825.1 64.7 reduce-scatter.12
  894.1 63.0 reduce-scatter.10
  961.5 63.0 reduce-scatter.14
  1028.3 70.9 all-reduce.17
  1103.1 438.1 all-reduce.15
  1544.9 128.0 reduce-scatter.16
where the time goes:
time: 1700 us; the launch traced here: 1690 us
  waiting for transfers between devices  1140 us (67%)
  local copies, waits for them, and re-layouts  185 us (11%)
  matrix products  136 us (8%)
  blocking collectives  115 us (7%)
  other arithmetic  80.3 us (5%)
    unnamed x17, waiting for transfers between devices  378 us
    all_gather x1, waiting for transfers between devices, local(): lax.all_gather(expand_low, ('dp', 'seq'), axis=0, tiled=True)  188 us
    all_gather x1, waiting for transfers between devices, local(): lax.all_gather(shrink_low, ('dp', 'seq'), axis=1, tiled=True)  107 us
    reduce_scatter x1, waiting for transfers between devices, local(): lax.psum_scatter(shrink_grad.astype(jnp.bfloat16), ('dp', 'seq'), scatter...  105 us
    unnamed x137, local copies, waits for them, and re-layouts  95.8 us
    psum x1, waiting for transfers between devices, local(): lax.psum(jnp.dot(activation, shrink_weight, preferred_element_type=jnp.fl...  72.6 us
    reduce_scatter x1, waiting for transfers between devices, local(): lax.psum_scatter(mixing_grad.astype(jnp.bfloat16), ('dp', 'seq'), scatter...  65.3 us
    all_gather x1, waiting for transfers between devices, local(): lax.all_gather(keyvalue_low, ('dp', 'seq'), axis=0, tiled=True)  41.3 us
  transfers between devices with their start and end apart: 16, of which 15 were waited for; matrix products, arithmetic and copies ran while one was open for 12% of the time, Pallas kernels for 0%

commit v1 on v0

v1 whole, which is shorter than its diff:
```python
import functools
import math

import jax
import jax.numpy as jnp
from jax import lax
from jax.experimental import pallas as pl
from jax.experimental.pallas import tpu as pltpu
from jax.sharding import PartitionSpec as P

D = 1536
H = 12
KV = 2
HD = 128
STEP = 5


norm_eps = 1e-06
rope_base = 1000000.0
beta_first = 0.5
beta_second = 0.5
adam_eps = 1e-08
masked_low = -1e30
learn_rates = (0.02, 0.02, 0.3, 0.02, 0.01, 0.2)
decay_rates = (0.1, 0.1, 0.1, 0.1, 0.1, 0.0)


def folded_places(row_ids, shard_rows, seq_count):
    owner_index = row_ids // shard_rows
    inside = row_ids % shard_rows
    halves = shard_rows // 2
    block_index = jnp.where(inside < halves, owner_index, 2 * seq_count - 1 - owner_index)
    return block_index * halves + inside % halves


def doc_starts(places, lengths):
    endings = jnp.cumsum(lengths)
    taken_lengths = jnp.where(endings[None, :] <= places[:, None], lengths[None, :], 0)
    return jnp.sum(taken_lengths, axis=1)


def rotate(values, places):
    halves = values.shape[-1] // 2
    powers = jnp.arange(halves, dtype=jnp.float32) * (-2.0 / values.shape[-1])
    frequency = jnp.power(jnp.float32(rope_base), powers)
    angles = places.astype(jnp.float32)[:, None] * frequency[None, :]
    cosine = jnp.cos(angles)[:, None, :]
    sine_term = jnp.sin(angles)[:, None, :]
    first_half = values[..., :halves]
    second_half = values[..., halves:]
    return jnp.concatenate(
        [
            first_half * cosine - second_half * sine_term,
            second_half * cosine + first_half * sine_term,
        ],
        axis=-1,
    )


def norm_back(grad_rows, values, scale_rows, gain_vector):
    unit_rows = values * scale_rows
    scaled = grad_rows * gain_vector
    mean_term = jnp.mean(scaled * unit_rows, axis=-1, keepdims=True)
    return (scale_rows * (scaled - unit_rows * mean_term), jnp.sum(grad_rows * unit_rows, axis=0))


def adamw(master, moment, square, grad_rows, rate_value, decay_value):
    first_new = beta_first * moment + (1.0 - beta_first) * grad_rows
    second_new = beta_second * square + (1.0 - beta_second) * grad_rows * grad_rows
    fix_first = 1.0 - beta_first**STEP
    fix_second = 1.0 - beta_second**STEP
    weight = master - rate_value * (
        first_new / fix_first / (jnp.sqrt(second_new / fix_second) + adam_eps)
        + decay_value * master
    )
    return (grad_rows, first_new, second_new, weight, weight.astype(jnp.bfloat16))


def shift(values, axis, steps):
    size = lax.axis_size(axis)
    return lax.ppermute(values, axis, [(i, (i + steps) % size) for i in range(size)])


def swap(values, axis, bit):
    size = lax.axis_size(axis)
    return lax.ppermute(values, axis, [(i, i ^ bit) for i in range(size)])


def dot_nn(left, right):
    return jnp.dot(left, right, preferred_element_type=jnp.float32)


def dot_nt(left, right):
    return lax.dot_general(left, right, (((1,), (1,)), ((), ())), preferred_element_type=jnp.float32)


def dot_tn(left, right):
    return lax.dot_general(left, right, (((0,), (0,)), ((), ())), preferred_element_type=jnp.float32)


def low(values):
    return values.astype(jnp.bfloat16)


def wide(values):
    return values.astype(jnp.float32)


def halve(values, which):
    size = values.shape[0] // 2
    mine = lax.dynamic_slice_in_dim(values, which * size, size, 0)
    other = lax.dynamic_slice_in_dim(values, (1 - which) * size, size, 0)
    return mine, other


def head_scatter(values):
    index = lax.axis_index("head")
    mine, other = halve(values, index % 2)
    values = mine + wide(swap(low(other), "head", 1))
    mine, other = halve(values, index // 2)
    return mine + wide(swap(low(other), "head", 2))


def head_gather(values, dim=0):
    index = lax.axis_index("head")
    for bit, which in ((2, index // 2), (1, index % 2)):
        got = swap(values, "head", bit)
        values = jnp.where(
            which == 0,
            jnp.concatenate([values, got], dim),
            jnp.concatenate([got, values], dim),
        )
    return values


def seq_sum(blocks):
    total = blocks[0]
    for s in range(1, len(blocks)):
        total = total + wide(shift(low(blocks[s]), "seq", -s))
    return total


def place(blocks):
    size = lax.axis_size("seq")
    dp_index, seq_index = lax.axis_index("dp"), lax.axis_index("seq")
    first = next(iter(blocks.values()))
    out = jnp.zeros((2 * size,) + first.shape, first.dtype)
    for (a, k), block in blocks.items():
        owner = lax.rem(dp_index + a, 2) * size + lax.rem(seq_index + size - k, size)
        out = lax.dynamic_update_slice(out, block[None], (owner,) + (0,) * first.ndim)
    return out


def weight_gather(block):
    size = lax.axis_size("seq")
    blocks = {}
    for k in range(size):
        if k > 0:
            block = shift(block, "seq", 1)
        blocks[0, k] = block
        blocks[1, k] = swap(block, "dp", 1)
    out = place(blocks)
    return out.reshape((-1,) + out.shape[2:])


def weight_exchange(packs):
    size = lax.axis_size("seq")
    seq_index = lax.axis_index("seq")
    blocks = {}
    for k in range(size):
        block = lax.dynamic_index_in_dim(packs, lax.rem(seq_index + k, size), 0, False)
        if k > 0:
            block = shift(block, "seq", k)
        blocks[0, k] = block
        blocks[1, k] = swap(block, "dp", 1)
    out = place(blocks)
    return out.reshape((-1,) + out.shape[2:])


def grad_exchange(parts, scatter):
    size = lax.axis_size("seq")
    dp_index, seq_index = lax.axis_index("dp"), lax.axis_index("seq")
    parts = parts.reshape(2, size, -1, parts.shape[1])
    total = jnp.zeros(parts.shape[2:], jnp.float32)
    out = jnp.zeros(parts.shape[1:], jnp.bfloat16)
    for k in range(size - 1, -1, -1):
        target = lax.rem(seq_index + k, size)
        pair = lax.dynamic_index_in_dim(parts, target, 1, False)
        mine = lax.dynamic_index_in_dim(pair, dp_index, 0, False)
        other = lax.dynamic_index_in_dim(pair, 1 - dp_index, 0, False)
        block = wide(mine) + wide(swap(low(other), "dp", 1))
        if k > 0:
            block = wide(shift(low(block), "seq", k))
        if scatter:
            total = total + block
        else:
            source = lax.rem(seq_index + size - k, size)
            out = lax.dynamic_update_slice(out, low(block)[None], (source, 0, 0))
    return total if scatter else out


def visible_blocks(starts_ref, block_rows, half):
    size = lax.axis_size("seq")
    index = lax.axis_index("seq")
    place_block = jnp.where(half == 0, index, 2 * size - 1 - index)
    return starts_ref[half] // block_rows, place_block


def key_offset(block, size, block_rows):
    owner = jnp.where(block < size, block, 2 * size - 1 - block)
    return owner * (2 * block_rows) + jnp.where(block < size, 0, block_rows)


def attention_forward(starts_ref, q_ref, k_ref, v_ref, o_ref, lse_ref):
    local_rows, heads = q_ref.shape[0], q_ref.shape[1] // HD
    block_rows = local_rows // 2
    size = lax.axis_size("seq")
    scale = 1.0 / math.sqrt(HD)
    stacked = heads * block_rows
    for half in range(2):
        begin, last = visible_blocks(starts_ref, block_rows, half)
        rows = pl.ds(half * block_rows, block_rows)
        q = jnp.concatenate([q_ref[rows, i * HD : (i + 1) * HD] for i in range(heads)], axis=0)

        def step(block, carried, diagonal, q=q):
            running_max, running_sum, running_out = carried
            keys = pl.ds(pl.multiple_of(key_offset(block, size, block_rows), block_rows), block_rows)
            scores = dot_nt(q, k_ref[keys, :]) * scale
            if diagonal:
                row = lax.broadcasted_iota(jnp.int32, (block_rows, block_rows), 0)
                col = lax.broadcasted_iota(jnp.int32, (block_rows, block_rows), 1)
                seen = jnp.concatenate([jnp.where(col <= row, 0.0, masked_low)] * heads, axis=0)
                scores = scores + seen
            new_max = jnp.maximum(running_max, jnp.max(scores, axis=-1, keepdims=True))
            probs = jnp.exp(scores - new_max)
            fade = jnp.exp(running_max - new_max)
            running_sum = running_sum * fade + jnp.sum(probs, axis=-1, keepdims=True)
            running_out = running_out * fade + dot_nn(low(probs), v_ref[keys, :])
            return new_max, running_sum, running_out

        carried = (
            jnp.full((stacked, 1), masked_low, jnp.float32),
            jnp.zeros((stacked, 1), jnp.float32),
            jnp.zeros((stacked, HD), jnp.float32),
        )
        carried = lax.fori_loop(begin, last, functools.partial(step, diagonal=False), carried)
        running_max, running_sum, running_out = step(last, carried, True)
        out = running_out / running_sum
        lse = running_max + jnp.log(running_sum)
        for i in range(heads):
            part = slice(i * block_rows, (i + 1) * block_rows)
            o_ref[rows, i * HD : (i + 1) * HD] = out[part]
            lse_ref[rows, i : i + 1] = lse[part]


def attention_backward(
    starts_ref, q_ref, k_ref, v_ref, do_ref, o_ref, lse_ref, dq_ref, dk_ref, dv_ref
):
    local_rows, heads = q_ref.shape[0], q_ref.shape[1] // HD
    block_rows = local_rows // 2
    size = lax.axis_size("seq")
    scale = 1.0 / math.sqrt(HD)
    stacked = heads * block_rows
    dk_ref[...] = jnp.zeros_like(dk_ref)
    dv_ref[...] = jnp.zeros_like(dv_ref)
    for half in range(2):
        begin, last = visible_blocks(starts_ref, block_rows, half)
        rows = pl.ds(half * block_rows, block_rows)

        def stack(ref):
            return jnp.concatenate([ref[rows, i * HD : (i + 1) * HD] for i in range(heads)], axis=0)

        q, do = stack(q_ref), stack(do_ref)
        delta = jnp.sum(wide(do) * stack(o_ref), axis=-1, keepdims=True)
        lse = jnp.concatenate([lse_ref[rows, i : i + 1] for i in range(heads)], axis=0)

        def step(block, dq, diagonal, q=q, do=do, delta=delta, lse=lse):
            keys = pl.ds(pl.multiple_of(key_offset(block, size, block_rows), block_rows), block_rows)
            k, v = k_ref[keys, :], v_ref[keys, :]
            scores = dot_nt(q, k) * scale
            if diagonal:
                row = lax.broadcasted_iota(jnp.int32, (block_rows, block_rows), 0)
                col = lax.broadcasted_iota(jnp.int32, (block_rows, block_rows), 1)
                seen = jnp.concatenate([jnp.where(col <= row, 0.0, masked_low)] * heads, axis=0)
                scores = scores + seen
            probs = jnp.exp(scores - lse)
            score_grad = low(probs * (dot_nt(do, v) - delta))
            dk_ref[keys, :] += dot_tn(score_grad, q) * scale
            dv_ref[keys, :] += dot_tn(low(probs), do)
            return dq + dot_nn(score_grad, k)

        dq = jnp.zeros((stacked, HD), jnp.float32)
        dq = lax.fori_loop(begin, last, functools.partial(step, diagonal=False), dq)
        dq = step(last, dq, True) * scale
        for i in range(heads):
            dq_ref[rows, i * HD : (i + 1) * HD] = dq[i * block_rows : (i + 1) * block_rows]


def in_vmem(kernel, outs, scalars, *arrays):
    return pl.pallas_call(
        kernel,
        out_shape=outs,
        in_specs=[pl.BlockSpec(memory_space=pltpu.SMEM)]
        + [pl.BlockSpec(memory_space=pltpu.VMEM)] * len(arrays),
        out_specs=[pl.BlockSpec(memory_space=pltpu.VMEM)] * len(outs),
        compiler_params=pltpu.CompilerParams(vmem_limit_bytes=40 * 1024 * 1024),
        cost_estimate=pl.CostEstimate(
            flops=12 * 10**9, bytes_accessed=8 * 10**6, transcendentals=10**7
        ),
    )(scalars, *arrays)


def local(
    tokens,
    cotangent,
    doc_lengths,
    queries_master,
    queries_moment,
    queries_square,
    keyvalue_master,
    keyvalue_moment,
    keyvalue_square,
    mixing_master,
    mixing_moment,
    mixing_square,
    expand_master,
    expand_moment,
    expand_square,
    shrink_master,
    shrink_moment,
    shrink_square,
    scalars_master,
    scalars_moment,
    scalars_square,
):
    local_rows, width = tokens.shape[1], tokens.shape[2]
    seq_count = lax.axis_size("seq")
    head_count = lax.axis_size("head")
    head_index = lax.axis_index("head")
    seq_index = lax.axis_index("seq")
    local_heads = H // head_count
    wide_heads = local_heads * HD
    kv_head = head_index * local_heads // (H // KV)
    core = head_index % 2
    quarter = local_rows // 4
    row_begin = (head_index % 2) * (2 * quarter) + (head_index // 2) * quarter
    hidden_units = expand_master.shape[2]
    units = 64 * -(-hidden_units // (64 * seq_count))
    more = ((0, 0), (0, units * seq_count - hidden_units))

    attn_pack = jnp.concatenate(
        [
            low(queries_master),
            low(mixing_master).T,
            low(lax.dynamic_slice_in_dim(keyvalue_master, kv_head * HD, HD, 1)),
            low(lax.dynamic_slice_in_dim(keyvalue_master, (KV + kv_head) * HD, HD, 1)),
        ],
        axis=1,
    )
    expand_low = low(expand_master)

    def cut(values):
        values = jnp.pad(values, more)
        return values.reshape(values.shape[0], seq_count, units).transpose(1, 0, 2)

    ff_packs = jnp.concatenate(
        [cut(expand_low[:, 0]), cut(expand_low[:, 1]), cut(low(shrink_master).T)], axis=2
    )
    scalar_values = wide(lax.all_gather(low(scalars_master), ("dp", "seq"), axis=0, tiled=True))
    attn_weight = weight_gather(attn_pack)
    ff_weight = weight_exchange(ff_packs)
    query_weight = attn_weight[:, :wide_heads]
    mixing_t = attn_weight[:, wide_heads : 2 * wide_heads]
    key_value_weight = attn_weight[:, 2 * wide_heads :]
    expand_weight = ff_weight[:, : 2 * units]
    shrink_t = ff_weight[:, 2 * units :]

    cot_rows = cotangent[0]
    cot_own = lax.dynamic_slice_in_dim(cot_rows, row_begin, quarter, 0)
    cot_blocks = [cot_rows]
    moving = cot_own
    for s in range(1, seq_count):
        moving = shift(moving, "seq", 1)
        cot_blocks.append(head_gather(moving))

    gain_one = scalar_values[:width]
    gain_two = scalar_values[width : 2 * width]
    bias_query = lax.dynamic_slice_in_dim(
        scalar_values, 2 * width + head_index * wide_heads, wide_heads
    )
    bias_keyvalue = scalar_values[2 * width + H * HD :]
    key_bias = lax.dynamic_slice_in_dim(bias_keyvalue, kv_head * HD, HD)
    value_bias = lax.dynamic_slice_in_dim(bias_keyvalue, (KV + kv_head) * HD, HD)
    x_rows = wide(tokens[0])
    lengths = doc_lengths[0]
    places = folded_places(
        seq_index * local_rows + jnp.arange(local_rows, dtype=jnp.int32), local_rows, seq_count
    )
    starts = doc_starts(places, lengths)
    half_starts = jnp.stack([starts[0], starts[local_rows // 2]])
    within = places - starts
    scale_one = lax.rsqrt(jnp.mean(x_rows * x_rows, axis=-1, keepdims=True) + norm_eps)
    normed = low(x_rows * scale_one * gain_one)
    query_pre = dot_nn(normed, query_weight) + bias_query
    queries = low(rotate(query_pre.reshape(local_rows, local_heads, HD), within)).reshape(
        local_rows, wide_heads
    )
    key_value_pre = dot_nn(normed, key_value_weight)
    key_rows = low(rotate((key_value_pre[:, :HD] + key_bias)[:, None, :], within)[:, 0, :])
    value_rows = low(key_value_pre[:, HD:] + value_bias)
    moving = jnp.concatenate([key_rows, value_rows], axis=1)
    all_rows = jnp.zeros((seq_count,) + moving.shape, moving.dtype)
    for s in range(seq_count):
        if s > 0:
            moving = shift(moving, "seq", 1)
        owner = lax.rem(seq_index + seq_count - s, seq_count)
        all_rows = lax.dynamic_update_slice(all_rows, moving[None], (owner, 0, 0))
    all_rows = all_rows.reshape(-1, 2 * HD)
    all_keys, all_values = all_rows[:, :HD], all_rows[:, HD:]
    stream_rows = all_rows.shape[0]
    attended, log_total = in_vmem(
        attention_forward,
        [
            jax.ShapeDtypeStruct((local_rows, wide_heads), jnp.float32),
            jax.ShapeDtypeStruct((local_rows, local_heads), jnp.float32),
        ],
        half_starts,
        queries,
        all_keys,
        all_values,
    )
    attended_low = low(attended)
    x_own = lax.dynamic_slice_in_dim(x_rows, row_begin, quarter, 0)
    hidden = x_own + head_scatter(dot_nt(attended_low, mixing_t))
    scale_two = lax.rsqrt(jnp.mean(hidden * hidden, axis=-1, keepdims=True) + norm_eps)
    normed_two = low(hidden * scale_two * gain_two)

    normed_blocks, grad_blocks, act_blocks, back_parts, out_parts = [], [], [], [], []
    moving = normed_two
    for s in range(seq_count):
        if s > 0:
            moving = shift(moving, "seq", 1)
        block = head_gather(moving)
        both = dot_nn(block, expand_weight)
        gate_value, up_value = both[:, :units], both[:, units:]
        gate_sigmoid = jax.nn.sigmoid(gate_value)
        activation = low(gate_value * gate_sigmoid * up_value)
        act_grad = wide(low(dot_nn(cot_blocks[s], shrink_t)))
        gate_grad = low(act_grad * up_value * gate_sigmoid * (1.0 + gate_value * (1.0 - gate_sigmoid)))
        up_grad = low(act_grad * gate_value * gate_sigmoid)
        both_grad = jnp.concatenate([gate_grad, up_grad], axis=1)
        back_parts.append(head_scatter(dot_nt(both_grad, expand_weight)))
        out_parts.append(head_scatter(dot_nt(activation, shrink_t)))
        normed_blocks.append(block)
        grad_blocks.append(both_grad)
        act_blocks.append(activation)
    norm_two_grad = seq_sum(back_parts)
    back_two, gain_two_grad = norm_back(norm_two_grad, hidden, scale_two, gain_two)
    hidden_grad = wide(lax.dynamic_slice_in_dim(cot_rows, row_begin, quarter, 0)) + back_two
    branch_grad = head_gather(low(hidden_grad))
    feedforward = seq_sum(out_parts)
    layer_out = head_gather(low(hidden + feedforward))
    expand_part = dot_tn(jnp.concatenate(normed_blocks), jnp.concatenate(grad_blocks))
    shrink_part = dot_tn(jnp.concatenate(cot_blocks), jnp.concatenate(act_blocks))
    ff_grads = grad_exchange(low(jnp.concatenate([expand_part, shrink_part], axis=1)), False)

    attended_grad = low(dot_nn(branch_grad, mixing_t))
    query_sum, key_sum, value_sum = in_vmem(
        attention_backward,
        [
            jax.ShapeDtypeStruct((local_rows, wide_heads), jnp.float32),
            jax.ShapeDtypeStruct((stream_rows, HD), jnp.float32),
            jax.ShapeDtypeStruct((stream_rows, HD), jnp.float32),
        ],
        half_starts,
        queries,
        all_keys,
        all_values,
        attended_grad,
        attended,
        log_total,
    )
    mine = jnp.where(core == 0, key_sum, value_sum)
    other = jnp.where(core == 0, value_sum, key_sum)
    mine = mine + wide(swap(low(other), "head", 1))
    mine = mine.reshape(seq_count, local_rows, HD)
    own_sum = seq_sum(
        [
            lax.dynamic_index_in_dim(mine, lax.rem(seq_index + seq_count - s, seq_count), 0, False)
            for s in range(seq_count)
        ]
    )
    own_sum = low(jnp.where(core == 0, rotate(own_sum[:, None, :], -within)[:, 0, :], own_sum))
    query_grad = low(
        rotate(query_sum.reshape(local_rows, local_heads, HD), -within).reshape(
            local_rows, wide_heads
        )
    )
    own_weight = lax.dynamic_slice_in_dim(key_value_weight, core * HD, HD, 1)
    norm_one_grad = head_scatter(dot_nt(query_grad, query_weight) + dot_nt(own_sum, own_weight))
    scale_own = lax.dynamic_slice_in_dim(scale_one, row_begin, quarter, 0)
    back_one, gain_one_grad = norm_back(norm_one_grad, x_own, scale_own, gain_one)
    input_grad = head_gather(low(hidden_grad + back_one))
    attn_part = jnp.concatenate(
        [
            dot_tn(normed, query_grad),
            dot_tn(branch_grad, attended_low),
            dot_tn(normed, own_sum),
        ],
        axis=1,
    )
    attn_grads = grad_exchange(attn_part, True)
    kv_block = low(attn_grads[:, 2 * wide_heads :])
    small = jnp.zeros((scalars_master.shape[0] * 2 * seq_count,), jnp.float32)
    small = lax.dynamic_update_slice(small, jnp.concatenate([gain_one_grad, gain_two_grad]), (0,))
    small = lax.dynamic_update_slice(
        small, jnp.sum(wide(query_grad), axis=0), (2 * width + head_index * wide_heads,)
    )
    kv_column = core * KV * HD + kv_head * HD
    small = lax.dynamic_update_slice(
        small, jnp.sum(wide(own_sum), axis=0), (2 * width + H * HD + kv_column,)
    )
    small = lax.psum(small, "head")
    shared_scalars = lax.psum_scatter(small, ("dp", "seq"), scatter_dimension=0, tiled=True)
    gathered = head_gather(kv_block, 1)
    shared_keyvalue = wide(gathered)

    def joined(part):
        part = ff_grads[:, :, part * units : (part + 1) * units].transpose(1, 0, 2)
        return wide(part.reshape(part.shape[0], -1)[:, :hidden_units])

    grads = (
        attn_grads[:, :wide_heads],
        shared_keyvalue,
        attn_grads[:, wide_heads : 2 * wide_heads].T,
        jnp.stack([joined(0), joined(1)], axis=1),
        joined(2).T,
        shared_scalars,
    )
    masters = (
        (queries_master, queries_moment, queries_square),
        (keyvalue_master, keyvalue_moment, keyvalue_square),
        (mixing_master, mixing_moment, mixing_square),
        (expand_master, expand_moment, expand_square),
        (shrink_master, shrink_moment, shrink_square),
        (scalars_master, scalars_moment, scalars_square),
    )
    results = [layer_out[None], input_grad[None]]
    for held, grad, rate, decay in zip(masters, grads, learn_rates, decay_rates):
        results.extend(adamw(*held, wide(low(grad)), rate, decay))
    return tuple(results)


def solution(mesh):
    placed = (
        P("dp", "seq", None),
        P("dp", "seq", None),
        P("dp", None),
        P(("dp", "seq"), "head"),
        P(("dp", "seq"), "head"),
        P(("dp", "seq"), "head"),
        P(("dp", "seq"), None),
        P(("dp", "seq"), None),
        P(("dp", "seq"), None),
        P("head", ("dp", "seq")),
        P("head", ("dp", "seq")),
        P("head", ("dp", "seq")),
        P(("dp", "seq"), None, "head"),
        P(("dp", "seq"), None, "head"),
        P(("dp", "seq"), None, "head"),
        P("head", ("dp", "seq")),
        P("head", ("dp", "seq")),
        P("head", ("dp", "seq")),
        P(("dp", "seq")),
        P(("dp", "seq")),
        P(("dp", "seq")),
    )
    return jax.shard_map(
        local,
        mesh=mesh,
        in_specs=placed,
        out_specs=(
            P("dp", "seq", None),
            P("dp", "seq", None),
            P(("dp", "seq"), "head"),
            P(("dp", "seq"), "head"),
            P(("dp", "seq"), "head"),
            P(("dp", "seq"), "head"),
            P(("dp", "seq"), "head"),
            P(("dp", "seq"), None),
            P(("dp", "seq"), None),
            P(("dp", "seq"), None),
            P(("dp", "seq"), None),
            P(("dp", "seq"), None),
            P("head", ("dp", "seq")),
            P("head", ("dp", "seq")),
            P("head", ("dp", "seq")),
            P("head", ("dp", "seq")),
            P("head", ("dp", "seq")),
            P(("dp", "seq"), None, "head"),
            P(("dp", "seq"), None, "head"),
            P(("dp", "seq"), None, "head"),
            P(("dp", "seq"), None, "head"),
            P(("dp", "seq"), None, "head"),
            P("head", ("dp", "seq")),
            P("head", ("dp", "seq")),
            P("head", ("dp", "seq")),
            P("head", ("dp", "seq")),
            P("head", ("dp", "seq")),
            P(("dp", "seq")),
            P(("dp", "seq")),
            P(("dp", "seq")),
            P(("dp", "seq")),
            P(("dp", "seq")),
        ),
        check_vma=False,
    )
```

time: 1700 us -> 883 us (0.52)
  waiting for transfers between devices: 1140 us -> 267 us
  starting transfers between devices: 11.9 us -> 108 us
  matrix products: 136 us -> 71.1 us
  local copies, waits for them, and re-layouts: 185 us -> 219 us
  Pallas kernels: 0 us -> 17.1 us
    unnamed x17 -> x0, waiting for transfers between devices: 378 us -> none
    all_gather x5 -> x0, waiting for transfers between devices: 338 us -> none  [the longest x1 188 us: local(): lax.all_gather(expand_low, ('dp', 'seq'), axis=0, tiled=True)]
    ppermute x0 -> x89, waiting for transfers between devices: none -> 267 us  [the longest x59 161 us: swap(): return lax.ppermute(values, axis, [(i, i ^ bit) for i in range(size)])]
    reduce_scatter x6 -> x0, waiting for transfers between devices: 253 us -> none  [the longest x1 105 us: local(): lax.psum_scatter(shrink_grad.astype(jnp.bfloat16), ('dp', 'seq'), scatter...]
    psum x4 -> x0, waiting for transfers between devices: 170 us -> none  [the longest x1 72.6 us: local(): lax.psum(jnp.dot(activation, shrink_weight, preferred_element_type=jnp.fl...]
    ppermute x0 -> x89, starting transfers between devices: none -> 108 us  [the longest x30 65.1 us: shift(): lax.ppermute(values, axis, [(i, (i + steps) % size) for i in range(size)])]
    dynamic_update_slice x3 -> x24, local copies, waits for them, and re-layouts: 3.35 us -> 105 us  [the longest x4 91.6 us: grad_exchange(): out = lax.dynamic_update_slice(out, low(block)[None], (source, 0, 0))]
    dot_general x47 -> x27, matrix products: 136 us -> 71.1 us  [the longest x5 28.7 us: dot_tn(): lax.dot_general(left, right, (((0,), (0,)), ((), ())), preferred_element_...]
  transfers between devices with their start and end apart: 16 -> 89, of which waited for: 15 -> 32; matrix products, arithmetic and copies ran while one was open for 12% -> 38% of each run, Pallas kernels for 0% -> 1%
where the time goes in v1:
time: 883 us; the launch traced here: 867 us
  waiting for transfers between devices  267 us (30%)
  local copies, waits for them, and re-layouts  219 us (25%)
  starting transfers between devices  108 us (12%)
  blocking collectives  105 us (12%)
  other arithmetic  75.9 us (9%)
  matrix products  71.1 us (8%)
  Pallas kernels  17.1 us (2%)
    ppermute x59, waiting for transfers between devices, swap(): return lax.ppermute(values, axis, [(i, i ^ bit) for i in range(size)])  161 us
    ppermute x30, waiting for transfers between devices, shift(): lax.ppermute(values, axis, [(i, (i + steps) % size) for i in range(size)])  106 us
    dynamic_update_slice x4, local copies, waits for them, and re-layouts, grad_exchange(): out = lax.dynamic_update_slice(out, low(block)[None], (source, 0, 0))  91.6 us
    all_gather x1, blocking collectives, local(): lax.all_gather(low(scalars_master), ('dp', 'seq'), axis=0, tiled=True)  65.7 us
    ppermute x30, starting transfers between devices, shift(): lax.ppermute(values, axis, [(i, (i + steps) % size) for i in range(size)])  65.1 us
    ppermute x59, starting transfers between devices, swap(): return lax.ppermute(values, axis, [(i, i ^ bit) for i in range(size)])  42.9 us
    unnamed x284, local copies, waits for them, and re-layouts  36 us
    unnamed x1, blocking collectives  33.2 us
  transfers between devices with their start and end apart: 89, of which 32 were waited for; matrix products, arithmetic and copies ran while one was open for 38% of the time, Pallas kernels for 1%

profile of v1, /device:TPU:0, one launch (start us, length us, event | category | flops | bytes accessed | tf_op | source)
XLA Modules:
  0.0 866.9 jit_solution(17286427076125226731)
XLA Ops:
  18.6 8.1 concatenate.274
  40.1 65.7 %all-gather = bf16[8,1,640]{2,1,0:T(2,128)(2,1)S(1)} all-gather(bf16[1,1,640]{2,1,0:T(2,128)(2,1)S(1)} %reshape.727), channel_id=1, replica_groups=mesh['dp'=2,'seq'=4,'head'=4] {'dp','seq'}, dimensions={0}, use_global_device_ids=true | all-gather | bytes 11520 | tf_op jit(solution)/shard_map/all_gather | solution.py:369
  126.0 13.8 %collective-permute-done.45 = bf16[128,1536]{1,0:T(8,128)(2,1)S(1)} collective-permute-done((bf16[128,1536]{1,0:T(8,128)(2,1)S(1)}, bf16[128,1536]{1,0:T(8,128)(2,1)S(1)}, u32[]{:S(2)}, u32[]{:S(2)}) %collective-permute-start.45) | collective-permute-done | bytes 393248 | tf_op jit(solution)/shard_map/ppermute | solution.py:81
  156.9 8.4 collective-permute-done.51
  181.8 30.9 %collective-permute-done.6 = bf16[192,1024]{1,0:T(8,128)(2,1)S(1)} collective-permute-done((bf16[192,1024]{1,0:T(8,128)(2,1)S(1)}, bf16[192,1024]{1,0:T(8,128)(2,1)S(1)}, u32[]{:S(2)}, u32[]{:S(2)}) %collective-permute-start.6) | collective-permute-done | bytes 393248 | tf_op jit(solution)/shard_map/ppermute | solution.py:86
  224.5 7.2 collective-permute-done.8
  243.0 6.9 shard_map.452
  255.5 9.8 %collective-permute-done.11 = bf16[128,1536]{1,0:T(8,128)(2,1)S(1)} collective-permute-done((bf16[128,1536]{1,0:T(8,128)(2,1)S(1)}, bf16[128,1536]{1,0:T(8,128)(2,1)S(1)}, u32[]{:S(2)}, u32[]{:S(2)}) %collective-permute-start.11) | collective-permute-done | bytes 393248 | tf_op jit(solution)/shard_map/ppermute | solution.py:86
  287.4 6.7 collective-permute-done.24
  350.3 14.6 %convolution_convert_fusion = bf16[1536,1152]{1,0:T(8,128)(2,1)} fusion(bf16[512,1536]{1,0:T(8,128)(2,1)} %copy-done.60, bf16[512,1536]{1,0:T(8,128)(2,1)} %copy-done.59, bf16[512,1536]{1,0:T(8,128)(2,1)} %copy-done.58, bf16[512,1536]{1,0:T(8,128)(2,1)} %copy-done.57, bf16[512,576]{0,1:T(8,128)(2,1)} %copy-done.129, bf16[512,576]{0,1:T(8,128)(2,1)} %copy-done.128, ...), kind=kOutput, calls=%fused_computation.16 | convolution fusion | flops 7312441344 | bytes 14548992 | tf_op jit(solution)/shard_map/dot_general | solution.py:98
  367.3 7.3 fusion.34
  392.3 8.3 collective-permute-done.88
  402.1 13.3 %collective-permute-done.82 = bf16[192,1728]{1,0:T(8,128)(2,1)S(1)} collective-permute-done((bf16[192,1728]{1,0:T(8,128)(2,1)S(1)}, bf16[192,1728]{1,0:T(8,128)(2,1)S(1)}, u32[]{:S(2)}, u32[]{:S(2)}) %collective-permute-start.82) | collective-permute-done | bytes 663584 | tf_op jit(solution)/shard_map/ppermute | solution.py:86
  415.4 14.7 %collective-permute-done.84 = bf16[192,1728]{1,0:T(8,128)(2,1)S(1)} collective-permute-done((bf16[192,1728]{1,0:T(8,128)(2,1)S(1)}, bf16[192,1728]{1,0:T(8,128)(2,1)S(1)}, u32[]{:S(2)}, u32[]{:S(2)}) %collective-permute-start.84) | collective-permute-done | bytes 663584 | tf_op jit(solution)/shard_map/ppermute | solution.py:86
  431.6 12.9 %collective-permute-done.86 = bf16[192,1728]{1,0:T(8,128)(2,1)S(1)} collective-permute-done((bf16[192,1728]{1,0:T(8,128)(2,1)S(1)}, bf16[192,1728]{1,0:T(8,128)(2,1)S(1)}, u32[]{:S(2)}, u32[]{:S(2)}) %collective-permute-start.86) | collective-permute-done | bytes 663584 | tf_op jit(solution)/shard_map/ppermute | solution.py:86
  457.5 7.5 collective-permute-done.61
  467.4 6.6 collective-permute-done.39
  480.8 36.2 %collective-permute-done.85 = bf16[192,1728]{1,0:T(8,128)(2,1)S(1)} collective-permute-done((bf16[192,1728]{1,0:T(8,128)(2,1)S(1)}, bf16[192,1728]{1,0:T(8,128)(2,1)S(1)}, u32[]{:S(2)}, u32[]{:S(2)}) %collective-permute-start.85) | collective-permute-done | bytes 663584 | tf_op jit(solution)/shard_map/ppermute | solution.py:81
  523.5 23.2 %dynamic_update_slice.101 = bf16[4,192,1728]{2,0,1:T(4,128)(2,1)} dynamic-update-slice(bf16[4,192,1728]{2,0,1:T(4,128)(2,1)} %broadcast_in_dim.161, bf16[1,192,1728]{2,0,1:T(2,128)(2,1)} %copy.239, s32[]{:T(128)S(6)} %select_n.500, s32[]{:T(128)} %constant.655.clone.1, s32[]{:T(128)} %constant.655.clone.1) | dynamic-update-slice | bytes 1327108 | tf_op jit(solution)/shard_map/dynamic_update_slice | solution.py:198
  546.7 22.8 %dynamic_update_slice.102 = bf16[4,192,1728]{2,0,1:T(4,128)(2,1)} dynamic-update-slice(bf16[4,192,1728]{2,0,1:T(4,128)(2,1)} %dynamic_update_slice.101, bf16[1,192,1728]{2,0,1:T(2,128)(2,1)} %copy.240, s32[]{:T(128)S(6)} %select_n.499, s32[]{:T(128)} %constant.655.clone.1, s32[]{:T(128)} %constant.655.clone.1) | dynamic-update-slice | bytes 1327108 | tf_op jit(solution)/shard_map/dynamic_update_slice | solution.py:198
  569.5 22.8 %dynamic_update_slice.103 = bf16[4,192,1728]{2,0,1:T(4,128)(2,1)} dynamic-update-slice(bf16[4,192,1728]{2,0,1:T(4,128)(2,1)} %dynamic_update_slice.102, bf16[1,192,1728]{2,0,1:T(2,128)(2,1)} %copy.241, s32[]{:T(128)S(6)} %select_n.498, s32[]{:T(128)} %constant.655.clone.1, s32[]{:T(128)} %constant.655.clone.1) | dynamic-update-slice | bytes 1327108 | tf_op jit(solution)/shard_map/dynamic_update_slice | solution.py:198
  592.4 22.7 %dynamic_update_slice.104 = bf16[4,192,1728]{2,0,1:T(4,128)(2,1)} dynamic-update-slice(bf16[4,192,1728]{2,0,1:T(4,128)(2,1)} %dynamic_update_slice.103, bf16[1,192,1728]{2,0,1:T(2,128)(2,1)S(1)} %copy.242, s32[]{:T(128)S(6)} %select_n.497, s32[]{:T(128)} %constant.655.clone.1, s32[]{:T(128)} %constant.655.clone.1) | dynamic-update-slice | bytes 1327108 | tf_op jit(solution)/shard_map/dynamic_update_slice | solution.py:198
  631.2 7.4 fusion.198
  650.4 10.2 %shard_map.453 = (f32[512,384]{1,0:T(8,128)S(1)}, f32[2048,128]{1,0:T(8,128)S(1)}, f32[2048,128]{1,0:T(8,128)S(1)}) custom-call(s32[2]{0:T(128)S(1)} %copy-done.10, bf16[512,384]{1,0:T(8,128)(2,1)S(1)} %copy-done.8, bf16[2048,128]{1,0:T(8,128)(2,1)S(1)} %copy-done.6, bf16[2048,128]{1,0:T(8,128)(2,1)S(1)} %copy-done.4, ...), custom_call_target="tpu_custom_call" | custom-call | flops 12000000000 | bytes 8000000 | tf_op jit(solution)/shard_map/pallas_call | solution.py:300
  671.8 10.8 %collective-permute-start.68 = (bf16[512,128]{0,1:T(8,128)(2,1)S(1)}, bf16[512,128]{0,1:T(8,128)(2,1)S(1)}, u32[]{:S(2)}, u32[]{:S(2)}) collective-permute-start(bf16[512,128]{0,1:T(8,128)(2,1)S(1)} %bitcast.285), channel_id=1, source_target_pairs={{0,4},{4,8},{8,12},{12,0},{1,5},{5,9},{9,13},{13,1},{2,6},{6,10},{... | collective-permute-start | bytes 393224 | tf_op jit(solution)/shard_map/ppermute | solution.py:81
  718.8 7.4 collective-permute-done.77
  726.2 7.4 collective-permute-done.75
  775.4 14.9 %collective-permute-start.40 = (bf16[128,1536]{1,0:T(8,128)(2,1)S(1)}, bf16[128,1536]{1,0:T(8,128)(2,1)S(1)}, u32[]{:S(2)}, u32[]{:S(2)}) collective-permute-start(bf16[128,1536]{1,0:T(8,128)(2,1)S(1)} %copy-done.82), channel_id=1, source_target_pairs={{0,4},{4,8},{8,12},{12,0},{1,5},{5,9},{9,13},{13,1},{2,6},{6,10},{... | collective-permute-start | bytes 1179656 | tf_op jit(solution)/shard_map/ppermute | solution.py:81
  790.8 10.5 %collective-permute-done.34 = bf16[128,1536]{1,0:T(8,128)(2,1)S(1)} collective-permute-done((bf16[128,1536]{1,0:T(8,128)(2,1)S(1)}, bf16[128,1536]{1,0:T(8,128)(2,1)S(1)}, u32[]{:S(2)}, u32[]{:S(2)}) %collective-permute-start.34) | collective-permute-done | bytes 393248 | tf_op jit(solution)/shard_map/ppermute | solution.py:81
  807.7 7.4 collective-permute-done.41
  815.4 7.2 collective-permute-done.71
  823.3 33.2 %all-reduce.4 = f32[5120]{0:T(1024)S(1)} all-reduce(f32[5120]{0:T(1024)S(1)} %dynamic_update_slice.107), channel_id=2, replica_groups=mesh['dp'=2,'seq'=4,'head'=4] {'dp','seq'}, use_global_device_ids=true, to_apply=%region_11.12.clone | all-reduce | flops 5120 | bytes 40960
  (641 shorter events, 375.5 us)
Async XLA Ops:
  5.2 113.4 %collective-permute-start = (bf16[192,1024]{1,0:T(8,128)(2,1)}, bf16[192,1024]{1,0:T(8,128)(2,1)}, u32[]{:S(2)}, u32[]{:S(2)}) collective-permute-start(bf16[192,1024]{1,0:T(8,128)(2,1)} %pad_maximum_fusion.1), channel_id=1, source_target_pairs={{0,16},{16,0},{1,17},{17,1},{2,18},{18,2},{3,19},{19,3},{4,20},{20... | collective-permute-start | bytes 1179656 | tf_op jit(solution)/shard_map/ppermute | solution.py:86
  8.2 114.1 %collective-permute-start.1 = (bf16[192,1024]{1,0:T(8,128)(2,1)}, bf16[192,1024]{1,0:T(8,128)(2,1)}, u32[]{:S(2)}, u32[]{:S(2)}) collective-permute-start(bf16[192,1024]{1,0:T(8,128)(2,1)} %pad_maximum_fusion.1), channel_id=1, source_target_pairs={{0,4},{4,8},{8,12},{12,0},{1,5},{5,9},{9,13},{13,1},{2,6},{6,10},{... | collective-permute-start | bytes 1179656 | tf_op jit(solution)/shard_map/ppermute | solution.py:81
  34.6 88.9 %collective-permute-start.14 = (bf16[192,1728]{1,0:T(8,128)(2,1)}, bf16[192,1728]{1,0:T(8,128)(2,1)}, u32[]{:S(2)}, u32[]{:S(2)}) collective-permute-start(bf16[192,1728]{1,0:T(8,128)(2,1)} %get-tuple-element.278), channel_id=1, source_target_pairs={{0,16},{16,0},{1,17},{17,1},{2,18},{18,2},{3,19},{19,3},{4,20},{20... | collective-permute-start | bytes 1990664 | tf_op jit(solution)/shard_map/ppermute | solution.py:86
  36.0 106.2 %collective-permute-start.15 = (bf16[192,1728]{1,0:T(8,128)(2,1)}, bf16[192,1728]{1,0:T(8,128)(2,1)}, u32[]{:S(2)}, u32[]{:S(2)}) collective-permute-start(bf16[192,1728]{1,0:T(8,128)(2,1)} %bitcast.231), channel_id=1, source_target_pairs={{0,4},{4,8},{8,12},{12,0},{1,5},{5,9},{9,13},{13,1},{2,6},{6,10},{... | collective-permute-start | bytes 1990664 | tf_op jit(solution)/shard_map/ppermute | solution.py:81
  38.5 116.2 %collective-permute-start.17 = (bf16[192,1728]{1,0:T(8,128)(2,1)}, bf16[192,1728]{1,0:T(8,128)(2,1)}, u32[]{:S(2)}, u32[]{:S(2)}) collective-permute-start(bf16[192,1728]{1,0:T(8,128)(2,1)} %bitcast.230), channel_id=1, source_target_pairs={{0,8},{4,12},{8,0},{12,4},{1,9},{5,13},{9,1},{13,5},{2,10},{6,14},... | collective-permute-start | bytes 1990664 | tf_op jit(solution)/shard_map/ppermute | solution.py:81
  119.2 35.6 %collective-permute-start.19 = (bf16[192,1728]{1,0:T(8,128)(2,1)S(1)}, bf16[192,1728]{1,0:T(8,128)(2,1)}, u32[]{:S(2)}, u32[]{:S(2)}) collective-permute-start(bf16[192,1728]{1,0:T(8,128)(2,1)S(1)} %bitcast.281), channel_id=1, source_target_pairs={{0,12},{4,0},{8,4},{12,8},{1,13},{5,1},{9,5},{13,9},{2,14},{6,2},{... | collective-permute-start | bytes 1990664 | tf_op jit(solution)/shard_map/ppermute | solution.py:81
  154.9 96.2 %collective-permute-start.18 = (bf16[192,1728]{1,0:T(8,128)(2,1)}, bf16[192,1728]{1,0:T(8,128)(2,1)}, u32[]{:S(2)}, u32[]{:S(2)}) collective-permute-start(bf16[192,1728]{1,0:T(8,128)(2,1)} %collective-permute-done.17), channel_id=1, source_target_pairs={{0,16},{16,0},{1,17},{17,1},{2,18},{18,2},{3,19},{19,3},{4,20},{20... | collective-permute-start | bytes 1990664 | tf_op jit(solution)/shard_map/ppermute | solution.py:86
  165.3 89.1 %collective-permute-start.20 = (bf16[192,1728]{1,0:T(8,128)(2,1)}, bf16[192,1728]{1,0:T(8,128)(2,1)}, u32[]{:S(2)}, u32[]{:S(2)}) collective-permute-start(bf16[192,1728]{1,0:T(8,128)(2,1)} %collective-permute-done.19), channel_id=1, source_target_pairs={{0,16},{16,0},{1,17},{17,1},{2,18},{18,2},{3,19},{19,3},{4,20},{20... | collective-permute-start | bytes 1990664 | tf_op jit(solution)/shard_map/ppermute | solution.py:86
  170.2 99.9 %collective-permute-start.47 = (bf16[256,1536]{1,0:T(8,128)(2,1)S(1)}, bf16[256,1536]{1,0:T(8,128)(2,1)}, u32[]{:S(2)}, u32[]{:S(2)}) collective-permute-start(bf16[256,1536]{1,0:T(8,128)(2,1)S(1)} %maximum_select_fusion.15), channel_id=1, source_target_pairs={{0,1},{1,0},{2,3},{3,2},{4,5},{5,4},{6,7},{7,6},{8,9},{9,8},{10,11... | collective-permute-start | bytes 2359304 | tf_op jit(solution)/shard_map/ppermute | solution.py:86
  173.8 61.6 %collective-permute-start.57 = (bf16[128,1536]{1,0:T(8,128)(2,1)}, bf16[128,1536]{1,0:T(8,128)(2,1)}, u32[]{:S(2)}, u32[]{:S(2)}) collective-permute-start(bf16[128,1536]{1,0:T(8,128)(2,1)} %collective-permute-done.51), channel_id=1, source_target_pairs={{0,4},{4,8},{8,12},{12,0},{1,5},{5,9},{9,13},{13,1},{2,6},{6,10},{... | collective-permute-start | bytes 1179656 | tf_op jit(solution)/shard_map/ppermute | solution.py:81
  178.2 34.5 %collective-permute-start.6 = (bf16[192,1024]{1,0:T(8,128)(2,1)S(1)}, bf16[192,1024]{1,0:T(8,128)(2,1)S(1)}, u32[]{:S(2)}, u32[]{:S(2)}) collective-permute-start(bf16[192,1024]{1,0:T(8,128)(2,1)S(1)} %collective-permute-done.5), channel_id=1, source_target_pairs={{0,16},{16,0},{1,17},{17,1},{2,18},{18,2},{3,19},{19,3},{4,20},{20... | collective-permute-start | bytes 1179656 | tf_op jit(solution)/shard_map/ppermute | solution.py:86
  235.4 49.4 %collective-permute-start.53 = (bf16[256,1536]{1,0:T(8,128)(2,1)S(1)}, bf16[256,1536]{1,0:T(8,128)(2,1)}, u32[]{:S(2)}, u32[]{:S(2)}) collective-permute-start(bf16[256,1536]{1,0:T(8,128)(2,1)S(1)} %maximum_select_fusion.16), channel_id=1, source_target_pairs={{0,1},{1,0},{2,3},{3,2},{4,5},{5,4},{6,7},{7,6},{8,9},{9,8},{10,11... | collective-permute-start | bytes 2359304 | tf_op jit(solution)/shard_map/ppermute | solution.py:86
  331.9 50.5 %collective-permute-start.54 = (bf16[256,1536]{1,0:T(8,128)(2,1)}, bf16[256,1536]{1,0:T(8,128)(2,1)}, u32[]{:S(2)}, u32[]{:S(2)}) collective-permute-start(bf16[256,1536]{1,0:T(8,128)(2,1)} %dynamic-slice_convert_fusion.2), channel_id=1, source_target_pairs={{0,1},{1,0},{2,3},{3,2},{4,5},{5,4},{6,7},{7,6},{8,9},{9,8},{10,11... | collective-permute-start | bytes 2359304 | tf_op jit(solution)/shard_map/ppermute | solution.py:86
  335.3 49.8 %collective-permute-start.32 = (bf16[256,1536]{1,0:T(8,128)(2,1)}, bf16[256,1536]{1,0:T(8,128)(2,1)}, u32[]{:S(2)}, u32[]{:S(2)}) collective-permute-start(bf16[256,1536]{1,0:T(8,128)(2,1)} %dynamic-slice_convert_fusion.6), channel_id=1, source_target_pairs={{0,1},{1,0},{2,3},{3,2},{4,5},{5,4},{6,7},{7,6},{8,9},{9,8},{10,11... | collective-permute-start | bytes 2359304 | tf_op jit(solution)/shard_map/ppermute | solution.py:86
  337.1 50.4 %collective-permute-start.49 = (bf16[128,1536]{1,0:T(8,128)(2,1)}, bf16[128,1536]{1,0:T(8,128)(2,1)S(1)}, u32[]{:S(2)}, u32[]{:S(2)}) collective-permute-start(bf16[128,1536]{1,0:T(8,128)(2,1)} %dynamic-slice_convert_fusion.13), channel_id=1, source_target_pairs={{0,2},{1,3},{2,0},{3,1},{4,6},{5,7},{6,4},{7,5},{8,10},{9,11},{10,... | collective-permute-start | bytes 1179656 | tf_op jit(solution)/shard_map/ppermute | solution.py:86
  339.7 49.8 %collective-permute-start.27 = (bf16[128,1536]{1,0:T(8,128)(2,1)}, bf16[128,1536]{1,0:T(8,128)(2,1)}, u32[]{:S(2)}, u32[]{:S(2)}) collective-permute-start(bf16[128,1536]{1,0:T(8,128)(2,1)} %dynamic-slice_convert_fusion.17), channel_id=1, source_target_pairs={{0,2},{1,3},{2,0},{3,1},{4,6},{5,7},{6,4},{7,5},{8,10},{9,11},{10,... | collective-permute-start | bytes 1179656 | tf_op jit(solution)/shard_map/ppermute | solution.py:86
  367.3 80.5 %collective-permute-start.60 = (bf16[256,1536]{1,0:T(8,128)(2,1)}, bf16[256,1536]{1,0:T(8,128)(2,1)}, u32[]{:S(2)}, u32[]{:S(2)}) collective-permute-start(bf16[256,1536]{1,0:T(8,128)(2,1)} %dynamic-slice_convert_fusion.1), channel_id=1, source_target_pairs={{0,1},{1,0},{2,3},{3,2},{4,5},{5,4},{6,7},{7,6},{8,9},{9,8},{10,11... | collective-permute-start | bytes 2359304 | tf_op jit(solution)/shard_map/ppermute | solution.py:86
  387.5 42.6 %collective-permute-start.84 = (bf16[192,1728]{1,0:T(8,128)(2,1)S(1)}, bf16[192,1728]{1,0:T(8,128)(2,1)S(1)}, u32[]{:S(2)}, u32[]{:S(2)}) collective-permute-start(bf16[192,1728]{1,0:T(8,128)(2,1)S(1)} %get-tuple-element.248), channel_id=1, source_target_pairs={{0,16},{16,0},{1,17},{17,1},{2,18},{18,2},{3,19},{19,3},{4,20},{20... | collective-permute-start | bytes 1990664 | tf_op jit(solution)/shard_map/ppermute | solution.py:86
  389.6 54.9 %collective-permute-start.86 = (bf16[192,1728]{1,0:T(8,128)(2,1)S(1)}, bf16[192,1728]{1,0:T(8,128)(2,1)S(1)}, u32[]{:S(2)}, u32[]{:S(2)}) collective-permute-start(bf16[192,1728]{1,0:T(8,128)(2,1)S(1)} %get-tuple-element.249), channel_id=1, source_target_pairs={{0,16},{16,0},{1,17},{17,1},{2,18},{18,2},{3,19},{19,3},{4,20},{20... | collective-permute-start | bytes 1990664 | tf_op jit(solution)/shard_map/ppermute | solution.py:86
  400.7 224.9 %collective-permute-start.44 = (bf16[128,1536]{1,0:T(8,128)(2,1)}, bf16[128,1536]{1,0:T(8,128)(2,1)S(1)}, u32[]{:S(2)}, u32[]{:S(2)}) collective-permute-start(bf16[128,1536]{1,0:T(8,128)(2,1)} %dynamic-slice_convert_fusion.14), channel_id=1, source_target_pairs={{0,2},{1,3},{2,0},{3,1},{4,6},{5,7},{6,4},{7,5},{8,10},{9,11},{10,... | collective-permute-start | bytes 1179656 | tf_op jit(solution)/shard_map/ppermute | solution.py:86
  415.4 37.6 %collective-permute-start.38 = (bf16[256,1536]{1,0:T(8,128)(2,1)S(1)}, bf16[256,1536]{1,0:T(8,128)(2,1)S(1)}, u32[]{:S(2)}, u32[]{:S(2)}) collective-permute-start(bf16[256,1536]{1,0:T(8,128)(2,1)S(1)} %dynamic-slice_convert_fusion.5), channel_id=1, source_target_pairs={{0,1},{1,0},{2,3},{3,2},{4,5},{5,4},{6,7},{7,6},{8,9},{9,8},{10,11... | collective-permute-start | bytes 2359304 | tf_op jit(solution)/shard_map/ppermute | solution.py:86
  447.8 30.8 %collective-permute-start.83 = (bf16[192,1728]{1,0:T(8,128)(2,1)S(1)}, bf16[192,1728]{1,0:T(8,128)(2,1)S(1)}, u32[]{:S(2)}, u32[]{:S(2)}) collective-permute-start(bf16[192,1728]{1,0:T(8,128)(2,1)S(1)} %get-tuple-element.243), channel_id=1, source_target_pairs={{0,12},{4,0},{8,4},{12,8},{1,13},{5,1},{9,5},{13,9},{2,14},{6,2},{... | collective-permute-start | bytes 1990664 | tf_op jit(solution)/shard_map/ppermute | solution.py:81
  453.0 64.0 %collective-permute-start.85 = (bf16[192,1728]{1,0:T(8,128)(2,1)S(1)}, bf16[192,1728]{1,0:T(8,128)(2,1)S(1)}, u32[]{:S(2)}, u32[]{:S(2)}) collective-permute-start(bf16[192,1728]{1,0:T(8,128)(2,1)S(1)} %get-tuple-element.244), channel_id=1, source_target_pairs={{0,8},{4,12},{8,0},{12,4},{1,9},{5,13},{9,1},{13,5},{2,10},{6,14},... | collective-permute-start | bytes 1990664 | tf_op jit(solution)/shard_map/ppermute | solution.py:81
  453.4 65.7 %collective-permute-start.87 = (bf16[192,1728]{1,0:T(8,128)(2,1)S(1)}, bf16[192,1728]{1,0:T(8,128)(2,1)S(1)}, u32[]{:S(2)}, u32[]{:S(2)}) collective-permute-start(bf16[192,1728]{1,0:T(8,128)(2,1)S(1)} %get-tuple-element.245), channel_id=1, source_target_pairs={{0,4},{4,8},{8,12},{12,0},{1,5},{5,9},{9,13},{13,1},{2,6},{6,10},{... | collective-permute-start | bytes 1990664 | tf_op jit(solution)/shard_map/ppermute | solution.py:81
  474.0 151.6 %collective-permute-start.50 = (bf16[128,1536]{1,0:T(8,128)(2,1)}, bf16[128,1536]{1,0:T(8,128)(2,1)}, u32[]{:S(2)}, u32[]{:S(2)}) collective-permute-start(bf16[128,1536]{1,0:T(8,128)(2,1)} %add_convert_fusion.3), channel_id=1, source_target_pairs={{0,12},{4,0},{8,4},{12,8},{1,13},{5,1},{9,5},{13,9},{2,14},{6,2},{... | collective-permute-start | bytes 1179656 | tf_op jit(solution)/shard_map/ppermute | solution.py:81
  478.6 147.0 %collective-permute-start.56 = (bf16[128,1536]{1,0:T(8,128)(2,1)}, bf16[128,1536]{1,0:T(8,128)(2,1)}, u32[]{:S(2)}, u32[]{:S(2)}) collective-permute-start(bf16[128,1536]{1,0:T(8,128)(2,1)} %add_convert_fusion.2), channel_id=1, source_target_pairs={{0,8},{4,12},{8,0},{12,4},{1,9},{5,13},{9,1},{13,5},{2,10},{6,14},... | collective-permute-start | bytes 1179656 | tf_op jit(solution)/shard_map/ppermute | solution.py:81
  517.0 108.6 %collective-permute-start.62 = (bf16[128,1536]{1,0:T(8,128)(2,1)}, bf16[128,1536]{1,0:T(8,128)(2,1)}, u32[]{:S(2)}, u32[]{:S(2)}) collective-permute-start(bf16[128,1536]{1,0:T(8,128)(2,1)} %add_convert_fusion.1), channel_id=1, source_target_pairs={{0,4},{4,8},{8,12},{12,0},{1,5},{5,9},{9,13},{13,1},{2,6},{6,10},{... | collective-permute-start | bytes 1179656 | tf_op jit(solution)/shard_map/ppermute | solution.py:81
  714.4 54.2 %collective-permute-start.69 = (bf16[256,1536]{1,0:T(8,128)(2,1)S(1)}, bf16[256,1536]{1,0:T(8,128)(2,1)S(1)}, u32[]{:S(2)}, u32[]{:S(2)}) collective-permute-start(bf16[256,1536]{1,0:T(8,128)(2,1)S(1)} %dynamic-slice_convert_fusion), channel_id=1, source_target_pairs={{0,1},{1,0},{2,3},{3,2},{4,5},{5,4},{6,7},{7,6},{8,9},{9,8},{10,11... | collective-permute-start | bytes 2359304 | tf_op jit(solution)/shard_map/ppermute | solution.py:86
  714.5 48.3 %collective-permute-start.79 = (bf16[192,896]{1,0:T(8,128)(2,1)S(1)}, bf16[192,896]{1,0:T(8,128)(2,1)S(1)}, u32[]{:S(2)}, u32[]{:S(2)}) collective-permute-start(bf16[192,896]{1,0:T(8,128)(2,1)S(1)} %get-tuple-element.254), channel_id=1, source_target_pairs={{0,16},{16,0},{1,17},{17,1},{2,18},{18,2},{3,19},{19,3},{4,20},{20... | collective-permute-start | bytes 1032200 | tf_op jit(solution)/shard_map/ppermute | solution.py:86
  764.8 36.5 %collective-permute-start.34 = (bf16[128,1536]{1,0:T(8,128)(2,1)S(1)}, bf16[128,1536]{1,0:T(8,128)(2,1)S(1)}, u32[]{:S(2)}, u32[]{:S(2)}) collective-permute-start(bf16[128,1536]{1,0:T(8,128)(2,1)S(1)} %copy-done.81), channel_id=1, source_target_pairs={{0,8},{4,12},{8,0},{12,4},{1,9},{5,13},{9,1},{13,5},{2,10},{6,14},... | collective-permute-start | bytes 1179656 | tf_op jit(solution)/shard_map/ppermute | solution.py:81
  815.3 47.6 %collective-permute-start.42 = (bf16[256,1536]{1,0:T(8,128)(2,1)S(1)}, bf16[256,1536]{1,0:T(8,128)(2,1)S(1)}, u32[]{:S(2)}, u32[]{:S(2)}) collective-permute-start(bf16[256,1536]{1,0:T(8,128)(2,1)S(1)} %maximum_select_fusion.14), channel_id=1, source_target_pairs={{0,1},{1,0},{2,3},{3,2},{4,5},{5,4},{6,7},{7,6},{8,9},{9,8},{10,11... | collective-permute-start | bytes 2359304 | tf_op jit(solution)/shard_map/ppermute | solution.py:86
  822.8 41.8 %collective-permute-start.72 = (bf16[256,1536]{1,0:T(8,128)(2,1)S(1)}, bf16[256,1536]{1,0:T(8,128)(2,1)S(1)}, u32[]{:S(2)}, u32[]{:S(2)}) collective-permute-start(bf16[256,1536]{1,0:T(8,128)(2,1)S(1)} %maximum_select_fusion.19), channel_id=1, source_target_pairs={{0,1},{1,0},{2,3},{3,2},{4,5},{5,4},{6,7},{7,6},{8,9},{9,8},{10,11... | collective-permute-start | bytes 2359304 | tf_op jit(solution)/shard_map/ppermute | solution.py:86
  (191 other events, 3013.5 us)

commit v2 on v1

--- a/solution.py
+++ b/solution.py
@@ -199,11 +199,13 @@
     return total if scatter else out
 
 
-def visible_blocks(starts_ref, block_rows, half):
-    size = lax.axis_size("seq")
+def hidden_before(starts_ref, half, block, block_rows):
+    return jnp.where(block * block_rows >= starts_ref[half], 0.0, masked_low)
+
+
+def last_block(half):
     index = lax.axis_index("seq")
-    place_block = jnp.where(half == 0, index, 2 * size - 1 - index)
-    return starts_ref[half] // block_rows, place_block
+    return index if half == 0 else 2 * lax.axis_size("seq") - 1 - index
 
 
 def key_offset(block, size, block_rows):
@@ -211,26 +213,37 @@
     return owner * (2 * block_rows) + jnp.where(block < size, 0, block_rows)
 
 
-def attention_forward(starts_ref, q_ref, k_ref, v_ref, o_ref, lse_ref):
+def seen_bias(block_rows, heads):
+    row = lax.broadcasted_iota(jnp.int32, (block_rows, block_rows), 0)
+    col = lax.broadcasted_iota(jnp.int32, (block_rows, block_rows), 1)
+    return jnp.concatenate([jnp.where(col <= row, 0.0, masked_low)] * heads, axis=0)
+
+
+def stacked_heads(ref, half):
+    block_rows, heads = ref.shape[0] // 2, ref.shape[1] // HD
+    rows = pl.ds(half * block_rows, block_rows)
+    return jnp.concatenate([ref[rows, i * HD : (i + 1) * HD] for i in range(heads)], axis=0)
+
+
+def attention_forward(starts_ref, q_ref, k_ref, v_ref, o_ref, lse_ref, halves=(0, 1)):
     local_rows, heads = q_ref.shape[0], q_ref.shape[1] // HD
     block_rows = local_rows // 2
     size = lax.axis_size("seq")
     scale = 1.0 / math.sqrt(HD)
     stacked = heads * block_rows
-    for half in range(2):
-        begin, last = visible_blocks(starts_ref, block_rows, half)
+    for half in halves:
+        last = last_block(half)
         rows = pl.ds(half * block_rows, block_rows)
-        q = jnp.concatenate([q_ref[rows, i * HD : (i + 1) * HD] for i in range(heads)], axis=0)
-
-        def step(block, carried, diagonal, q=q):
+        q = stacked_heads(q_ref, half)
+
+        def step(block, carried, diagonal, q=q, half=half):
             running_max, running_sum, running_out = carried
             keys = pl.ds(pl.multiple_of(key_offset(block, size, block_rows), block_rows), block_rows)
             scores = dot_nt(q, k_ref[keys, :]) * scale
             if diagonal:
-                row = lax.broadcasted_iota(jnp.int32, (block_rows, block_rows), 0)
-                col = lax.broadcasted_iota(jnp.int32, (block_rows, block_rows), 1)
-                seen = jnp.concatenate([jnp.where(col <= row, 0.0, masked_low)] * heads, axis=0)
-                scores = scores + seen
+                scores = scores + seen_bias(block_rows, heads)
+            else:
+                scores = scores + hidden_before(starts_ref, half, block, block_rows)
             new_max = jnp.maximum(running_max, jnp.max(scores, axis=-1, keepdims=True))
             probs = jnp.exp(scores - new_max)
             fade = jnp.exp(running_max - new_max)
@@ -243,7 +256,7 @@
             jnp.zeros((stacked, 1), jnp.float32),
             jnp.zeros((stacked, HD), jnp.float32),
         )
-        carried = lax.fori_loop(begin, last, functools.partial(step, diagonal=False), carried)
+        carried = lax.fori_loop(0, last, functools.partial(step, diagonal=False), carried)
         running_max, running_sum, running_out = step(last, carried, True)
         out = running_out / running_sum
         lse = running_max + jnp.log(running_sum)
@@ -254,35 +267,31 @@
 
 
 def attention_backward(
-    starts_ref, q_ref, k_ref, v_ref, do_ref, o_ref, lse_ref, dq_ref, dk_ref, dv_ref
+    starts_ref, q_ref, k_ref, v_ref, do_ref, o_ref, lse_ref, dq_ref, dk_ref, dv_ref, halves=(0, 1)
 ):
     local_rows, heads = q_ref.shape[0], q_ref.shape[1] // HD
     block_rows = local_rows // 2
     size = lax.axis_size("seq")
     scale = 1.0 / math.sqrt(HD)
     stacked = heads * block_rows
-    dk_ref[...] = jnp.zeros_like(dk_ref)
-    dv_ref[...] = jnp.zeros_like(dv_ref)
-    for half in range(2):
-        begin, last = visible_blocks(starts_ref, block_rows, half)
+    for half in halves:
+        if half == 0:
+            dk_ref[...] = jnp.zeros_like(dk_ref)
+            dv_ref[...] = jnp.zeros_like(dv_ref)
+        last = last_block(half)
         rows = pl.ds(half * block_rows, block_rows)
-
-        def stack(ref):
-            return jnp.concatenate([ref[rows, i * HD : (i + 1) * HD] for i in range(heads)], axis=0)
-
-        q, do = stack(q_ref), stack(do_ref)
-        delta = jnp.sum(wide(do) * stack(o_ref), axis=-1, keepdims=True)
+        q, do = stacked_heads(q_ref, half), stacked_heads(do_ref, half)
+        delta = jnp.sum(wide(do) * stacked_heads(o_ref, half), axis=-1, keepdims=True)
         lse = jnp.concatenate([lse_ref[rows, i : i + 1] for i in range(heads)], axis=0)
 
-        def step(block, dq, diagonal, q=q, do=do, delta=delta, lse=lse):
+        def step(block, dq, diagonal, q=q, do=do, delta=delta, lse=lse, half=half):
             keys = pl.ds(pl.multiple_of(key_offset(block, size, block_rows), block_rows), block_rows)
             k, v = k_ref[keys, :], v_ref[keys, :]
             scores = dot_nt(q, k) * scale
             if diagonal:
-                row = lax.broadcasted_iota(jnp.int32, (block_rows, block_rows), 0)
-                col = lax.broadcasted_iota(jnp.int32, (block_rows, block_rows), 1)
-                seen = jnp.concatenate([jnp.where(col <= row, 0.0, masked_low)] * heads, axis=0)
-                scores = scores + seen
+                scores = scores + seen_bias(block_rows, heads)
+            else:
+                scores = scores + hidden_before(starts_ref, half, block, block_rows)
             probs = jnp.exp(scores - lse)
             score_grad = low(probs * (dot_nt(do, v) - delta))
             dk_ref[keys, :] += dot_tn(score_grad, q) * scale
@@ -290,7 +299,7 @@
             return dq + dot_nn(score_grad, k)
 
         dq = jnp.zeros((stacked, HD), jnp.float32)
-        dq = lax.fori_loop(begin, last, functools.partial(step, diagonal=False), dq)
+        dq = lax.fori_loop(0, last, functools.partial(step, diagonal=False), dq)
         dq = step(last, dq, True) * scale
         for i in range(heads):
             dq_ref[rows, i * HD : (i + 1) * HD] = dq[i * block_rows : (i + 1) * block_rows]
@@ -308,6 +317,876 @@
             flops=12 * 10**9, bytes_accessed=8 * 10**6, transcendentals=10**7
         ),
     )(scalars, *arrays)
+
+
+class Links:
+    def __init__(self, send_sems, recv_sems):
+        self.send_sems, self.recv_sems, self.started = send_sems, recv_sems, []
+
+    def to(self, source, target, **where):
+        number = len(self.started)
+        copy = pltpu.make_async_remote_copy(
+            src_ref=source,
+            dst_ref=target,
+            send_sem=self.send_sems.at[number],
+            recv_sem=self.recv_sems.at[number],
+            device_id=where,
+            device_id_type=pl.DeviceIdType.MESH,
+        )
+        copy.start()
+        self.started.append(copy)
+        return copy
+
+    def finish(self):
+        for copy in self.started:
+            copy.wait_send()
+
+
+def greet(partners):
+    barrier = pltpu.get_barrier_semaphore()
+    for where in partners:
+        pl.semaphore_signal(
+            barrier, inc=1, device_id=where, device_id_type=pl.DeviceIdType.MESH
+        )
+    pl.semaphore_wait(barrier, len(partners))
+
+
+def at_rows(ref, block, size):
+    return ref.at[pl.ds(pl.multiple_of(block * size, size), size), :]
+
+
+def rows_of(begin, size):
+    return pl.ds(pl.multiple_of(begin, size), size)
+
+
+def turn(values, cosine, sine_term):
+    return values * cosine + pltpu.roll(values, HD // 2, 1) * sine_term
+
+
+def vector_of(scal_ref, begin, size):
+    per = scal_ref.shape[2] // 128
+    tiles = []
+    for i in range(size // 128):
+        tile = begin // 128 + i
+        if isinstance(tile, int):
+            owner, column = tile // per, tile % per * 128
+        else:
+            owner, column = lax.div(tile, per), pl.multiple_of(lax.rem(tile, per) * 128, 128)
+        tiles.append(scal_ref[owner, 0:1, pl.ds(column, 128)])
+    return jnp.concatenate(tiles, axis=1)
+
+
+def front_kernel(
+    starts_ref, scal_in, pack, ff_packs, x_ref, cot_ref, cos_ref, sin_ref,
+    scal_ref, attn_w, ff_w, cot_all, normed_ref, q_ref, k_all, v_all, att_ref, lse_ref, hid_ref, nt_ref,
+    send_c, recv_c, send_x, recv_x, kept, send_sems, recv_sems, local_sems,
+):
+    rows, width = x_ref.shape
+    quarter, half = rows // 4, rows // 2
+    block_rows = pack.shape[0]
+    size = lax.axis_size("seq")
+    y, z, head = lax.axis_index("dp"), lax.axis_index("seq"), lax.axis_index("head")
+    core, xx = lax.rem(head, 2), lax.div(head, 2)
+    heads = q_ref.shape[1] // HD
+    wide_heads = heads * HD
+    row_begin = core * half + xx * quarter
+    me = y * size + z
+    ahead = [lax.rem(z + k, size) for k in range(size)]
+    behind = [lax.rem(z + size - k, size) for k in range(size)]
+    to_y, to_x, to_core = {"dp": 1 - y}, {"head": head + 2 - 4 * xx}, {"head": head + 1 - 2 * core}
+    greet([{"seq": ahead[k]} for k in range(1, size)] + [to_y, to_x, to_core])
+    links = Links(send_sems, recv_sems)
+
+    own_scal = pltpu.make_async_copy(scal_in, scal_ref.at[me], local_sems.at[0])
+    own_scal.start()
+    own_pack = pltpu.make_async_copy(pack, at_rows(attn_w, me, block_rows), local_sems.at[1])
+    own_pack.start()
+    own_cot = pltpu.make_async_copy(cot_ref, at_rows(cot_all, z, rows), local_sems.at[2])
+    own_cot.start()
+    own_ff = pltpu.make_async_copy(ff_packs.at[z], at_rows(ff_w, me, block_rows), local_sems.at[3])
+    own_ff.start()
+    scal_z = [links.to(scal_in, scal_ref.at[me], seq=ahead[k]) for k in range(1, size)]
+    scal_y = [links.to(scal_in, scal_ref.at[me], **to_y)]
+    attn_z = [
+        links.to(pack, at_rows(attn_w, me, block_rows), seq=ahead[k]) for k in range(1, size)
+    ]
+    attn_y = [links.to(pack, at_rows(attn_w, me, block_rows), **to_y)]
+    for k in range(1, size):
+        scal_z[k - 1].wait_recv()
+        owner = y * size + behind[k]
+        scal_y.append(links.to(scal_ref.at[owner], scal_ref.at[owner], **to_y))
+    for copy in scal_y:
+        copy.wait_recv()
+    own_scal.wait()
+    gain_one = vector_of(scal_ref, 0, width)
+
+    def norm_rows(i, unused):
+        part = rows_of(i * quarter, quarter)
+        values = wide(x_ref[part, :])
+        scale = lax.rsqrt(jnp.mean(values * values, axis=-1, keepdims=True) + norm_eps)
+        normed_ref[part, :] = low(values * scale * gain_one)
+        return unused
+
+    lax.fori_loop(0, 4, norm_rows, 0)
+    for k in range(1, size):
+        attn_z[k - 1].wait_recv()
+        block = at_rows(attn_w, y * size + behind[k], block_rows)
+        attn_y.append(links.to(block, block, **to_y))
+    ff_z = [
+        links.to(ff_packs.at[ahead[k]], at_rows(ff_w, me, block_rows), seq=ahead[k])
+        for k in range(1, size)
+    ]
+    ff_y = [links.to(ff_packs.at[z], at_rows(ff_w, me, block_rows), **to_y)]
+    own_pack.wait()
+    for copy in attn_y:
+        copy.wait_recv()
+
+    base = 2 * width + H * HD
+    kv_head = lax.div(head * heads, H // KV)
+    bias_q = vector_of(scal_ref, 2 * width + head * wide_heads, wide_heads)
+    bias_k = vector_of(scal_ref, base + kv_head * HD, HD)
+    bias_v = vector_of(scal_ref, base + (KV + kv_head) * HD, HD)
+    own_k, own_v = at_rows(k_all, z, rows), at_rows(v_all, z, rows)
+
+    def project(i, unused):
+        part = rows_of(i * half, half)
+        normed = normed_ref[part, :]
+        cosine, sine_term = cos_ref[part, :], sin_ref[part, :]
+        pre = dot_nn(normed, attn_w[:, 2 * wide_heads : 2 * wide_heads + 2 * HD])
+        own = rows_of(z * rows + i * half, half)
+        k_all[own, :] = low(turn(pre[:, :HD] + bias_k, cosine, sine_term))
+        v_all[own, :] = low(pre[:, HD:] + bias_v)
+        pre = dot_nn(normed, attn_w[:, :wide_heads]) + bias_q
+        for n in range(heads):
+            at = slice(n * HD, (n + 1) * HD)
+            q_ref[part, at] = low(turn(pre[:, at], cosine, sine_term))
+        return unused
+
+    lax.fori_loop(0, 2, project, 0)
+    kv_send = [0] * (size - 1)
+    first = len(links.started)
+    for k in range(1, size):
+        for which, ref in ((0, own_k), (1, own_v)):
+            copy = pltpu.make_async_remote_copy(
+                src_ref=ref, dst_ref=ref,
+                send_sem=send_sems.at[first + k - 1], recv_sem=recv_sems.at[first + k - 1],
+                device_id={"seq": ahead[k]}, device_id_type=pl.DeviceIdType.MESH,
+            )
+            pl.when(core == which)(copy.start)
+        links.started.append(copy)
+        kv_send[k - 1] = copy
+    cot_own = cot_ref.at[rows_of(row_begin, quarter), :]
+    cot_z = [
+        links.to(cot_own, cot_all.at[rows_of(z * rows + row_begin, quarter), :], seq=ahead[k])
+        for k in range(1, size)
+    ]
+    first = len(links.started)
+    for k in range(1, size):
+        kv_send[k - 1].wait_recv()
+        for which, ref in ((0, k_all), (1, v_all)):
+            block = at_rows(ref, behind[k], rows)
+            copy = pltpu.make_async_remote_copy(
+                src_ref=block, dst_ref=block,
+                send_sem=send_sems.at[first + k - 1], recv_sem=recv_sems.at[first + k - 1],
+                device_id=to_core, device_id_type=pl.DeviceIdType.MESH,
+            )
+            pl.when(core == which)(copy.start)
+        links.started.append(copy)
+        kv_send.append(copy)
+    for copy in kv_send[size - 1 :]:
+        copy.wait_recv()
+    attention_forward(starts_ref, q_ref, k_all, v_all, att_ref, lse_ref)
+
+    mixing = attn_w.at[:, wide_heads : 2 * wide_heads]
+
+    def branch_part(begin, size_rows):
+        return dot_nt(low(att_ref[rows_of(begin, size_rows), :]), mixing[...])
+
+    def branch_send(i, unused):
+        part = rows_of(i * quarter, quarter)
+        send_c[part, :] = low(branch_part((1 - core) * half + i * quarter, quarter))
+        return unused
+
+    lax.fori_loop(0, 2, branch_send, 0)
+    to_c = links.to(send_c, recv_c, **to_core)
+
+    def branch_keep(i, unused):
+        part = rows_of(i * quarter, quarter)
+        kept[part, :] = branch_part(core * half + i * quarter, quarter)
+        return unused
+
+    lax.fori_loop(0, 2, branch_keep, 0)
+    to_c.wait_recv()
+    other, mine = rows_of((1 - xx) * quarter, quarter), rows_of(xx * quarter, quarter)
+    send_x[...] = low(kept[other, :] + wide(recv_c[other, :]))
+    to_xx = links.to(send_x, recv_x, **to_x)
+    for k in range(1, size):
+        ff_z[k - 1].wait_recv()
+        block = at_rows(ff_w, y * size + behind[k], block_rows)
+        ff_y.append(links.to(block, block, **to_y))
+    to_xx.wait_recv()
+    gain_two = vector_of(scal_ref, width, width)
+    hidden = wide(x_ref[rows_of(row_begin, quarter), :]) + (
+        kept[mine, :] + wide(recv_c[mine, :]) + wide(recv_x[...])
+    )
+    hid_ref[...] = hidden
+    scale = lax.rsqrt(jnp.mean(hidden * hidden, axis=-1, keepdims=True) + norm_eps)
+    nt_ref[...] = low(hidden * scale * gain_two)
+    cot_x, cot_core = [], []
+    for k in range(1, size):
+        cot_z[k - 1].wait_recv()
+        block = cot_all.at[rows_of(behind[k] * rows + row_begin, quarter), :]
+        cot_x.append(links.to(block, block, **to_x))
+        cot_core.append(links.to(block, block, **to_core))
+    for k in range(1, size):
+        cot_x[k - 1].wait_recv()
+        begin = behind[k] * rows + core * half + (1 - xx) * quarter
+        block = cot_all.at[rows_of(begin, quarter), :]
+        cot_core.append(links.to(block, block, **to_core))
+    for copy in cot_core + ff_y:
+        copy.wait_recv()
+    links.finish()
+    own_cot.wait()
+    own_ff.wait()
+
+
+def front(starts, scal_in, pack, ff_packs, x_rows, cot_rows, cosine, sine_term, wide_heads):
+    rows, width = x_rows.shape
+    size = lax.axis_size("seq")
+    quarter, half, count = rows // 4, rows // 2, 2 * size
+    bf16, f32 = jnp.bfloat16, jnp.float32
+    shape = jax.ShapeDtypeStruct
+    in_vmem_spec, anywhere = pl.BlockSpec(memory_space=pltpu.VMEM), pl.BlockSpec(memory_space=pl.ANY)
+    outs = [
+        (shape((count,) + scal_in.shape, f32), in_vmem_spec),
+        (shape((count * pack.shape[0], pack.shape[1]), bf16), in_vmem_spec),
+        (shape((count * pack.shape[0], ff_packs.shape[2]), bf16), anywhere),
+        (shape((size * rows, width), bf16), anywhere),
+        (shape((rows, width), bf16), in_vmem_spec),
+        (shape((rows, wide_heads), bf16), in_vmem_spec),
+        (shape((size * rows, HD), bf16), in_vmem_spec),
+        (shape((size * rows, HD), bf16), in_vmem_spec),
+        (shape((rows, wide_heads), f32), in_vmem_spec),
+        (shape((rows, wide_heads // HD), f32), in_vmem_spec),
+        (shape((quarter, width), f32), in_vmem_spec),
+        (shape((quarter, width), bf16), in_vmem_spec),
+    ]
+    return pl.pallas_call(
+        front_kernel,
+        out_shape=[o[0] for o in outs],
+        in_specs=[
+            pl.BlockSpec(memory_space=pltpu.SMEM), in_vmem_spec, in_vmem_spec, anywhere,
+            in_vmem_spec, anywhere, in_vmem_spec, in_vmem_spec,
+        ],
+        out_specs=[o[1] for o in outs],
+        scratch_shapes=[
+            pltpu.VMEM((half, width), bf16),
+            pltpu.VMEM((half, width), bf16),
+            pltpu.VMEM((quarter, width), bf16),
+            pltpu.VMEM((quarter, width), bf16),
+            pltpu.VMEM((half, width), f32),
+            pltpu.SemaphoreType.DMA((48,)),
+            pltpu.SemaphoreType.DMA((48,)),
+            pltpu.SemaphoreType.DMA((4,)),
+        ],
+        compiler_params=pltpu.CompilerParams(
+            collective_id=1, has_side_effects=True, vmem_limit_bytes=48 * 1024 * 1024
+        ),
+        cost_estimate=pl.CostEstimate(
+            flops=6 * 10**9, bytes_accessed=30 * 10**6, transcendentals=10**7
+        ),
+    )(starts, scal_in, pack, ff_packs, x_rows, cot_rows, cosine, sine_term)
+
+
+def gated(gate_value, up_value, act_grad):
+    gate_sigmoid = jax.nn.sigmoid(gate_value)
+    silu = gate_value * gate_sigmoid
+    gate_grad = act_grad * up_value * gate_sigmoid * (1.0 + gate_value * (1.0 - gate_sigmoid))
+    return silu * up_value, gate_grad, act_grad * silu
+
+
+def ff_kernel(
+    nt_ref, ff_w, cot_all, hid_ref, scal_ref,
+    hg_ref, bg_ref, gain_ref, gw_ref, out_ref,
+    nt_all, cot_v, w_v, both_v, act_v, send_c, recv_c, kept, send_x, recv_x, send_z, recv_z, total, grad_v, out_v,
+    send_sems, recv_sems, local_sems,
+):
+    quarter, width = nt_ref.shape
+    half, rows = 2 * quarter, 4 * quarter
+    y, z, head = lax.axis_index("dp"), lax.axis_index("seq"), lax.axis_index("head")
+    core, xx = lax.rem(head, 2), lax.div(head, 2)
+    row_begin = core * half + xx * quarter
+    x_begin = core * half + (1 - xx) * quarter
+    wide_units = both_v.shape[1]
+    main = wide_units // 256 * 128
+    owners = [z, z + 1 - 2 * lax.rem(z, 2), lax.rem(z + 2, 4), 3 - z]
+    to_x, to_core = {"head": head + 2 - 4 * xx}, {"head": head + 1 - 2 * core}
+    load_w = pltpu.make_async_copy(ff_w, w_v, local_sems.at[0])
+    load_w.start()
+    load_cot = pltpu.make_async_copy(cot_all, cot_v, local_sems.at[1])
+    load_cot.start()
+    greet([{"seq": owners[d]} for d in (1, 2, 3)] + [to_x, to_core])
+    links = Links(send_sems, recv_sems)
+
+    def piece(owner, begin):
+        return nt_all.at[rows_of(owner * rows + begin, quarter), :]
+
+    nt_x = [links.to(nt_ref, piece(z, row_begin), **to_x)]
+    nt_core = [links.to(nt_ref, piece(z, row_begin), **to_core)]
+    nt_z = [links.to(nt_ref, piece(z, row_begin), seq=owners[1])]
+    nt_z.append(links.to(nt_ref, piece(z, row_begin), seq=owners[2]))
+    nt_all[rows_of(z * rows + row_begin, quarter), :] = nt_ref[...]
+    load_w.wait()
+    load_cot.wait()
+
+    def act_grad_rows(i, unused):
+        part = rows_of(i * half, half)
+        act_v[part, :] = low(dot_nn(cot_v[part, :], w_v[:, wide_units:]))
+        return unused
+
+    def forward(s):
+        block = piece(owners[s], row_begin)
+        if s > 0:
+            nt_z[s - 1].wait_recv()
+            if s == 2:
+                nt_z.append(links.to(block, block, seq=owners[1]))
+            nt_x.append(links.to(block, block, **to_x))
+            nt_core.append(links.to(block, block, **to_core))
+
+    def forward_x(s):
+        nt_x[s].wait_recv()
+        block = piece(owners[s], x_begin)
+        nt_core.append(links.to(block, block, **to_core))
+        return nt_core[-1]
+
+    lax.fori_loop(0, 4, act_grad_rows, 0)
+    first_core = [nt_core[0], forward_x(0)]
+    lax.fori_loop(4, 8, act_grad_rows, 0)
+
+    def gates(begin):
+        part = rows_of(begin, half)
+        values = dot_nn(nt_all[part, :], w_v[:, :wide_units])
+        act_grad = wide(act_v[part, :])
+        act, gate_grad, up_grad = gated(
+            values[:, :main], values[:, main : 2 * main], act_grad[:, :main]
+        )
+        act_v[part, :main] = low(act)
+        both_v[part, :main] = low(gate_grad)
+        both_v[part, main : 2 * main] = low(up_grad)
+        last = values[:, 2 * main :]
+        act, gate_grad, up_grad = gated(last, pltpu.roll(last, 64, 1), act_grad[:, main:])
+        left = lax.broadcasted_iota(jnp.int32, last.shape, 1) < 64
+        act_v[part, main:] = low(jnp.where(left, act, 0.0))
+        both_v[part, 2 * main :] = low(jnp.where(left, gate_grad, pltpu.roll(up_grad, 64, 1)))
+
+    def back_part(begin):
+        return low(dot_nt(both_v[rows_of(begin, half), :], w_v[:, :wide_units]))
+
+    mine, other = rows_of(xx * quarter, quarter), rows_of((1 - xx) * quarter, quarter)
+    steps_c, steps_x, steps_z = [], [], [None]
+
+    def finish_step(s):
+        steps_x[s].wait_recv()
+        value = wide(kept[s % 2, mine, :]) + wide(recv_c[s, mine, :]) + wide(recv_x[s])
+        if s == 0:
+            total[...] = value
+        else:
+            send_z[s - 1] = low(value)
+            steps_z.append(links.to(send_z.at[s - 1], recv_z.at[s - 1], seq=owners[s]))
+
+    core_pairs = [first_core]
+    for s in range(4):
+        for copy in core_pairs[s]:
+            copy.wait_recv()
+        base = owners[s] * rows
+        gates(base + (1 - core) * half)
+        if s >= 2:
+            steps_c[s - 2].wait_send()
+        send_c[s % 2] = back_part(base + (1 - core) * half)
+        steps_c.append(links.to(send_c.at[s % 2], recv_c.at[s], **to_core))
+        if s == 0:
+            forward(1)
+        if s < 3:
+            own_core = nt_core[-1]
+        gates(base + core * half)
+        if s == 0:
+            forward(2)
+        value = back_part(base + core * half)
+        if s > 0:
+            finish_step(s - 1)
+        kept[s % 2] = value
+        steps_c[s].wait_recv()
+        if s >= 2:
+            steps_x[s - 2].wait_send()
+        send_x[s % 2] = low(wide(kept[s % 2, other, :]) + wide(recv_c[s, other, :]))
+        steps_x.append(links.to(send_x.at[s % 2], recv_x.at[s], **to_x))
+        if s == 0:
+            core_pairs.append([nt_core[2], forward_x(1)])
+        if s == 1:
+            forward(3)
+            core_pairs.append([nt_core[3], forward_x(2)])
+        if s == 2:
+            core_pairs.append([nt_core[5], forward_x(3)])
+
+    count = both_v.shape[0] // rows
+    pair_rows = grad_v.shape[1]
+
+    def weight_grads(first, stores):
+        for i in range(2):
+            begin = pl.multiple_of((first * 2 + i) * pair_rows, 128)
+            if len(stores) >= 2:
+                stores[-2].wait()
+            slot = grad_v.at[i]
+            columns = pl.ds(begin, pair_rows)
+            slot[:, :wide_units] = low(dot_tn(nt_all[:, columns], both_v[...]))
+            slot[:, wide_units:] = low(dot_tn(cot_v[:, columns], act_v[...]))
+            store = pltpu.make_async_copy(
+                slot, gw_ref.at[pl.ds(begin, pair_rows), :], local_sems.at[i]
+            )
+            store.start()
+            stores.append(store)
+
+    finish_step(3)
+    stores = []
+    weight_grads(1 - y, stores)
+    n2 = total[...]
+    for s in range(1, 4):
+        steps_z[s].wait_recv()
+        n2 = n2 + wide(recv_z[s - 1])
+    hidden = hid_ref[...]
+    gain_two = vector_of(scal_ref, width, width)
+    scale = lax.rsqrt(jnp.mean(hidden * hidden, axis=-1, keepdims=True) + norm_eps)
+    back, gain_grad = norm_back(n2, hidden, scale, gain_two)
+    gain_ref[...] = gain_grad[None]
+    hidden_grad = wide(cot_v[rows_of(z * rows + row_begin, quarter), :]) + back
+    hg_ref[...] = hidden_grad
+    own = bg_ref.at[rows_of(row_begin, quarter), :]
+    own[...] = low(hidden_grad)
+    bg_x = links.to(own, own, **to_x)
+    bg_core = [links.to(own, own, **to_core)]
+    weight_grads(y, stores)
+    out_stores = []
+    for i in range(2 * count):
+        part = pl.ds(i * half, half)
+        if i >= 2:
+            out_stores[i - 2].wait()
+        out_v[i % 2] = low(dot_nt(act_v[part, :], w_v[:, wide_units:]))
+        store = pltpu.make_async_copy(out_v.at[i % 2], out_ref.at[part, :], local_sems.at[2 + i % 2])
+        store.start()
+        out_stores.append(store)
+        if i == 1:
+            bg_x.wait_recv()
+            block = bg_ref.at[rows_of(x_begin, quarter), :]
+            bg_core.append(links.to(block, block, **to_core))
+    for copy in bg_core:
+        copy.wait_recv()
+    for store in stores[-2:] + out_stores[-2:]:
+        store.wait()
+    waited = {id(copy) for copy in (steps_c[0], steps_c[1], steps_x[0], steps_x[1])}
+    for copy in links.started:
+        if id(copy) not in waited:
+            copy.wait_send()
+
+
+def feed_forward(nt, ff_w, cot_all, hidden, scal, units):
+    quarter, width = nt.shape
+    rows, stream, columns = 4 * quarter, cot_all.shape[0], ff_w.shape[1]
+    bf16, f32 = jnp.bfloat16, jnp.float32
+    shape = jax.ShapeDtypeStruct
+    in_vmem_spec, anywhere = pl.BlockSpec(memory_space=pltpu.VMEM), pl.BlockSpec(memory_space=pl.ANY)
+    outs = [
+        (shape((quarter, width), f32), in_vmem_spec),
+        (shape((rows, width), bf16), in_vmem_spec),
+        (shape((1, width), f32), in_vmem_spec),
+        (shape((width, columns), bf16), anywhere),
+        (shape((stream, width), bf16), anywhere),
+    ]
+    return pl.pallas_call(
+        ff_kernel,
+        out_shape=[o[0] for o in outs],
+        in_specs=[in_vmem_spec, anywhere, anywhere, in_vmem_spec, in_vmem_spec],
+        out_specs=[o[1] for o in outs],
+        scratch_shapes=[
+            pltpu.VMEM((stream, width), bf16),
+            pltpu.VMEM((stream, width), bf16),
+            pltpu.VMEM((width, columns), bf16),
+            pltpu.VMEM((stream, 2 * units), bf16),
+            pltpu.VMEM((stream, columns - 2 * units), bf16),
+            pltpu.VMEM((2, 2 * quarter, width), bf16),
+            pltpu.VMEM((4, 2 * quarter, width), bf16),
+            pltpu.VMEM((2, 2 * quarter, width), bf16),
+            pltpu.VMEM((2, quarter, width), bf16),
+            pltpu.VMEM((4, quarter, width), bf16),
+            pltpu.VMEM((3, quarter, width), bf16),
+            pltpu.VMEM((3, quarter, width), bf16),
+            pltpu.VMEM((quarter, width), f32),
+            pltpu.VMEM((2, width // 4, columns), bf16),
+            pltpu.VMEM((2, 2 * quarter, width), bf16),
+            pltpu.SemaphoreType.DMA((40,)),
+            pltpu.SemaphoreType.DMA((40,)),
+            pltpu.SemaphoreType.DMA((4,)),
+        ],
+        compiler_params=pltpu.CompilerParams(
+            collective_id=2, has_side_effects=True, vmem_limit_bytes=62 * 1024 * 1024
+        ),
+        cost_estimate=pl.CostEstimate(
+            flops=33 * 10**9, bytes_accessed=40 * 10**6, transcendentals=10**6
+        ),
+    )(nt, ff_w, cot_all, hidden, scal)
+
+
+def back_kernel(
+    starts_ref, scal_ref, x_own, hid_ref, hg_ref, gain_two_ref, bg_ref, attn_w, normed_ref, q_ref, k_all, v_all,
+    att_ref, lse_ref, cos_ref, sin_ref, gw_ref, part_ref,
+    layer_ref, input_ref, ff_grads, attn_ref, kv_ref, small_ref,
+    ff_y, ff_own, out_c, out_own, out_sx, out_rx, out_sz, out_rz, dk, dv, do, dq, dkv_s, dkv_r, dkv_rz, dkv_own,
+    qg, one_sc, one_rc, one_keep, one_sx, one_rx, layer_own, input_own, a_other, a_own, a_y, a_z, a_sz,
+    small, small_y, small_s, small_z, small_h, kv_own,
+    send_sems, recv_sems, local_sems,
+):
+    quarter, width = x_own.shape
+    half, rows = 2 * quarter, 4 * quarter
+    block_rows = attn_ref.shape[0]
+    y, z, head = lax.axis_index("dp"), lax.axis_index("seq"), lax.axis_index("head")
+    core, xx = lax.rem(head, 2), lax.div(head, 2)
+    size = lax.axis_size("seq")
+    heads = q_ref.shape[1] // HD
+    wide_heads = heads * HD
+    row_begin = core * half + xx * quarter
+    x_begin = core * half + (1 - xx) * quarter
+    owners = [z, z + 1 - 2 * lax.rem(z, 2), lax.rem(z + 2, 4), 3 - z]
+    to_y, to_x, to_core = {"dp": 1 - y}, {"head": head + 2 - 4 * xx}, {"head": head + 1 - 2 * core}
+    mine, other = rows_of(xx * quarter, quarter), rows_of((1 - xx) * quarter, quarter)
+    is_core = wide(core)
+    loads = []
+
+    def load(source, target):
+        copy = pltpu.make_async_copy(source, target, local_sems.at[len(loads)])
+        copy.start()
+        loads.append(copy)
+        return copy
+
+    greet([to_y] + [{"seq": owners[d]} for d in (1, 2, 3)] + [to_x, to_core])
+    links = Links(send_sems, recv_sems)
+
+    order = (3, 2, 1, 0)
+
+    def grad_rows(ref, which, d):
+        return at_rows(ref, which * size + owners[d], block_rows)
+
+    ff_sent, ff_load = {}, {}
+    for d in order:
+        ff_sent[d] = links.to(grad_rows(gw_ref, 1 - y, d), ff_y.at[d], **to_y)
+    out_sent, out_load = [], []
+    for s in range(4):
+        begin = owners[s] * rows
+        source = part_ref.at[rows_of(begin + (1 - core) * half, half), :]
+        out_sent.append(links.to(source, out_c.at[s], **to_core))
+    for s in range(4):
+        source = part_ref.at[rows_of(owners[s] * rows + core * half, half), :]
+        out_load.append(load(source, out_own.at[s]))
+    for d in order:
+        ff_load[d] = load(grad_rows(gw_ref, y, d), ff_own.at[d])
+
+    ff_over_z = {}
+
+    def ff_step(d):
+        ff_sent[d].wait_recv()
+        ff_load[d].wait()
+
+        def add(i, unused):
+            part = rows_of(i * 64, 64)
+            ff_own[d, part, :] = low(wide(ff_own[d, part, :]) + wide(ff_y[d, part, :]))
+            return unused
+
+        lax.fori_loop(0, block_rows // 64, add, 0)
+        if d == 0:
+            load(ff_own.at[d], ff_grads.at[z])
+        else:
+            ff_over_z[d] = links.to(ff_own.at[d], ff_grads.at[z], seq=owners[d])
+
+    out_x, out_z = [], {}
+
+    def out_step_c(s):
+        out_sent[s].wait_recv()
+        out_load[s].wait()
+        out_sx[s] = low(wide(out_own[s, other, :]) + wide(out_c[s, other, :]))
+        out_x.append(links.to(out_sx.at[s], out_rx.at[s], **to_x))
+
+    def out_value(s):
+        out_x[s].wait_recv()
+        return wide(out_own[s, mine, :]) + wide(out_c[s, mine, :]) + wide(out_rx[s])
+
+    def out_step_x(s):
+        out_sz[s - 1] = low(out_value(s))
+        out_z[s] = links.to(out_sz.at[s - 1], out_rz.at[s - 1], seq=owners[s])
+
+    def do_rows(i, unused):
+        part = rows_of(i * half, half)
+        do[part, :] = low(dot_nn(bg_ref[part, :], attn_w[:, wide_heads : 2 * wide_heads]))
+        return unused
+
+    lax.fori_loop(0, 2, do_rows, 0)
+    attention_backward(starts_ref, q_ref, k_all, v_all, do, att_ref, lse_ref, dq, dk, dv, (0,))
+    for s in (3, 2):
+        pass
+    attention_backward(starts_ref, q_ref, k_all, v_all, do, att_ref, lse_ref, dq, dk, dv, (1,))
+    dkv_s[...] = low(dv[...] * (1.0 - is_core) + dk[...] * is_core)
+    dkv_core = links.to(dkv_s, dkv_r, **to_core)
+    for n in range(heads):
+        at = slice(n * HD, (n + 1) * HD)
+        qg[:, at] = low(turn(dq[:, at], cos_ref[...], -sin_ref[...]))
+    for s in range(4):
+        out_step_c(s)
+    dkv_core.wait_recv()
+
+    def dkv_block(d):
+        part = rows_of(owners[d] * rows, rows)
+        return dk[part, :] * (1.0 - is_core) + dv[part, :] * is_core + wide(dkv_r[part, :])
+
+    dkv_z = []
+    for d in (1, 2, 3):
+        dkv_own[d] = low(dkv_block(d))
+        dkv_z.append(links.to(dkv_own.at[d], dkv_rz.at[d - 1], seq=owners[d]))
+    total = dkv_block(0)
+    ff_step(3)
+    for d in (1, 2, 3):
+        dkv_z[d - 1].wait_recv()
+        total = total + wide(dkv_rz[d - 1])
+    turned = turn(total, cos_ref[...], -sin_ref[...])
+    dkv_own[0] = low(turned * (1.0 - is_core) + total * is_core)
+    key_columns = pl.ds(pl.multiple_of(2 * wide_heads + core * HD, HD), HD)
+
+    def one_part(begin):
+        part = rows_of(begin, quarter)
+        return dot_nt(qg[part, :], attn_w[:, :wide_heads]) + dot_nt(
+            dkv_own[0, part, :], attn_w[:, key_columns]
+        )
+
+    def one_send(i, unused):
+        one_sc[rows_of(i * quarter, quarter), :] = low(one_part((1 - core) * half + i * quarter))
+        return unused
+
+    def one_own(i, unused):
+        one_keep[rows_of(i * quarter, quarter), :] = one_part(core * half + i * quarter)
+        return unused
+
+    lax.fori_loop(0, 2, one_send, 0)
+    one_c = links.to(one_sc, one_rc, **to_core)
+    lax.fori_loop(0, 2, one_own, 0)
+    one_c.wait_recv()
+    one_sx[...] = low(one_keep[other, :] + wide(one_rc[other, :]))
+    one_x = links.to(one_sx, one_rx, **to_x)
+
+    def attn_grads(which, target):
+        columns = pl.ds(pl.multiple_of(which * (width // 2), 128), width // 2)
+        normed = normed_ref[:, columns]
+        target[:, :wide_heads] = low(dot_tn(normed, qg[...]))
+        target[:, wide_heads : 2 * wide_heads] = low(
+            dot_tn(bg_ref[:, columns], low(att_ref[...]))
+        )
+        target[:, 2 * wide_heads :] = low(dot_tn(normed, dkv_own[0]))
+
+    attn_grads(1 - y, a_other)
+    attn_sent = {
+        d: links.to(at_rows(a_other, owners[d], block_rows), a_y.at[d], **to_y) for d in order
+    }
+    attn_grads(y, a_own)
+    ff_step(2)
+    out_step_x(3)
+
+    one_x.wait_recv()
+    norm_one_grad = one_keep[mine, :] + wide(one_rc[mine, :]) + wide(one_rx[...])
+    x_rows = wide(x_own[...])
+    gain_one = vector_of(scal_ref, 0, width)
+    scale = lax.rsqrt(jnp.mean(x_rows * x_rows, axis=-1, keepdims=True) + norm_eps)
+    back, gain_grad = norm_back(norm_one_grad, x_rows, scale, gain_one)
+    input_own[...] = low(hg_ref[...] + back)
+
+    def gather(source, target):
+        place = target.at[rows_of(row_begin, quarter), :]
+        load(source, place)
+        return links.to(source, place, **to_x), [links.to(source, place, **to_core)]
+
+    def gather_on(sent, target):
+        sent[0].wait_recv()
+        block = target.at[rows_of(x_begin, quarter), :]
+        sent[1].append(links.to(block, block, **to_core))
+
+    input_sent = gather(input_own, input_ref)
+    small[...] = jnp.zeros_like(small)
+    per = small.shape[2] // 128
+
+    def put(begin, values):
+        for i in range(values.shape[1] // 128):
+            tile = begin // 128 + i
+            value = values[:, i * 128 : (i + 1) * 128]
+            if isinstance(tile, int):
+                small[tile // per, 0:1, tile % per * 128 : tile % per * 128 + 128] = value
+            else:
+                column = pl.ds(pl.multiple_of(lax.rem(tile, per) * 128, 128), 128)
+                small[lax.div(tile, per), 0:1, column] = value
+
+    put(0, gain_grad[None])
+    put(width, gain_two_ref[...])
+    put(2 * width + head * wide_heads, jnp.sum(wide(qg[...]), axis=0, keepdims=True))
+    kv_begin = 2 * width + H * HD + (core * KV + lax.div(head * heads, H // KV)) * HD
+    put(kv_begin, jnp.sum(wide(dkv_own[0]), axis=0, keepdims=True))
+    small_sent = links.to(small.at[pl.ds((1 - y) * size, size)], small_y, **to_y)
+    out_step_x(2)
+    ff_step(1)
+    out_step_x(1)
+    gather_on(input_sent, input_ref)
+    small_sent.wait_recv()
+    small_s[...] = small[pl.ds(y * size, size)] + small_y[...]
+    small_over_z = [
+        links.to(small_s.at[owners[d]], small_z.at[d - 1], seq=owners[d]) for d in (1, 2, 3)
+    ]
+    layer = hid_ref[...] + out_value(0)
+    attn_over_z = {}
+
+    def attn_step(d):
+        attn_sent[d].wait_recv()
+        block = wide(at_rows(a_own, owners[d], block_rows)[...]) + wide(a_y[d])
+        if d == 0:
+            return block
+        a_sz[d - 1] = low(block)
+        attn_over_z[d] = links.to(a_sz.at[d - 1], a_z.at[d - 1], seq=owners[d])
+        return None
+
+    for d in (3, 2, 1):
+        attn_step(d)
+    for d in (3, 2, 1):
+        out_z[d].wait_recv()
+        layer = layer + wide(out_rz[d - 1])
+    layer_own[...] = low(layer)
+    layer_sent = gather(layer_own, layer_ref)
+    ff_step(0)
+    value = small_s[z]
+    for d in (1, 2, 3):
+        small_over_z[d - 1].wait_recv()
+        value = value + small_z[d - 1]
+    small_h[0] = value
+    small_x = links.to(small_h.at[0], small_h.at[1], **to_x)
+    block = attn_step(0)
+    small_x.wait_recv()
+    small_h[2] = small_h[0] + small_h[1]
+    small_c = links.to(small_h.at[2], small_h.at[3], **to_core)
+    gather_on(layer_sent, layer_ref)
+    for d in (3, 2, 1):
+        attn_over_z[d].wait_recv()
+        block = block + wide(a_z[d - 1])
+    attn_ref[...] = block
+    place = kv_ref.at[core * 2 + xx]
+    kv_own[...] = low(block[:, 2 * wide_heads :])
+    place[...] = kv_own[...]
+    kv_x = links.to(kv_own, place, **to_x)
+    kv_core = [links.to(kv_own, place, **to_core)]
+    small_c.wait_recv()
+    small_ref[...] = small_h[2] + small_h[3]
+    kv_x.wait_recv()
+    place = kv_ref.at[core * 2 + 1 - xx]
+    kv_core.append(links.to(place, place, **to_core))
+    for copy in kv_core + input_sent[1] + layer_sent[1] + [ff_over_z[d] for d in (3, 2, 1)]:
+        copy.wait_recv()
+    links.finish()
+    for copy in loads[8:]:
+        copy.wait()
+
+
+def back(
+    starts, scal, x_own, hidden, hidden_grad, gain_two_grad, branch_grad, attn_w, normed, q, k_all, v_all, attended, lse,
+    cosine, sine_term, gw, out_part,
+):
+    quarter, width = x_own.shape
+    half, rows = 2 * quarter, 4 * quarter
+    size = lax.axis_size("seq")
+    block_rows, columns = gw.shape[0] // (2 * size), gw.shape[1]
+    wide_heads = q.shape[1]
+    attn_columns = 2 * wide_heads + HD
+    stream = k_all.shape[0]
+    bf16, f32 = jnp.bfloat16, jnp.float32
+    shape = jax.ShapeDtypeStruct
+    in_vmem_spec, anywhere = pl.BlockSpec(memory_space=pltpu.VMEM), pl.BlockSpec(memory_space=pl.ANY)
+    outs = [
+        (shape((rows, width), bf16), anywhere),
+        (shape((rows, width), bf16), anywhere),
+        (shape((size, block_rows, columns), bf16), anywhere),
+        (shape((block_rows, attn_columns), f32), in_vmem_spec),
+        (shape((4, block_rows, HD), bf16), in_vmem_spec),
+        (shape(scal.shape[1:], f32), in_vmem_spec),
+    ]
+    small = (size,) + scal.shape[1:]
+    scratch = [
+        ((size, block_rows, columns), bf16),
+        ((size, block_rows, columns), bf16),
+        ((4, half, width), bf16),
+        ((4, half, width), bf16),
+        ((4, quarter, width), bf16),
+        ((4, quarter, width), bf16),
+        ((3, quarter, width), bf16),
+        ((3, quarter, width), bf16),
+        ((stream, HD), f32),
+        ((stream, HD), f32),
+        ((rows, wide_heads), bf16),
+        ((rows, wide_heads), f32),
+        ((stream, HD), bf16),
+        ((stream, HD), bf16),
+        ((3, rows, HD), bf16),
+        ((4, rows, HD), bf16),
+        ((rows, wide_heads), bf16),
+        ((half, width), bf16),
+        ((half, width), bf16),
+        ((half, width), f32),
+        ((quarter, width), bf16),
+        ((quarter, width), bf16),
+        ((quarter, width), bf16),
+        ((quarter, width), bf16),
+        ((width // 2, attn_columns), bf16),
+        ((width // 2, attn_columns), bf16),
+        ((4, block_rows, attn_columns), bf16),
+        ((3, block_rows, attn_columns), bf16),
+        ((3, block_rows, attn_columns), bf16),
+        (scal.shape, f32),
+        (small, f32),
+        (small, f32),
+        ((3,) + scal.shape[1:], f32),
+        ((4,) + scal.shape[1:], f32),
+        ((block_rows, HD), bf16),
+    ]
+    return pl.pallas_call(
+        back_kernel,
+        out_shape=[o[0] for o in outs],
+        in_specs=[pl.BlockSpec(memory_space=pltpu.SMEM)] + [in_vmem_spec] * 15 + [anywhere] * 2,
+        out_specs=[o[1] for o in outs],
+        scratch_shapes=[pltpu.VMEM(*one) for one in scratch]
+        + [
+            pltpu.SemaphoreType.DMA((56,)),
+            pltpu.SemaphoreType.DMA((56,)),
+            pltpu.SemaphoreType.DMA((12,)),
+        ],
+        compiler_params=pltpu.CompilerParams(
+            collective_id=3, has_side_effects=True, vmem_limit_bytes=62 * 1024 * 1024
+        ),
+        cost_estimate=pl.CostEstimate(
+            flops=10 * 10**9, bytes_accessed=40 * 10**6, transcendentals=10**6
+        ),
+    )(
+        starts, scal, x_own, hidden, hidden_grad, gain_two_grad, branch_grad, attn_w, normed, q, k_all, v_all, attended,
+        lse, cosine, sine_term, gw, out_part,
+    )
+
+
+def rope_tables(places):
+    halves = HD // 2
+    powers = jnp.arange(halves, dtype=jnp.float32) * (-2.0 / HD)
+    frequency = jnp.power(jnp.float32(rope_base), powers)
+    angles = places.astype(jnp.float32)[:, None] * frequency[None, :]
+    cosine, sine_term = jnp.cos(angles), jnp.sin(angles)
+    return (
+        jnp.concatenate([cosine, cosine], axis=1),
+        jnp.concatenate([-sine_term, sine_term], axis=1),
+    )
 
 
 def local(
@@ -551,6 +1430,134 @@
     return tuple(results)
 
 
+def local_fast(
+    tokens,
+    cotangent,
+    doc_lengths,
+    queries_master,
+    queries_moment,
+    queries_square,
+    keyvalue_master,
+    keyvalue_moment,
+    keyvalue_square,
+    mixing_master,
+    mixing_moment,
+    mixing_square,
+    expand_master,
+    expand_moment,
+    expand_square,
+    shrink_master,
+    shrink_moment,
+    shrink_square,
+    scalars_master,
+    scalars_moment,
+    scalars_square,
+):
+    local_rows, width = tokens.shape[1], tokens.shape[2]
+    seq_count = lax.axis_size("seq")
+    head_count = lax.axis_size("head")
+    head_index = lax.axis_index("head")
+    seq_index = lax.axis_index("seq")
+    local_heads = H // head_count
+    wide_heads = local_heads * HD
+    kv_head = head_index * local_heads // (H // KV)
+    core = head_index % 2
+    quarter = local_rows // 4
+    row_begin = (head_index % 2) * (2 * quarter) + (head_index // 2) * quarter
+    hidden_units = expand_master.shape[2]
+    units = 64 * -(-hidden_units // (64 * seq_count))
+    more = ((0, 0), (0, units * seq_count - hidden_units))
+
+    attn_pack = jnp.concatenate(
+        [
+            low(queries_master),
+            low(mixing_master).T,
+            low(lax.dynamic_slice_in_dim(keyvalue_master, kv_head * HD, HD, 1)),
+            low(lax.dynamic_slice_in_dim(keyvalue_master, (KV + kv_head) * HD, HD, 1)),
+        ],
+        axis=1,
+    )
+    expand_low = low(expand_master)
+
+    def cut(values):
+        values = jnp.pad(values, more)
+        return values.reshape(values.shape[0], seq_count, units).transpose(1, 0, 2)
+
+    main = units // 128 * 128
+    gate_cut, up_cut = cut(expand_low[:, 0]), cut(expand_low[:, 1])
+    ff_packs = jnp.concatenate(
+        [
+            gate_cut[..., :main],
+            up_cut[..., :main],
+            gate_cut[..., main:],
+            up_cut[..., main:],
+            cut(low(shrink_master).T),
+            jnp.zeros(gate_cut.shape[:2] + (64,), jnp.bfloat16),
+        ],
+        axis=2,
+    )
+    x_low, cot_rows = tokens[0], cotangent[0]
+    lengths = doc_lengths[0]
+    places = folded_places(
+        seq_index * local_rows + jnp.arange(local_rows, dtype=jnp.int32), local_rows, seq_count
+    )
+    starts = doc_starts(places, lengths)
+    half_starts = jnp.stack([starts[0], starts[local_rows // 2]])
+    within = places - starts
+    cosine, sine_term = rope_tables(within)
+    scal_in = jnp.broadcast_to(wide(low(scalars_master))[None], (8, scalars_master.shape[0]))
+    (
+        scal_all, attn_weight, ff_weight, cot_all, normed, queries, all_keys, all_values,
+        attended, log_total, hidden, normed_two,
+    ) = front(
+        half_starts, scal_in, attn_pack, ff_packs, x_low, cot_rows, cosine, sine_term, wide_heads
+    )
+    hidden_grad, branch_grad, gain_two_grad, ff_part, out_part = feed_forward(
+        normed_two, ff_weight, cot_all, hidden, scal_all, units
+    )
+    x_own = lax.dynamic_slice_in_dim(x_low, row_begin, quarter, 0)
+    layer_out, input_grad, ff_grads, attn_grads, kv_blocks, small = back(
+        half_starts, scal_all, x_own, hidden, hidden_grad, gain_two_grad, branch_grad, attn_weight, normed, queries,
+        all_keys, all_values, attended, log_total, cosine, sine_term, ff_part, out_part,
+    )
+    shared_keyvalue = wide(jnp.concatenate([kv_blocks[i] for i in range(4)], axis=1))
+    shared_scalars = small[0]
+
+    def joined(part):
+        if part < 2:
+            rest = 2 * main + part * (units - main)
+            pieces = [
+                ff_grads[:, :, part * main : (part + 1) * main],
+                ff_grads[:, :, rest : rest + units - main],
+            ]
+            part = jnp.concatenate(pieces, axis=2)
+        else:
+            part = ff_grads[:, :, 2 * units : 3 * units]
+        part = part.transpose(1, 0, 2)
+        return wide(part.reshape(part.shape[0], -1)[:, :hidden_units])
+
+    grads = (
+        attn_grads[:, :wide_heads],
+        shared_keyvalue,
+        attn_grads[:, wide_heads : 2 * wide_heads].T,
+        jnp.stack([joined(0), joined(1)], axis=1),
+        joined(2).T,
+        shared_scalars,
+    )
+    masters = (
+        (queries_master, queries_moment, queries_square),
+        (keyvalue_master, keyvalue_moment, keyvalue_square),
+        (mixing_master, mixing_moment, mixing_square),
+        (expand_master, expand_moment, expand_square),
+        (shrink_master, shrink_moment, shrink_square),
+        (scalars_master, scalars_moment, scalars_square),
+    )
+    results = [layer_out[None], input_grad[None]]
+    for held, grad, rate, decay in zip(masters, grads, learn_rates, decay_rates):
+        results.extend(adamw(*held, wide(low(grad)), rate, decay))
+    return tuple(results)
+
+
 def solution(mesh):
     placed = (
         P("dp", "seq", None),
@@ -575,8 +1582,9 @@
         P(("dp", "seq")),
         P(("dp", "seq")),
     )
+    small = dict(mesh.shape) == {"dp": 2, "seq": 4, "head": 4}
     return jax.shard_map(
-        local,
+        local_fast if small else local,
         mesh=mesh,
         in_specs=placed,
         out_specs=(

time: 883 us -> 597 us (0.68)
  the two profiles are of different devices: /device:TPU:0 before, /device:TPU:31 now
where the time goes in v2:
time: 597 us; the launch traced here: 589 us
  Pallas kernels  499 us (84%)
  local copies, waits for them, and re-layouts  65.9 us (11%)
  other arithmetic  23 us (4%)
    pallas_call x1, Pallas kernels, back(): pl.pallas_call(back_kernel, out_shape=[o[0] for o in outs], in_specs=[pl....  193 us
    pallas_call x1, Pallas kernels, front(): pl.pallas_call(front_kernel, out_shape=[o[0] for o in outs], in_specs=[pl...  189 us
    pallas_call x1, Pallas kernels, feed_forward(): pl.pallas_call(ff_kernel, out_shape=[o[0] for o in outs], in_specs=[in_vm...  117 us
    unnamed x74, local copies, waits for them, and re-layouts  33.5 us
    convert_element_type x6, other arithmetic, adamw(): weight.astype(jnp.bfloat16)  15.5 us

profile of v2, /device:TPU:31, one launch (start us, length us, event | category | flops | bytes accessed | tf_op | source)
XLA Modules:
  0.0 589.5 jit_solution(8994749432770771325)
XLA Ops:
  2.7 1.0 convert_element_type.95
  5.3 1.0 fusion.5
  7.1 1.4 pad_add_fusion.starts_ref
  8.5 2.2 copy.96
  10.7 1.0 slice_bitcast_fusion.3
  11.8 1.1 reshape.170
  15.2 2.6 reshape.171
  19.8 1.1 reshape.172
  21.1 5.1 concatenate.22.ff_packs
  26.2 189.4 %shard_map.452 = (f32[8,8,640]{2,1,0:T(8,128)S(1)}, bf16[1536,1024]{1,0:T(8,128)(2,1)}, bf16[1536,1792]{1,0:T(8,128)(2,1)}, bf16[2048,1536]{1,0:T(8,128)(2,1)}, ...) custom-call(s32[2]{0:T(128)S(1)} %pad_add_fusion.starts_ref, ...), custom_call_target="tpu_custom_call" | custom-call | flops 6000000000 | bytes 30000000 | tf_op jit(solution)/shard_map/pallas_call | solution.py:574
  221.8 116.8 %shard_map.453 = (f32[128,1536]{1,0:T(8,128)}, bf16[512,1536]{1,0:T(8,128)(2,1)}, f32[1,1536]{1,0:T(1,128)}, bf16[1536,1792]{1,0:T(8,128)(2,1)}, bf16[2048,1536]{1,0:T(8,128)(2,1)}) custom-call(bf16[128,1536]{1,0:T(8,128)(2,1)} %copy-done.8, bf16[1536,1792]{1,0:T(8,128)(2,1)} %get-tuple-element.58.ff_w, bf16[2048,1536]{1,0:T(8,128)(2,1)} %get-tuple-element.59.cot_all, ...), custom_call_target="tpu_custom_call" | custom-call | flops 32999999488 | bytes 40000000 | tf_op jit(solution)/shard_map/pallas_call | solution.py:804
  338.6 1.8 dynamic-slice_bitcast_fusion.x_own
  340.4 193.0 %shard_map.454 = (bf16[512,1536]{1,0:T(8,128)(2,1)}, bf16[512,1536]{1,0:T(8,128)(2,1)}, bf16[4,192,1792]{2,1,0:T(8,128)(2,1)}, f32[192,896]{1,0:T(8,128)}, bf16[...) custom-call(s32[2]{0:T(128)} %copy-done.2, f32[8,8,640]{2,1,0:T(8,128)} %copy-done.10, ...), custom_call_target="tpu_custom_call" | custom-call | flops 10000000000 | bytes 40000000 | tf_op jit(solution)/shard_map/pallas_call | solution.py:1157
  533.4 1.5 fusion.27
  534.9 1.1 fusion.28
  538.7 1.7 copy.74
  540.4 2.9 reshape.174
  543.3 1.2 slice_bitcast_fusion.1
  544.6 5.2 fusion.19
  549.8 4.5 copy.81
  554.3 4.5 copy.82
  558.8 4.5 copy.83
  563.3 3.0 copy.84
  566.6 4.7 copy.80
  571.3 1.3 slice_bitcast_fusion
  573.4 1.6 reshape.175
  575.1 6.1 %fusion.17 = (bf16[2240,192]{0,1:T(8,128)(2,1)}, f32[2240,192]{0,1:T(8,128)}, f32[2240,192]{0,1:T(8,128)}, f32[2240,192]{0,1:T(8,128)}, f32[2240,192]{0,1:T(8,128)}) fusion(f32[2240,192]{0,1:T(8,128)S(1)} %copy-done.14, f32[2240,192]{0,1:T(8,128)} %param.38, f32[2240,192]{0,1:T(8,128)} %param.37, bf16[192,2304]{1,0:T(8,128)(2,1)} %reshape.175), kind=kLoop, calls=%fused_computation.83 | loop fusion | flops 6881280 | bytes 13762560 | tf_op jit(solution)/shard_map/convert_element_type | solution.py:76
  581.3 1.3 fusion.23
  583.2 1.1 fusion.25
  584.3 1.1 fusion.21
  587.0 1.1 copy.105
  588.1 1.1 copy.106
  (101 shorter events, 20.7 us)
Async XLA Ops:
  6.5 19.7 %copy-start = (f32[512,128]{1,0:T(8,128)}, f32[512,128]{1,0:T(8,128)S(1)}, u32[]{:S(2)}) copy-start(f32[512,128]{1,0:T(8,128)S(1)} %get-tuple-element.187.cos_ref) | copy-start | bytes 786436
  6.5 19.6 %copy-start.1 = (f32[512,128]{1,0:T(8,128)}, f32[512,128]{1,0:T(8,128)S(1)}, u32[]{:S(2)}) copy-start(f32[512,128]{1,0:T(8,128)S(1)} %get-tuple-element.188.sin_ref) | copy-start | bytes 786436
  8.5 17.7 %copy-start.2 = (s32[2]{0:T(128)}, s32[2]{0:T(128)S(1)}, u32[]{:S(2)}) copy-start(s32[2]{0:T(128)S(1)} %pad_add_fusion.starts_ref) | copy-start | bytes 28
  13.0 1.3 copy-start.15
  17.8 1.8 copy-start.13
  21.1 5.1 copy-start.29
  215.6 0.9 copy-start.3
  216.5 0.9 copy-start.4
  217.4 0.8 copy-start.5
  218.2 0.8 copy-start.6
  219.0 0.7 copy-start.7
  219.7 0.7 copy-start.8
  220.4 0.7 copy-start.9
  540.4 4.2 copy-start.11
  563.3 3.0 copy-start.12
  572.6 2.4 copy-start.14
  575.0 6.2 %copy-start.28 = (bf16[4,192,128]{2,1,0:T(8,128)(2,1)S(1)}, bf16[4,192,128]{2,1,0:T(8,128)(2,1)}, u32[]{:S(2)}) copy-start(bf16[4,192,128]{2,1,0:T(8,128)(2,1)} %get-tuple-element.75) | copy-start | bytes 589828
  575.0 6.2 %copy-start.21 = (f32[192,512]{1,0:T(8,128)S(1)}, f32[192,512]{1,0:T(8,128)}, u32[]{:S(2)}) copy-start(f32[192,512]{1,0:T(8,128)} %param.27) | copy-start | bytes 1179652
  575.0 6.2 %copy-start.22 = (f32[192,512]{1,0:T(8,128)S(1)}, f32[192,512]{1,0:T(8,128)}, u32[]{:S(2)}) copy-start(f32[192,512]{1,0:T(8,128)} %param.29) | copy-start | bytes 1179652
  575.0 6.2 %copy-start.23 = (f32[192,512]{1,0:T(8,128)S(1)}, f32[192,512]{1,0:T(8,128)}, u32[]{:S(2)}) copy-start(f32[192,512]{1,0:T(8,128)} %param.28) | copy-start | bytes 1179652
  581.2 1.4 copy-start.20
  581.2 1.4 copy-start.18
  581.3 1.7 copy-start.24
  581.3 1.9 copy-start.25
  582.6 1.7 copy-start.19
  582.6 1.7 copy-start.26
  582.6 1.7 copy-start.27
  583.2 3.1 copy-start.31
  583.2 3.1 copy-start.32
  583.2 3.8 copy-start.17
  585.4 2.7 copy-start.16
  586.3 2.9 copy-start.30
  (1 other events, 0.7 us)

commit v3 on v2

--- a/solution.py
+++ b/solution.py
@@ -5,6 +5,7 @@
 import jax.numpy as jnp
 from jax import lax
 from jax.experimental import pallas as pl
+from jax.experimental.layout import Layout, with_layout_constraint
 from jax.experimental.pallas import tpu as pltpu
 from jax.sharding import PartitionSpec as P
 
@@ -34,9 +35,11 @@
 
 
 def doc_starts(places, lengths):
-    endings = jnp.cumsum(lengths)
-    taken_lengths = jnp.where(endings[None, :] <= places[:, None], lengths[None, :], 0)
-    return jnp.sum(taken_lengths, axis=1)
+    end, total = jnp.int32(0), jnp.zeros_like(places)
+    for i in range(lengths.shape[0]):
+        end = end + lengths[i]
+        total = total + jnp.where(end <= places, lengths[i], 0)
+    return total
 
 
 def rotate(values, places):
@@ -377,9 +380,9 @@
 
 
 def front_kernel(
-    starts_ref, scal_in, pack, ff_packs, x_ref, cot_ref, cos_ref, sin_ref,
-    scal_ref, attn_w, ff_w, cot_all, normed_ref, q_ref, k_all, v_all, att_ref, lse_ref, hid_ref, nt_ref,
-    send_c, recv_c, send_x, recv_x, kept, send_sems, recv_sems, local_sems,
+    starts_ref, scal_in, pack, ff_packs, x_ref, cot_one, cot_two, cos_ref, sin_ref,
+    scal_ref, attn_w, ff_w, cot_all, normed_ref, q_ref, k_all, v_all, att_ref, lse_ref, hid_ref, nt_all,
+    nt_ref, send_c, recv_c, send_x, recv_x, kept, send_sems, recv_sems, local_sem,
 ):
     rows, width = x_ref.shape
     quarter, half = rows // 4, rows // 2
@@ -391,33 +394,24 @@
     wide_heads = heads * HD
     row_begin = core * half + xx * quarter
     me = y * size + z
-    ahead = [lax.rem(z + k, size) for k in range(size)]
-    behind = [lax.rem(z + size - k, size) for k in range(size)]
+    owners = [z, z + 1 - 2 * lax.rem(z, 2), lax.rem(z + 2, 4), 3 - z]
     to_y, to_x, to_core = {"dp": 1 - y}, {"head": head + 2 - 4 * xx}, {"head": head + 1 - 2 * core}
-    greet([{"seq": ahead[k]} for k in range(1, size)] + [to_y, to_x, to_core])
+    greet([{"seq": owners[d]} for d in (1, 2, 3)] + [to_y, to_x, to_core])
     links = Links(send_sems, recv_sems)
 
-    own_scal = pltpu.make_async_copy(scal_in, scal_ref.at[me], local_sems.at[0])
-    own_scal.start()
-    own_pack = pltpu.make_async_copy(pack, at_rows(attn_w, me, block_rows), local_sems.at[1])
-    own_pack.start()
-    own_cot = pltpu.make_async_copy(cot_ref, at_rows(cot_all, z, rows), local_sems.at[2])
-    own_cot.start()
-    own_ff = pltpu.make_async_copy(ff_packs.at[z], at_rows(ff_w, me, block_rows), local_sems.at[3])
-    own_ff.start()
-    scal_z = [links.to(scal_in, scal_ref.at[me], seq=ahead[k]) for k in range(1, size)]
+    scal_ref[me] = scal_in[...]
+    attn_w[rows_of(me * block_rows, block_rows), :] = pack[...]
+    scal_z = {d: links.to(scal_in, scal_ref.at[me], seq=owners[d]) for d in (1, 2, 3)}
     scal_y = [links.to(scal_in, scal_ref.at[me], **to_y)]
-    attn_z = [
-        links.to(pack, at_rows(attn_w, me, block_rows), seq=ahead[k]) for k in range(1, size)
-    ]
-    attn_y = [links.to(pack, at_rows(attn_w, me, block_rows), **to_y)]
-    for k in range(1, size):
-        scal_z[k - 1].wait_recv()
-        owner = y * size + behind[k]
+    attn_own = at_rows(attn_w, me, block_rows)
+    attn_z = {d: links.to(pack, attn_own, seq=owners[d]) for d in (1, 2)}
+    attn_y = [links.to(pack, attn_own, **to_y)]
+    for d in (1, 2, 3):
+        scal_z[d].wait_recv()
+        owner = y * size + owners[d]
         scal_y.append(links.to(scal_ref.at[owner], scal_ref.at[owner], **to_y))
     for copy in scal_y:
         copy.wait_recv()
-    own_scal.wait()
     gain_one = vector_of(scal_ref, 0, width)
 
     def norm_rows(i, unused):
@@ -428,16 +422,45 @@
         return unused
 
     lax.fori_loop(0, 4, norm_rows, 0)
-    for k in range(1, size):
-        attn_z[k - 1].wait_recv()
-        block = at_rows(attn_w, y * size + behind[k], block_rows)
+
+    def attn_arrival(d):
+        attn_z[d].wait_recv()
+        block = at_rows(attn_w, y * size + owners[d], block_rows)
+        if d == 2:
+            attn_z[3] = links.to(block, block, seq=owners[1])
         attn_y.append(links.to(block, block, **to_y))
-    ff_z = [
-        links.to(ff_packs.at[ahead[k]], at_rows(ff_w, me, block_rows), seq=ahead[k])
-        for k in range(1, size)
-    ]
-    ff_y = [links.to(ff_packs.at[z], at_rows(ff_w, me, block_rows), **to_y)]
-    own_pack.wait()
+
+    def quarter_of(ref, d, begin):
+        return ref.at[rows_of(owners[d] * rows + begin, quarter), :]
+
+    x_begin = core * half + (1 - xx) * quarter
+    cot_z = links.to(cot_two, quarter_of(cot_all, 2, row_begin), seq=owners[1])
+    cot_x, cot_core = {}, []
+    for d, ref in ((1, cot_one), (2, cot_two)):
+        cot_x[d] = links.to(ref, quarter_of(cot_all, d, row_begin), **to_x)
+        cot_core.append(links.to(ref, quarter_of(cot_all, d, row_begin), **to_core))
+
+    def cot_on(d):
+        cot_x[d].wait_recv()
+        block = quarter_of(cot_all, d, x_begin)
+        cot_core.append(links.to(block, block, **to_core))
+
+    attn_arrival(2)
+    attn_arrival(1)
+    ff_own = at_rows(ff_w, me, block_rows)
+    ff_z, ff_y = {}, []
+
+    def ff_start(d):
+        ff_z[d] = links.to(ff_packs.at[owners[d]], ff_own, seq=owners[d])
+
+    def ff_arrival(d):
+        ff_z[d].wait_recv()
+        block = at_rows(ff_w, y * size + owners[d], block_rows)
+        ff_y.append(links.to(block, block, **to_y))
+
+    ff_start(2)
+    attn_arrival(3)
+    ff_y.append(links.to(ff_packs.at[z], ff_own, **to_y))
     for copy in attn_y:
         copy.wait_recv()
 
@@ -463,37 +486,37 @@
         return unused
 
     lax.fori_loop(0, 2, project, 0)
-    kv_send = [0] * (size - 1)
-    first = len(links.started)
-    for k in range(1, size):
-        for which, ref in ((0, own_k), (1, own_v)):
+    def keys_or_values(owner, where):
+        number = len(links.started)
+        for which, ref in ((0, k_all), (1, v_all)):
+            block = at_rows(ref, owner, rows)
             copy = pltpu.make_async_remote_copy(
-                src_ref=ref, dst_ref=ref,
-                send_sem=send_sems.at[first + k - 1], recv_sem=recv_sems.at[first + k - 1],
-                device_id={"seq": ahead[k]}, device_id_type=pl.DeviceIdType.MESH,
+                src_ref=block,
+                dst_ref=block,
+                send_sem=send_sems.at[number],
+                recv_sem=recv_sems.at[number],
+                device_id=where,
+                device_id_type=pl.DeviceIdType.MESH,
             )
             pl.when(core == which)(copy.start)
         links.started.append(copy)
-        kv_send[k - 1] = copy
-    cot_own = cot_ref.at[rows_of(row_begin, quarter), :]
-    cot_z = [
-        links.to(cot_own, cot_all.at[rows_of(z * rows + row_begin, quarter), :], seq=ahead[k])
-        for k in range(1, size)
-    ]
-    first = len(links.started)
-    for k in range(1, size):
-        kv_send[k - 1].wait_recv()
-        for which, ref in ((0, k_all), (1, v_all)):
-            block = at_rows(ref, behind[k], rows)
-            copy = pltpu.make_async_remote_copy(
-                src_ref=block, dst_ref=block,
-                send_sem=send_sems.at[first + k - 1], recv_sem=recv_sems.at[first + k - 1],
-                device_id=to_core, device_id_type=pl.DeviceIdType.MESH,
-            )
-            pl.when(core == which)(copy.start)
-        links.started.append(copy)
-        kv_send.append(copy)
-    for copy in kv_send[size - 1 :]:
+        return copy
+
+    kv_z = {d: keys_or_values(z, {"seq": owners[d]}) for d in (3, 2, 1)}
+    kv_core = []
+    ff_start(1)
+    ff_start(3)
+    cot_z.wait_recv()
+    block = quarter_of(cot_all, 3, row_begin)
+    cot_x[3] = links.to(block, block, **to_x)
+    cot_core.append(links.to(block, block, **to_core))
+    cot_on(1)
+    cot_on(2)
+    for d in (1, 2, 3):
+        kv_z[d].wait_recv()
+        kv_core.append(keys_or_values(owners[d], to_core))
+    ff_arrival(2)
+    for copy in kv_core:
         copy.wait_recv()
     attention_forward(starts_ref, q_ref, k_all, v_all, att_ref, lse_ref)
 
@@ -520,10 +543,6 @@
     other, mine = rows_of((1 - xx) * quarter, quarter), rows_of(xx * quarter, quarter)
     send_x[...] = low(kept[other, :] + wide(recv_c[other, :]))
     to_xx = links.to(send_x, recv_x, **to_x)
-    for k in range(1, size):
-        ff_z[k - 1].wait_recv()
-        block = at_rows(ff_w, y * size + behind[k], block_rows)
-        ff_y.append(links.to(block, block, **to_y))
     to_xx.wait_recv()
     gain_two = vector_of(scal_ref, width, width)
     hidden = wide(x_ref[rows_of(row_begin, quarter), :]) + (
@@ -532,25 +551,42 @@
     hid_ref[...] = hidden
     scale = lax.rsqrt(jnp.mean(hidden * hidden, axis=-1, keepdims=True) + norm_eps)
     nt_ref[...] = low(hidden * scale * gain_two)
-    cot_x, cot_core = [], []
-    for k in range(1, size):
-        cot_z[k - 1].wait_recv()
-        block = cot_all.at[rows_of(behind[k] * rows + row_begin, quarter), :]
-        cot_x.append(links.to(block, block, **to_x))
-        cot_core.append(links.to(block, block, **to_core))
-    for k in range(1, size):
-        cot_x[k - 1].wait_recv()
-        begin = behind[k] * rows + core * half + (1 - xx) * quarter
-        block = cot_all.at[rows_of(begin, quarter), :]
-        cot_core.append(links.to(block, block, **to_core))
-    for copy in cot_core + ff_y:
+    own = quarter_of(nt_all, 0, row_begin)
+    own_copy = pltpu.make_async_copy(nt_ref, own, local_sem.at[0])
+    own_copy.start()
+    nt_z = {d: links.to(nt_ref, own, seq=owners[d]) for d in (2, 1)}
+    nt_x = {0: links.to(nt_ref, own, **to_x)}
+    nt_core = [links.to(nt_ref, own, **to_core)]
+
+    def nt_arrival(d):
+        nt_z[d].wait_recv()
+        block = quarter_of(nt_all, d, row_begin)
+        if d == 2:
+            nt_z[3] = links.to(block, block, seq=owners[1])
+        nt_x[d] = links.to(block, block, **to_x)
+        nt_core.append(links.to(block, block, **to_core))
+
+    def nt_on(d):
+        nt_x[d].wait_recv()
+        block = quarter_of(nt_all, d, x_begin)
+        nt_core.append(links.to(block, block, **to_core))
+
+    ff_arrival(1)
+    nt_on(0)
+    cot_on(3)
+    ff_arrival(3)
+    nt_arrival(2)
+    nt_arrival(1)
+    nt_arrival(3)
+    for d in (2, 1, 3):
+        nt_on(d)
+    for copy in cot_core + ff_y + nt_core:
         copy.wait_recv()
     links.finish()
-    own_cot.wait()
-    own_ff.wait()
-
-
-def front(starts, scal_in, pack, ff_packs, x_rows, cot_rows, cosine, sine_term, wide_heads):
+    own_copy.wait()
+
+
+def front(starts, scal_in, pack, ff_packs, x_rows, cot_one, cot_two, cosine, sine_term, wide_heads):
     rows, width = x_rows.shape
     size = lax.axis_size("seq")
     quarter, half, count = rows // 4, rows // 2, 2 * size
@@ -569,25 +605,26 @@
         (shape((rows, wide_heads), f32), in_vmem_spec),
         (shape((rows, wide_heads // HD), f32), in_vmem_spec),
         (shape((quarter, width), f32), in_vmem_spec),
-        (shape((quarter, width), bf16), in_vmem_spec),
+        (shape((size * rows, width), bf16), anywhere),
     ]
     return pl.pallas_call(
         front_kernel,
         out_shape=[o[0] for o in outs],
         in_specs=[
             pl.BlockSpec(memory_space=pltpu.SMEM), in_vmem_spec, in_vmem_spec, anywhere,
-            in_vmem_spec, anywhere, in_vmem_spec, in_vmem_spec,
+            in_vmem_spec, anywhere, anywhere, in_vmem_spec, in_vmem_spec,
         ],
         out_specs=[o[1] for o in outs],
         scratch_shapes=[
+            pltpu.VMEM((quarter, width), bf16),
             pltpu.VMEM((half, width), bf16),
             pltpu.VMEM((half, width), bf16),
             pltpu.VMEM((quarter, width), bf16),
             pltpu.VMEM((quarter, width), bf16),
             pltpu.VMEM((half, width), f32),
-            pltpu.SemaphoreType.DMA((48,)),
-            pltpu.SemaphoreType.DMA((48,)),
-            pltpu.SemaphoreType.DMA((4,)),
+            pltpu.SemaphoreType.DMA((56,)),
+            pltpu.SemaphoreType.DMA((56,)),
+            pltpu.SemaphoreType.DMA((1,)),
         ],
         compiler_params=pltpu.CompilerParams(
             collective_id=1, has_side_effects=True, vmem_limit_bytes=48 * 1024 * 1024
@@ -595,7 +632,7 @@
         cost_estimate=pl.CostEstimate(
             flops=6 * 10**9, bytes_accessed=30 * 10**6, transcendentals=10**7
         ),
-    )(starts, scal_in, pack, ff_packs, x_rows, cot_rows, cosine, sine_term)
+    )(starts, scal_in, pack, ff_packs, x_rows, cot_one, cot_two, cosine, sine_term)
 
 
 def gated(gate_value, up_value, act_grad):
@@ -606,12 +643,12 @@
 
 
 def ff_kernel(
-    nt_ref, ff_w, cot_all, hid_ref, scal_ref,
-    hg_ref, bg_ref, gain_ref, gw_ref, out_ref,
+    nt_ref, ff_w, ff_packs, cot_all, cot_ref, cot_one, cot_two, hid_ref, scal_ref,
+    hg_ref, bg_ref, gain_ref, gw_ref, out_ref, early_ref,
     nt_all, cot_v, w_v, both_v, act_v, send_c, recv_c, kept, send_x, recv_x, send_z, recv_z, total, grad_v, out_v,
     send_sems, recv_sems, local_sems,
 ):
-    quarter, width = nt_ref.shape
+    quarter, width = hid_ref.shape
     half, rows = 2 * quarter, 4 * quarter
     y, z, head = lax.axis_index("dp"), lax.axis_index("seq"), lax.axis_index("head")
     core, xx = lax.rem(head, 2), lax.div(head, 2)
@@ -621,47 +658,43 @@
     main = wide_units // 256 * 128
     owners = [z, z + 1 - 2 * lax.rem(z, 2), lax.rem(z + 2, 4), 3 - z]
     to_x, to_core = {"head": head + 2 - 4 * xx}, {"head": head + 1 - 2 * core}
-    load_w = pltpu.make_async_copy(ff_w, w_v, local_sems.at[0])
-    load_w.start()
-    load_cot = pltpu.make_async_copy(cot_all, cot_v, local_sems.at[1])
-    load_cot.start()
-    greet([{"seq": owners[d]} for d in (1, 2, 3)] + [to_x, to_core])
+    size, block_rows = 4, ff_packs.shape[1]
+    me = y * size + z
+    loads = []
+
+    def load(source, target):
+        copy = pltpu.make_async_copy(source, target, local_sems.at[4 + len(loads)])
+        copy.start()
+        loads.append(copy)
+
+    load(ff_packs.at[z], at_rows(w_v, me, block_rows))
+    for k in range(1, 2 * size):
+        owner = lax.rem(me + k, 2 * size)
+        load(at_rows(ff_w, owner, block_rows), at_rows(w_v, owner, block_rows))
+    load(cot_ref, at_rows(cot_v, z, rows))
+    for d in (1, 2, 3):
+        part = rows_of(owners[d] * rows + row_begin, quarter)
+        load((cot_one, cot_two, cot_all.at[part, :])[d - 1], cot_v.at[part, :])
+        part = rows_of(owners[d] * rows + x_begin, quarter)
+        load(cot_all.at[part, :], cot_v.at[part, :])
+        part = rows_of(owners[d] * rows + (1 - core) * half, half)
+        load(cot_all.at[part, :], cot_v.at[part, :])
+    first_loads = list(loads)
+    load(nt_ref, nt_all)
+    to_y = {"dp": 1 - y}
+    greet([{"seq": owners[d]} for d in (1, 2, 3)] + [to_y, to_x, to_core])
     links = Links(send_sems, recv_sems)
 
-    def piece(owner, begin):
-        return nt_all.at[rows_of(owner * rows + begin, quarter), :]
-
-    nt_x = [links.to(nt_ref, piece(z, row_begin), **to_x)]
-    nt_core = [links.to(nt_ref, piece(z, row_begin), **to_core)]
-    nt_z = [links.to(nt_ref, piece(z, row_begin), seq=owners[1])]
-    nt_z.append(links.to(nt_ref, piece(z, row_begin), seq=owners[2]))
-    nt_all[rows_of(z * rows + row_begin, quarter), :] = nt_ref[...]
-    load_w.wait()
-    load_cot.wait()
+    for copy in first_loads:
+        copy.wait()
 
     def act_grad_rows(i, unused):
         part = rows_of(i * half, half)
         act_v[part, :] = low(dot_nn(cot_v[part, :], w_v[:, wide_units:]))
         return unused
 
-    def forward(s):
-        block = piece(owners[s], row_begin)
-        if s > 0:
-            nt_z[s - 1].wait_recv()
-            if s == 2:
-                nt_z.append(links.to(block, block, seq=owners[1]))
-            nt_x.append(links.to(block, block, **to_x))
-            nt_core.append(links.to(block, block, **to_core))
-
-    def forward_x(s):
-        nt_x[s].wait_recv()
-        block = piece(owners[s], x_begin)
-        nt_core.append(links.to(block, block, **to_core))
-        return nt_core[-1]
-
-    lax.fori_loop(0, 4, act_grad_rows, 0)
-    first_core = [nt_core[0], forward_x(0)]
-    lax.fori_loop(4, 8, act_grad_rows, 0)
+    lax.fori_loop(0, 2 * size, act_grad_rows, 0)
+    loads[-1].wait()
 
     def gates(begin):
         part = rows_of(begin, half)
@@ -683,7 +716,13 @@
         return low(dot_nt(both_v[rows_of(begin, half), :], w_v[:, :wide_units]))
 
     mine, other = rows_of(xx * quarter, quarter), rows_of((1 - xx) * quarter, quarter)
-    steps_c, steps_x, steps_z = [], [], [None]
+    steps_c, steps_x, steps_z = {}, {}, {}
+    sequence = (3, 2, 1, 0)
+
+    def start_step(s):
+        steps_c[s].wait_recv()
+        send_x[s] = low(wide(kept[s % 2, other, :]) + wide(recv_c[s, other, :]))
+        steps_x[s] = links.to(send_x.at[s], recv_x.at[s], **to_x)
 
     def finish_step(s):
         steps_x[s].wait_recv()
@@ -692,41 +731,20 @@
             total[...] = value
         else:
             send_z[s - 1] = low(value)
-            steps_z.append(links.to(send_z.at[s - 1], recv_z.at[s - 1], seq=owners[s]))
-
-    core_pairs = [first_core]
-    for s in range(4):
-        for copy in core_pairs[s]:
-            copy.wait_recv()
+            steps_z[s] = links.to(send_z.at[s - 1], recv_z.at[s - 1], seq=owners[s])
+
+    for s in sequence:
         base = owners[s] * rows
         gates(base + (1 - core) * half)
-        if s >= 2:
-            steps_c[s - 2].wait_send()
+        if s < 2:
+            steps_c[s + 2].wait_send()
         send_c[s % 2] = back_part(base + (1 - core) * half)
-        steps_c.append(links.to(send_c.at[s % 2], recv_c.at[s], **to_core))
-        if s == 0:
-            forward(1)
+        steps_c[s] = links.to(send_c.at[s % 2], recv_c.at[s], **to_core)
+        gates(base + core * half)
+        kept[s % 2] = back_part(base + core * half)
+        start_step(s)
         if s < 3:
-            own_core = nt_core[-1]
-        gates(base + core * half)
-        if s == 0:
-            forward(2)
-        value = back_part(base + core * half)
-        if s > 0:
-            finish_step(s - 1)
-        kept[s % 2] = value
-        steps_c[s].wait_recv()
-        if s >= 2:
-            steps_x[s - 2].wait_send()
-        send_x[s % 2] = low(wide(kept[s % 2, other, :]) + wide(recv_c[s, other, :]))
-        steps_x.append(links.to(send_x.at[s % 2], recv_x.at[s], **to_x))
-        if s == 0:
-            core_pairs.append([nt_core[2], forward_x(1)])
-        if s == 1:
-            forward(3)
-            core_pairs.append([nt_core[3], forward_x(2)])
-        if s == 2:
-            core_pairs.append([nt_core[5], forward_x(3)])
+            finish_step(s + 1)
 
     count = both_v.shape[0] // rows
     pair_rows = grad_v.shape[1]
@@ -746,9 +764,14 @@
             store.start()
             stores.append(store)
 
-    finish_step(3)
     stores = []
     weight_grads(1 - y, stores)
+    finish_step(0)
+    for store in stores:
+        store.wait()
+    stores = []
+    source = at_rows(gw_ref, (1 - y) * size + owners[3], block_rows)
+    early = links.to(source, early_ref, **to_y)
     n2 = total[...]
     for s in range(1, 4):
         steps_z[s].wait_recv()
@@ -778,18 +801,17 @@
             bg_x.wait_recv()
             block = bg_ref.at[rows_of(x_begin, quarter), :]
             bg_core.append(links.to(block, block, **to_core))
-    for copy in bg_core:
+    for copy in bg_core + [early]:
         copy.wait_recv()
     for store in stores[-2:] + out_stores[-2:]:
         store.wait()
-    waited = {id(copy) for copy in (steps_c[0], steps_c[1], steps_x[0], steps_x[1])}
     for copy in links.started:
-        if id(copy) not in waited:
+        if copy is not steps_c[2] and copy is not steps_c[3]:
             copy.wait_send()
 
 
-def feed_forward(nt, ff_w, cot_all, hidden, scal, units):
-    quarter, width = nt.shape
+def feed_forward(nt, ff_w, ff_packs, cot_all, cot, cot_one, cot_two, hidden, scal, units):
+    quarter, width = hidden.shape
     rows, stream, columns = 4 * quarter, cot_all.shape[0], ff_w.shape[1]
     bf16, f32 = jnp.bfloat16, jnp.float32
     shape = jax.ShapeDtypeStruct
@@ -800,11 +822,12 @@
         (shape((1, width), f32), in_vmem_spec),
         (shape((width, columns), bf16), anywhere),
         (shape((stream, width), bf16), anywhere),
+        (shape(ff_packs.shape[1:], bf16), anywhere),
     ]
     return pl.pallas_call(
         ff_kernel,
         out_shape=[o[0] for o in outs],
-        in_specs=[in_vmem_spec, anywhere, anywhere, in_vmem_spec, in_vmem_spec],
+        in_specs=[anywhere] * 7 + [in_vmem_spec] * 2,
         out_specs=[o[1] for o in outs],
         scratch_shapes=[
             pltpu.VMEM((stream, width), bf16),
@@ -815,7 +838,7 @@
             pltpu.VMEM((2, 2 * quarter, width), bf16),
             pltpu.VMEM((4, 2 * quarter, width), bf16),
             pltpu.VMEM((2, 2 * quarter, width), bf16),
-            pltpu.VMEM((2, quarter, width), bf16),
+            pltpu.VMEM((4, quarter, width), bf16),
             pltpu.VMEM((4, quarter, width), bf16),
             pltpu.VMEM((3, quarter, width), bf16),
             pltpu.VMEM((3, quarter, width), bf16),
@@ -824,7 +847,7 @@
             pltpu.VMEM((2, 2 * quarter, width), bf16),
             pltpu.SemaphoreType.DMA((40,)),
             pltpu.SemaphoreType.DMA((40,)),
-            pltpu.SemaphoreType.DMA((4,)),
+            pltpu.SemaphoreType.DMA((28,)),
         ],
         compiler_params=pltpu.CompilerParams(
             collective_id=2, has_side_effects=True, vmem_limit_bytes=62 * 1024 * 1024
@@ -832,12 +855,12 @@
         cost_estimate=pl.CostEstimate(
             flops=33 * 10**9, bytes_accessed=40 * 10**6, transcendentals=10**6
         ),
-    )(nt, ff_w, cot_all, hidden, scal)
+    )(nt, ff_w, ff_packs, cot_all, cot, cot_one, cot_two, hidden, scal)
 
 
 def back_kernel(
     starts_ref, scal_ref, x_own, hid_ref, hg_ref, gain_two_ref, bg_ref, attn_w, normed_ref, q_ref, k_all, v_all,
-    att_ref, lse_ref, cos_ref, sin_ref, gw_ref, part_ref,
+    att_ref, lse_ref, cos_ref, sin_ref, gw_ref, part_ref, early_ref,
     layer_ref, input_ref, ff_grads, attn_ref, kv_ref, small_ref,
     ff_y, ff_own, out_c, out_own, out_sx, out_rx, out_sz, out_rz, dk, dv, do, dq, dkv_s, dkv_r, dkv_rz, dkv_own,
     qg, one_sc, one_rc, one_keep, one_sx, one_rx, layer_own, input_own, a_other, a_own, a_y, a_z, a_sz,
@@ -875,8 +898,12 @@
         return at_rows(ref, which * size + owners[d], block_rows)
 
     ff_sent, ff_load = {}, {}
-    for d in order:
+
+    def ff_start(d):
         ff_sent[d] = links.to(grad_rows(gw_ref, 1 - y, d), ff_y.at[d], **to_y)
+
+    ff_start(2)
+    ff_early = load(early_ref, ff_y.at[3])
     out_sent, out_load = [], []
     for s in range(4):
         begin = owners[s] * rows
@@ -891,7 +918,10 @@
     ff_over_z = {}
 
     def ff_step(d):
-        ff_sent[d].wait_recv()
+        if d == 3:
+            ff_early.wait()
+        else:
+            ff_sent[d].wait_recv()
         ff_load[d].wait()
 
         def add(i, unused):
@@ -905,39 +935,42 @@
         else:
             ff_over_z[d] = links.to(ff_own.at[d], ff_grads.at[z], seq=owners[d])
 
-    out_x, out_z = [], {}
+    out_x, out_z = {}, {}
 
     def out_step_c(s):
         out_sent[s].wait_recv()
         out_load[s].wait()
         out_sx[s] = low(wide(out_own[s, other, :]) + wide(out_c[s, other, :]))
-        out_x.append(links.to(out_sx.at[s], out_rx.at[s], **to_x))
+        out_x[s] = links.to(out_sx.at[s], out_rx.at[s], **to_x)
 
     def out_value(s):
         out_x[s].wait_recv()
         return wide(out_own[s, mine, :]) + wide(out_c[s, mine, :]) + wide(out_rx[s])
 
     def out_step_x(s):
-        out_sz[s - 1] = low(out_value(s))
-        out_z[s] = links.to(out_sz.at[s - 1], out_rz.at[s - 1], seq=owners[s])
+        value = out_value(s)
+        if s == 2:
+            out_z[3].wait_recv()
+            value = value + wide(out_rz[2])
+        out_sz[s - 1] = low(value)
+        out_z[s] = links.to(out_sz.at[s - 1], out_rz.at[s - 1], seq=owners[2 if s == 2 else 1])
 
     def do_rows(i, unused):
         part = rows_of(i * half, half)
         do[part, :] = low(dot_nn(bg_ref[part, :], attn_w[:, wide_heads : 2 * wide_heads]))
         return unused
 
+    ff_step(3)
     lax.fori_loop(0, 2, do_rows, 0)
     attention_backward(starts_ref, q_ref, k_all, v_all, do, att_ref, lse_ref, dq, dk, dv, (0,))
-    for s in (3, 2):
-        pass
+    out_step_c(3)
+    out_step_c(2)
     attention_backward(starts_ref, q_ref, k_all, v_all, do, att_ref, lse_ref, dq, dk, dv, (1,))
     dkv_s[...] = low(dv[...] * (1.0 - is_core) + dk[...] * is_core)
     dkv_core = links.to(dkv_s, dkv_r, **to_core)
     for n in range(heads):
         at = slice(n * HD, (n + 1) * HD)
         qg[:, at] = low(turn(dq[:, at], cos_ref[...], -sin_ref[...]))
-    for s in range(4):
-        out_step_c(s)
     dkv_core.wait_recv()
 
     def dkv_block(d):
@@ -949,7 +982,7 @@
         dkv_own[d] = low(dkv_block(d))
         dkv_z.append(links.to(dkv_own.at[d], dkv_rz.at[d - 1], seq=owners[d]))
     total = dkv_block(0)
-    ff_step(3)
+    ff_step(2)
     for d in (1, 2, 3):
         dkv_z[d - 1].wait_recv()
         total = total + wide(dkv_rz[d - 1])
@@ -991,8 +1024,9 @@
     attn_sent = {
         d: links.to(at_rows(a_other, owners[d], block_rows), a_y.at[d], **to_y) for d in order
     }
+    out_step_c(1)
+    out_step_c(0)
     attn_grads(y, a_own)
-    ff_step(2)
     out_step_x(3)
 
     one_x.wait_recv()
@@ -1033,35 +1067,42 @@
     kv_begin = 2 * width + H * HD + (core * KV + lax.div(head * heads, H // KV)) * HD
     put(kv_begin, jnp.sum(wide(dkv_own[0]), axis=0, keepdims=True))
     small_sent = links.to(small.at[pl.ds((1 - y) * size, size)], small_y, **to_y)
+    ff_start(1)
+    ff_start(0)
+    attn_over_z = {}
+
+    def attn_step(d):
+        attn_sent[d].wait_recv()
+        block = wide(at_rows(a_own, owners[d], block_rows)[...]) + wide(a_y[d])
+        if d == 0:
+            return block
+        if d == 2:
+            attn_over_z[3].wait_recv()
+            block = block + wide(a_z[2])
+        a_sz[d - 1] = low(block)
+        attn_over_z[d] = links.to(
+            a_sz.at[d - 1], a_z.at[d - 1], seq=owners[2 if d == 2 else 1]
+        )
+        return None
+
+    attn_step(3)
+    out_step_x(1)
     out_step_x(2)
-    ff_step(1)
-    out_step_x(1)
     gather_on(input_sent, input_ref)
+    attn_step(1)
+    attn_step(2)
     small_sent.wait_recv()
     small_s[...] = small[pl.ds(y * size, size)] + small_y[...]
     small_over_z = [
         links.to(small_s.at[owners[d]], small_z.at[d - 1], seq=owners[d]) for d in (1, 2, 3)
     ]
     layer = hid_ref[...] + out_value(0)
-    attn_over_z = {}
-
-    def attn_step(d):
-        attn_sent[d].wait_recv()
-        block = wide(at_rows(a_own, owners[d], block_rows)[...]) + wide(a_y[d])
-        if d == 0:
-            return block
-        a_sz[d - 1] = low(block)
-        attn_over_z[d] = links.to(a_sz.at[d - 1], a_z.at[d - 1], seq=owners[d])
-        return None
-
-    for d in (3, 2, 1):
-        attn_step(d)
-    for d in (3, 2, 1):
+    for d in (1, 2):
         out_z[d].wait_recv()
         layer = layer + wide(out_rz[d - 1])
     layer_own[...] = low(layer)
     layer_sent = gather(layer_own, layer_ref)
-    ff_step(0)
+    ff_step(1)
     value = small_s[z]
     for d in (1, 2, 3):
         small_over_z[d - 1].wait_recv()
@@ -1073,7 +1114,7 @@
     small_h[2] = small_h[0] + small_h[1]
     small_c = links.to(small_h.at[2], small_h.at[3], **to_core)
     gather_on(layer_sent, layer_ref)
-    for d in (3, 2, 1):
+    for d in (1, 2):
         attn_over_z[d].wait_recv()
         block = block + wide(a_z[d - 1])
     attn_ref[...] = block
@@ -1087,16 +1128,17 @@
     kv_x.wait_recv()
     place = kv_ref.at[core * 2 + 1 - xx]
     kv_core.append(links.to(place, place, **to_core))
+    ff_step(0)
     for copy in kv_core + input_sent[1] + layer_sent[1] + [ff_over_z[d] for d in (3, 2, 1)]:
         copy.wait_recv()
     links.finish()
-    for copy in loads[8:]:
+    for copy in loads[9:]:
         copy.wait()
 
 
 def back(
     starts, scal, x_own, hidden, hidden_grad, gain_two_grad, branch_grad, attn_w, normed, q, k_all, v_all, attended, lse,
-    cosine, sine_term, gw, out_part,
+    cosine, sine_term, gw, out_part, early,
 ):
     quarter, width = x_own.shape
     half, rows = 2 * quarter, 4 * quarter
@@ -1157,7 +1199,7 @@
     return pl.pallas_call(
         back_kernel,
         out_shape=[o[0] for o in outs],
-        in_specs=[pl.BlockSpec(memory_space=pltpu.SMEM)] + [in_vmem_spec] * 15 + [anywhere] * 2,
+        in_specs=[pl.BlockSpec(memory_space=pltpu.SMEM)] + [in_vmem_spec] * 15 + [anywhere] * 3,
         out_specs=[o[1] for o in outs],
         scratch_shapes=[pltpu.VMEM(*one) for one in scratch]
         + [
@@ -1173,7 +1215,7 @@
         ),
     )(
         starts, scal, x_own, hidden, hidden_grad, gain_two_grad, branch_grad, attn_w, normed, q, k_all, v_all, attended,
-        lse, cosine, sine_term, gw, out_part,
+        lse, cosine, sine_term, gw, out_part, early,
     )
 
 
@@ -1466,7 +1508,10 @@
     row_begin = (head_index % 2) * (2 * quarter) + (head_index // 2) * quarter
     hidden_units = expand_master.shape[2]
     units = 64 * -(-hidden_units // (64 * seq_count))
-    more = ((0, 0), (0, units * seq_count - hidden_units))
+
+    cot_own = lax.dynamic_slice_in_dim(cotangent[0], row_begin, quarter, 0)
+    cot_two = lax.ppermute(cot_own, "seq", [(i, i ^ 2) for i in range(seq_count)])
+    cot_one = lax.ppermute(cot_own, "seq", [(i, i ^ 1) for i in range(seq_count)])
 
     attn_pack = jnp.concatenate(
         [
@@ -1477,25 +1522,26 @@
         ],
         axis=1,
     )
-    expand_low = low(expand_master)
-
-    def cut(values):
-        values = jnp.pad(values, more)
-        return values.reshape(values.shape[0], seq_count, units).transpose(1, 0, 2)
-
     main = units // 128 * 128
-    gate_cut, up_cut = cut(expand_low[:, 0]), cut(expand_low[:, 1])
-    ff_packs = jnp.concatenate(
-        [
-            gate_cut[..., :main],
-            up_cut[..., :main],
-            gate_cut[..., main:],
-            up_cut[..., main:],
-            cut(low(shrink_master).T),
-            jnp.zeros(gate_cut.shape[:2] + (64,), jnp.bfloat16),
-        ],
-        axis=2,
-    )
+    rest = units - main
+    gate_low, up_low = low(expand_master[:, 0]), low(expand_master[:, 1])
+    shrink_low = low(shrink_master).T
+
+    def own_units(values, j):
+        begin = main * seq_count + rest * j
+        last = values[:, begin : begin + rest]
+        last = jnp.pad(last, ((0, 0), (0, rest - last.shape[1])))
+        return values[:, main * j : main * (j + 1)], last
+
+    ff_packs = []
+    for j in range(seq_count):
+        gate_main, gate_rest = own_units(gate_low, j)
+        up_main, up_rest = own_units(up_low, j)
+        shrink_main, shrink_rest = own_units(shrink_low, j)
+        pieces = [gate_main, up_main, gate_rest, up_rest, shrink_main, shrink_rest]
+        pieces.append(jnp.zeros_like(shrink_rest))
+        ff_packs.append(jnp.concatenate(pieces, axis=1))
+    ff_packs = jnp.stack(ff_packs)
     x_low, cot_rows = tokens[0], cotangent[0]
     lengths = doc_lengths[0]
     places = folded_places(
@@ -1508,40 +1554,36 @@
     scal_in = jnp.broadcast_to(wide(low(scalars_master))[None], (8, scalars_master.shape[0]))
     (
         scal_all, attn_weight, ff_weight, cot_all, normed, queries, all_keys, all_values,
-        attended, log_total, hidden, normed_two,
+        attended, log_total, hidden, normed_all,
     ) = front(
-        half_starts, scal_in, attn_pack, ff_packs, x_low, cot_rows, cosine, sine_term, wide_heads
-    )
-    hidden_grad, branch_grad, gain_two_grad, ff_part, out_part = feed_forward(
-        normed_two, ff_weight, cot_all, hidden, scal_all, units
+        half_starts, scal_in, attn_pack, ff_packs, x_low, cot_one, cot_two, cosine, sine_term, wide_heads
+    )
+    hidden_grad, branch_grad, gain_two_grad, ff_part, out_part, early = feed_forward(
+        normed_all, ff_weight, ff_packs, cot_all, cot_rows, cot_one, cot_two, hidden, scal_all, units
     )
     x_own = lax.dynamic_slice_in_dim(x_low, row_begin, quarter, 0)
     layer_out, input_grad, ff_grads, attn_grads, kv_blocks, small = back(
         half_starts, scal_all, x_own, hidden, hidden_grad, gain_two_grad, branch_grad, attn_weight, normed, queries,
-        all_keys, all_values, attended, log_total, cosine, sine_term, ff_part, out_part,
+        all_keys, all_values, attended, log_total, cosine, sine_term, ff_part, out_part, early,
     )
     shared_keyvalue = wide(jnp.concatenate([kv_blocks[i] for i in range(4)], axis=1))
     shared_scalars = small[0]
 
-    def joined(part):
-        if part < 2:
-            rest = 2 * main + part * (units - main)
-            pieces = [
-                ff_grads[:, :, part * main : (part + 1) * main],
-                ff_grads[:, :, rest : rest + units - main],
-            ]
-            part = jnp.concatenate(pieces, axis=2)
-        else:
-            part = ff_grads[:, :, 2 * units : 3 * units]
-        part = part.transpose(1, 0, 2)
-        return wide(part.reshape(part.shape[0], -1)[:, :hidden_units])
-
+    def joined(begin, rest_begin):
+        pieces = [ff_grads[j, :, begin : begin + main] for j in range(seq_count)]
+        for j in range(seq_count):
+            size = min(rest, hidden_units - main * seq_count - rest * j)
+            pieces.append(ff_grads[j, :, rest_begin : rest_begin + size])
+        return jnp.concatenate(pieces, axis=1)
+
+    expand_grad = jnp.stack([joined(0, 2 * main), joined(main, 2 * main + rest)], axis=1)
+    expand_grad = with_layout_constraint(expand_grad, Layout(major_to_minor=(0, 1, 2)))
     grads = (
         attn_grads[:, :wide_heads],
         shared_keyvalue,
         attn_grads[:, wide_heads : 2 * wide_heads].T,
-        jnp.stack([joined(0), joined(1)], axis=1),
-        joined(2).T,
+        expand_grad,
+        joined(2 * units, 2 * units + main).T,
         shared_scalars,
     )
     masters = (

time: 597 us -> 477 us (0.80)
  the two profiles are of different devices: /device:TPU:31 before, /device:TPU:0 now
where the time goes in v3:
time: 477 us; the launch traced here: 470 us
  Pallas kernels  378 us (79%)
  local copies, waits for them, and re-layouts  44.5 us (9%)
  other arithmetic  38.7 us (8%)
  starting transfers between devices  5.61 us (1%)
    pallas_call x1, Pallas kernels, front(): pl.pallas_call(front_kernel, out_shape=[o[0] for o in outs], in_specs=[pl...  155 us
    pallas_call x1, Pallas kernels, back(): pl.pallas_call(back_kernel, out_shape=[o[0] for o in outs], in_specs=[pl....  145 us
    pallas_call x1, Pallas kernels, feed_forward(): pl.pallas_call(ff_kernel, out_shape=[o[0] for o in outs], in_specs=[anywh...  78.5 us
    convert_element_type x6, other arithmetic, adamw(): weight.astype(jnp.bfloat16)  26.8 us
    unnamed x83, local copies, waits for them, and re-layouts  12.7 us
  transfers between devices with their start and end apart: 2, of which 0 were waited for; matrix products, arithmetic and copies ran while one was open for 6% of the time, Pallas kernels for 0%

profile of v3, /device:TPU:0, one launch (start us, length us, event | category | flops | bytes accessed | tf_op | source)
XLA Modules:
  0.0 469.8 jit_solution(11336485585869422612)
XLA Ops:
  0.7 1.8 dynamic-slice_bitcast_fusion.1
  2.5 3.0 collective-permute-start
  5.5 2.6 collective-permute-start.1
  8.1 2.2 copy.61
  10.4 1.1 fusion.30
  17.4 1.3 subtract_convert_fusion
  19.3 1.7 fusion.5
  21.2 1.9 dynamic-slice_bitcast_fusion.x_own
  23.0 1.1 pad_maximum_fusion.3.sin_ref
  24.1 1.1 dynamic-slice_convert_fusion.1
  26.3 2.0 concatenate.37
  28.2 2.0 concatenate.34
  30.3 2.0 concatenate.35
  32.3 2.0 concatenate.36
  34.4 1.4 pad_add_fusion.starts_ref
  35.7 3.0 pad_maximum_fusion.ff_packs
  38.8 155.0 %shard_map.452 = (f32[8,8,640]{2,1,0:T(8,128)S(1)}, bf16[1536,1024]{1,0:T(8,128)(2,1)}, bf16[1536,1792]{1,0:T(8,128)(2,1)}, bf16[2048,1536]{1,0:T(8,128)(2,1)}, ...) custom-call(s32[2]{0:T(128)S(1)} %pad_add_fusion.starts_ref, ...), custom_call_target="tpu_custom_call" | custom-call | flops 6000000000 | bytes 30000000 | tf_op jit(solution)/shard_map/pallas_call | solution.py:610
  199.3 78.5 %shard_map.453 = (f32[128,1536]{1,0:T(8,128)}, bf16[512,1536]{1,0:T(8,128)(2,1)}, f32[1,1536]{1,0:T(1,128)}, bf16[1536,1792]{1,0:T(8,128)(2,1)}, bf16[2048,1536]{1,0:T(8,128)(2,1)}, /*index=5*/bf16[192,1792]{1,0:T(8,128)(2,1)}) custom-call(bf16[2048,1536]{1,0:T(8,128)(2,1)} %get-tuple-element.58.nt_ref, bf16[1536,1792]{1,0:T(8,128)(2,1)} %get-tuple-element.59.ff_w, ...), custom_call_target="tpu_custom_call" | custom-call | flops 32999999488 | bytes 40000000 | tf_op jit(solution)/shard_map/pallas_call | solution.py:827
  277.8 144.6 %shard_map.454 = (bf16[512,1536]{1,0:T(8,128)(2,1)}, bf16[512,1536]{1,0:T(8,128)(2,1)}, bf16[4,192,1792]{2,1,0:T(8,128)(2,1)}, f32[192,896]{1,0:T(8,128)}, bf16[...) custom-call(s32[2]{0:T(128)} %copy-done.4, f32[8,8,640]{2,1,0:T(8,128)} %copy-done.11, ...), custom_call_target="tpu_custom_call" | custom-call | flops 10000000000 | bytes 40000000 | tf_op jit(solution)/shard_map/pallas_call | solution.py:1199
  422.4 2.9 slice_bitcast_fusion.2
  425.3 1.7 slice_bitcast_fusion.14
  427.0 1.4 concatenate.41
  428.4 2.6 copy.58
  431.0 1.6 concatenate.42
  432.6 2.6 copy.59
  436.8 1.1 fusion.24
  437.9 1.1 fusion.20
  440.1 6.6 %fusion.16 = (bf16[2240,192]{0,1:T(8,128)(2,1)}, f32[2240,192]{0,1:T(8,128)}, f32[2240,192]{0,1:T(8,128)}, f32[2240,192]{0,1:T(8,128)}, f32[2240,192]{0,1:T(8,128)}) fusion(f32[2240,192]{0,1:T(8,128)S(1)} %copy-done.13, f32[2240,192]{0,1:T(8,128)} %param.38, f32[2240,192]{0,1:T(8,128)} %param.37, bf16[192,2240]{1,0:T(8,128)(2,1)S(1)} %concatenate.43), kind=kLoop, calls=%fused_computation.95 | loop fusion | flops 6881280 | bytes 13762560 | tf_op jit(solution)/shard_map/convert_element_type | solution.py:79
  449.1 16.0 %fusion.18 = (bf16[192,2,2240]{2,1,0:T(2,128)(2,1)}, f32[192,2,2240]{2,1,0:T(2,128)}, f32[192,2,2240]{2,1,0:T(2,128)}, f32[192,2,2240]{2,1,0:T(2,128)}, f32[192,2,2240]{2,1,0:T(2,128)}) fusion(f32[192,2,2240]{2,1,0:T(2,128)S(1)} %copy-done.12, f32[192,2,2240]{2,1,0:T(2,128)S(1)} %copy-done.16, f32[192,2,2240]{2,1,0:T(2,128)S(1)} %copy-done.17, ...), kind=kLoop, calls=%fused_computation.96 | loop fusion | flops 16343040 | bytes 27525120 | tf_op jit(solution)/shard_map/convert_element_type | solution.py:79
  465.1 1.3 fusion.22
  467.1 1.1 copy.64
  468.3 1.1 copy.65
  (102 shorter events, 17.5 us)
Async XLA Ops:
  2.5 36.3 %collective-permute-start = (bf16[128,1536]{1,0:T(8,128)(2,1)}, bf16[128,1536]{1,0:T(8,128)(2,1)S(1)}, u32[]{:S(2)}, u32[]{:S(2)}) collective-permute-start(bf16[128,1536]{1,0:T(8,128)(2,1)} %dynamic-slice_bitcast_fusion.1), channel_id=1, source_target_pairs={{0,4},{4,0},{8,12},{12,8},{1,5},{5,1},{9,13},{13,9},{2,6},{6,2},{1... | collective-permute-start | bytes 1179656 | tf_op jit(solution)/shard_map/ppermute | solution.py:1514
  5.5 33.3 %collective-permute-start.1 = (bf16[128,1536]{1,0:T(8,128)(2,1)}, bf16[128,1536]{1,0:T(8,128)(2,1)S(1)}, u32[]{:S(2)}, u32[]{:S(2)}) collective-permute-start(bf16[128,1536]{1,0:T(8,128)(2,1)} %dynamic-slice_bitcast_fusion.1), channel_id=1, source_target_pairs={{0,8},{4,12},{8,0},{12,4},{1,9},{5,13},{9,1},{13,5},{2,10},{6,14},... | collective-permute-start | bytes 1179656 | tf_op jit(solution)/shard_map/ppermute | solution.py:1513
  12.5 2.3 copy-start.20
  12.6 3.0 copy-start.39
  12.6 8.6 %copy-start.35 = (f32[640]{0:T(1024)S(1)}, f32[640]{0:T(1024)}, u32[]{:S(2)}) copy-start(f32[640]{0:T(1024)} %param.39) | copy-start | bytes 7684
  21.2 17.6 %copy-start.1 = (f32[512,128]{1,0:T(8,128)}, f32[512,128]{1,0:T(8,128)S(1)}, u32[]{:S(2)}) copy-start(f32[512,128]{1,0:T(8,128)S(1)} %pad_maximum_fusion.2.cos_ref) | copy-start | bytes 786436
  24.1 14.7 %copy-start = (f32[512,128]{1,0:T(8,128)}, f32[512,128]{1,0:T(8,128)S(1)}, u32[]{:S(2)}) copy-start(f32[512,128]{1,0:T(8,128)S(1)} %pad_maximum_fusion.3.sin_ref) | copy-start | bytes 786436
  35.7 3.1 copy-start.4
  38.7 155.1 %copy-start.2 = (bf16[128,1536]{1,0:T(8,128)(2,1)}, bf16[128,1536]{1,0:T(8,128)(2,1)S(1)}, u32[]{:S(2)}) copy-start(bf16[128,1536]{1,0:T(8,128)(2,1)S(1)} %collective-permute-done.cot_one) | copy-start | bytes 1179652
  38.8 155.1 %copy-start.3 = (bf16[128,1536]{1,0:T(8,128)(2,1)}, bf16[128,1536]{1,0:T(8,128)(2,1)S(1)}, u32[]{:S(2)}) copy-start(bf16[128,1536]{1,0:T(8,128)(2,1)S(1)} %collective-permute-done.1.cot_two) | copy-start | bytes 1179652
  432.6 2.6 copy-start.32
  432.6 3.3 copy-start.24
  432.6 4.1 copy-start.21
  432.6 4.1 copy-start.28
  432.6 4.1 copy-start.29
  435.8 2.1 copy-start.23
  435.8 2.1 copy-start.30
  435.8 2.1 copy-start.31
  436.7 9.9 %copy-start.36 = (f32[640]{0:T(1024)}, f32[640]{0:T(1024)S(1)}, u32[]{:S(2)}) copy-start(f32[640]{0:T(1024)S(1)} %fusion.8) | copy-start | bytes 7684
  437.9 8.8 %copy-start.37 = (f32[640]{0:T(1024)S(1)}, f32[640]{0:T(1024)}, u32[]{:S(2)}) copy-start(f32[640]{0:T(1024)} %param.41) | copy-start | bytes 7684
  437.9 8.8 %copy-start.38 = (f32[640]{0:T(1024)S(1)}, f32[640]{0:T(1024)}, u32[]{:S(2)}) copy-start(f32[640]{0:T(1024)} %param.40) | copy-start | bytes 7684
  440.0 7.3 %copy-start.12 = (f32[192,2,2240]{2,1,0:T(2,128)S(1)}, f32[192,2,2240]{2,1,0:T(2,128)}, u32[]{:S(2)}) copy-start(f32[192,2,2240]{2,1,0:T(2,128)} %param.33) | copy-start | bytes 10321924
  440.1 7.3 %copy-start.14 = (bf16[192,1,2240]{2,1,0:T(2,128)(2,1)S(1)}, bf16[192,1,2240]{2,1,0:T(2,128)(2,1)}, u32[]{:S(2)}) copy-start(bf16[192,1,2240]{2,1,0:T(2,128)(2,1)} %copy.58) | copy-start | bytes 2580484
  440.1 7.2 %copy-start.15 = (bf16[192,1,2240]{2,1,0:T(2,128)(2,1)S(1)}, bf16[192,1,2240]{2,1,0:T(2,128)(2,1)}, u32[]{:S(2)}) copy-start(bf16[192,1,2240]{2,1,0:T(2,128)(2,1)} %copy.59) | copy-start | bytes 2580484
  440.1 8.0 %copy-start.16 = (f32[192,2,2240]{2,1,0:T(2,128)S(1)}, f32[192,2,2240]{2,1,0:T(2,128)}, u32[]{:S(2)}) copy-start(f32[192,2,2240]{2,1,0:T(2,128)} %param.35) | copy-start | bytes 10321924
  440.1 9.0 %copy-start.17 = (f32[192,2,2240]{2,1,0:T(2,128)S(1)}, f32[192,2,2240]{2,1,0:T(2,128)}, u32[]{:S(2)}) copy-start(f32[192,2,2240]{2,1,0:T(2,128)} %param.34) | copy-start | bytes 10321924
  449.0 16.0 %copy-start.25 = (f32[192,512]{1,0:T(8,128)S(1)}, f32[192,512]{1,0:T(8,128)}, u32[]{:S(2)}) copy-start(f32[192,512]{1,0:T(8,128)} %param.27) | copy-start | bytes 1179652
  449.0 16.0 %copy-start.26 = (f32[192,512]{1,0:T(8,128)S(1)}, f32[192,512]{1,0:T(8,128)}, u32[]{:S(2)}) copy-start(f32[192,512]{1,0:T(8,128)} %param.29) | copy-start | bytes 1179652
  449.0 16.0 %copy-start.27 = (f32[192,512]{1,0:T(8,128)S(1)}, f32[192,512]{1,0:T(8,128)}, u32[]{:S(2)}) copy-start(f32[192,512]{1,0:T(8,128)} %param.28) | copy-start | bytes 1179652
  449.0 16.0 %copy-start.33 = (bf16[192,128]{1,0:T(8,128)(2,1)S(1)}, bf16[192,128]{1,0:T(8,128)(2,1)}, u32[]{:S(2)}) copy-start(bf16[192,128]{1,0:T(8,128)(2,1)} %get-tuple-element.157) | copy-start | bytes 147460
  449.1 16.0 %copy-start.34 = (bf16[192,128]{1,0:T(8,128)(2,1)S(1)}, bf16[192,128]{1,0:T(8,128)(2,1)}, u32[]{:S(2)}) copy-start(bf16[192,128]{1,0:T(8,128)(2,1)} %get-tuple-element.158) | copy-start | bytes 147460
  465.1 2.0 copy-start.19
  (10 other events, 11.1 us)

commit v4 on v3

--- a/solution.py
+++ b/solution.py
@@ -5,7 +5,6 @@
 import jax.numpy as jnp
 from jax import lax
 from jax.experimental import pallas as pl
-from jax.experimental.layout import Layout, with_layout_constraint
 from jax.experimental.pallas import tpu as pltpu
 from jax.sharding import PartitionSpec as P
 
@@ -379,14 +378,45 @@
     return jnp.concatenate(tiles, axis=1)
 
 
+def cut_units(expand_v, shrink_v, packs):
+    size, main, columns = packs.shape[0], 512, expand_v.shape[2]
+    left = lax.broadcasted_iota(jnp.int32, (16, 128), 1) < 64
+
+    def rows16(i, unused):
+        part = rows_of(i * 16, 16)
+
+        def rests(values):
+            begin = size * main
+            first = values[:, begin : begin + 128]
+            last = jnp.concatenate([values[:, begin + 128 :], jnp.zeros((16, 64), jnp.float32)], axis=1)
+            return first, pltpu.roll(first, 64, 1), last
+
+        gate, up, down = expand_v[part, 0, :], expand_v[part, 1, :], shrink_v[part, :]
+        for j in range(size):
+            own = slice(j * main, (j + 1) * main)
+            packs[j, part, :main] = low(gate[:, own])
+            packs[j, part, main : 2 * main] = low(up[:, own])
+            packs[j, part, 2 * main + 128 : 3 * main + 128] = low(down[:, own])
+        pieces = zip(rests(gate), rests(up), rests(down))
+        for j, (gate_rest, up_rest, down_rest) in enumerate(pieces):
+            both = jnp.where(left, gate_rest, pltpu.roll(up_rest, 64, 1))
+            packs[j, part, 2 * main : 2 * main + 128] = low(both)
+            packs[j, part, 3 * main + 128 :] = low(jnp.where(left, down_rest, 0.0))
+        packs[size - 1, part, 2 * main : 2 * main + 128] = jnp.zeros((16, 128), jnp.bfloat16)
+        packs[size - 1, part, 3 * main + 128 :] = jnp.zeros((16, 128), jnp.bfloat16)
+        return unused
+
+    lax.fori_loop(0, packs.shape[1] // 16, rows16, 0)
+
+
 def front_kernel(
-    starts_ref, scal_in, pack, ff_packs, x_ref, cot_one, cot_two, cos_ref, sin_ref,
-    scal_ref, attn_w, ff_w, cot_all, normed_ref, q_ref, k_all, v_all, att_ref, lse_ref, hid_ref, nt_all,
-    nt_ref, send_c, recv_c, send_x, recv_x, kept, send_sems, recv_sems, local_sem,
+    starts_ref, scal_in, query_ref, kv_ref, mixing_ref, expand_ref, shrink_ref, x_ref, cot_ref, cos_ref, sin_ref,
+    scal_ref, attn_w, mix_w, ff_w, cot_all, normed_ref, q_ref, k_all, v_all, att_ref, lse_ref, hid_ref, nt_all,
+    expand_v, shrink_v, ff_packs, nt_ref, send_c, recv_c, send_x, recv_x, kept, send_sems, recv_sems, local_sem,
 ):
     rows, width = x_ref.shape
     quarter, half = rows // 4, rows // 2
-    block_rows = pack.shape[0]
+    block_rows = query_ref.shape[0]
     size = lax.axis_size("seq")
     y, z, head = lax.axis_index("dp"), lax.axis_index("seq"), lax.axis_index("head")
     core, xx = lax.rem(head, 2), lax.div(head, 2)
@@ -400,12 +430,25 @@
     links = Links(send_sems, recv_sems)
 
     scal_ref[me] = scal_in[...]
-    attn_w[rows_of(me * block_rows, block_rows), :] = pack[...]
+    load_expand = pltpu.make_async_copy(expand_ref, expand_v, local_sem.at[1])
+    load_expand.start()
+    load_shrink = pltpu.make_async_copy(shrink_ref, shrink_v, local_sem.at[2])
+    load_shrink.start()
+    kv_head = lax.div(head * heads, H // KV)
+    own_rows = rows_of(me * block_rows, block_rows)
+    attn_w[own_rows, :wide_heads] = low(query_ref[...])
+    for i, column in enumerate((kv_head, KV + kv_head)):
+        columns = pl.ds(pl.multiple_of(column * HD, HD), HD)
+        attn_w[own_rows, wide_heads + i * HD : wide_heads + (i + 1) * HD] = low(kv_ref[:, columns])
+    mix_w[own_rows, :] = low(mixing_ref[...])
     scal_z = {d: links.to(scal_in, scal_ref.at[me], seq=owners[d]) for d in (1, 2, 3)}
     scal_y = [links.to(scal_in, scal_ref.at[me], **to_y)]
     attn_own = at_rows(attn_w, me, block_rows)
-    attn_z = {d: links.to(pack, attn_own, seq=owners[d]) for d in (1, 2)}
-    attn_y = [links.to(pack, attn_own, **to_y)]
+    attn_z = {d: links.to(attn_own, attn_own, seq=owners[d]) for d in (1, 2)}
+    attn_y = [links.to(attn_own, attn_own, **to_y)]
+    mix_own = at_rows(mix_w, me, block_rows)
+    mix_z = {d: links.to(mix_own, mix_own, seq=owners[d]) for d in (1, 2)}
+    mix_y = []
     for d in (1, 2, 3):
         scal_z[d].wait_recv()
         owner = y * size + owners[d]
@@ -430,24 +473,45 @@
             attn_z[3] = links.to(block, block, seq=owners[1])
         attn_y.append(links.to(block, block, **to_y))
 
+    def mix_arrival(d):
+        mix_z[d].wait_recv()
+        block = at_rows(mix_w, y * size + owners[d], block_rows)
+        if d == 2:
+            mix_z[3] = links.to(block, block, seq=owners[1])
+        mix_y.append(links.to(block, block, **to_y))
+
+    load_expand.wait()
+    load_shrink.wait()
+    cut_units(expand_v, shrink_v, ff_packs)
+    attn_arrival(2)
+    attn_arrival(1)
+    mix_arrival(2)
+    mix_arrival(1)
+    x_begin = core * half + (1 - xx) * quarter
+
     def quarter_of(ref, d, begin):
         return ref.at[rows_of(owners[d] * rows + begin, quarter), :]
 
-    x_begin = core * half + (1 - xx) * quarter
-    cot_z = links.to(cot_two, quarter_of(cot_all, 2, row_begin), seq=owners[1])
+    cot_own = cot_ref.at[rows_of(row_begin, quarter), :]
+    cot_z = {d: links.to(cot_own, quarter_of(cot_all, 0, row_begin), seq=owners[d]) for d in (2, 1)}
     cot_x, cot_core = {}, []
-    for d, ref in ((1, cot_one), (2, cot_two)):
-        cot_x[d] = links.to(ref, quarter_of(cot_all, d, row_begin), **to_x)
-        cot_core.append(links.to(ref, quarter_of(cot_all, d, row_begin), **to_core))
+
+    def cot_arrival(d):
+        cot_z[d].wait_recv()
+        block = quarter_of(cot_all, d, row_begin)
+        if d == 2:
+            cot_z[3] = links.to(block, block, seq=owners[1])
+        cot_x[d] = links.to(block, block, **to_x)
+        cot_core.append(links.to(block, block, **to_core))
 
     def cot_on(d):
         cot_x[d].wait_recv()
         block = quarter_of(cot_all, d, x_begin)
         cot_core.append(links.to(block, block, **to_core))
 
-    attn_arrival(2)
-    attn_arrival(1)
     ff_own = at_rows(ff_w, me, block_rows)
+    ff_copy = pltpu.make_async_copy(ff_packs.at[z], ff_own, local_sem.at[1])
+    ff_copy.start()
     ff_z, ff_y = {}, []
 
     def ff_start(d):
@@ -460,12 +524,15 @@
 
     ff_start(2)
     attn_arrival(3)
+    mix_y.append(links.to(mix_own, mix_own, **to_y))
+    mix_arrival(3)
+    cot_arrival(2)
+    cot_arrival(1)
     ff_y.append(links.to(ff_packs.at[z], ff_own, **to_y))
     for copy in attn_y:
         copy.wait_recv()
 
     base = 2 * width + H * HD
-    kv_head = lax.div(head * heads, H // KV)
     bias_q = vector_of(scal_ref, 2 * width + head * wide_heads, wide_heads)
     bias_k = vector_of(scal_ref, base + kv_head * HD, HD)
     bias_v = vector_of(scal_ref, base + (KV + kv_head) * HD, HD)
@@ -475,7 +542,7 @@
         part = rows_of(i * half, half)
         normed = normed_ref[part, :]
         cosine, sine_term = cos_ref[part, :], sin_ref[part, :]
-        pre = dot_nn(normed, attn_w[:, 2 * wide_heads : 2 * wide_heads + 2 * HD])
+        pre = dot_nn(normed, attn_w[:, wide_heads:])
         own = rows_of(z * rows + i * half, half)
         k_all[own, :] = low(turn(pre[:, :HD] + bias_k, cosine, sine_term))
         v_all[own, :] = low(pre[:, HD:] + bias_v)
@@ -506,24 +573,21 @@
     kv_core = []
     ff_start(1)
     ff_start(3)
-    cot_z.wait_recv()
-    block = quarter_of(cot_all, 3, row_begin)
-    cot_x[3] = links.to(block, block, **to_x)
-    cot_core.append(links.to(block, block, **to_core))
-    cot_on(1)
-    cot_on(2)
     for d in (1, 2, 3):
         kv_z[d].wait_recv()
         kv_core.append(keys_or_values(owners[d], to_core))
-    ff_arrival(2)
     for copy in kv_core:
         copy.wait_recv()
     attention_forward(starts_ref, q_ref, k_all, v_all, att_ref, lse_ref)
-
-    mixing = attn_w.at[:, wide_heads : 2 * wide_heads]
+    ff_arrival(2)
+    cot_on(2)
+    cot_on(1)
+
+    for copy in mix_y:
+        copy.wait_recv()
 
     def branch_part(begin, size_rows):
-        return dot_nt(low(att_ref[rows_of(begin, size_rows), :]), mixing[...])
+        return dot_nt(low(att_ref[rows_of(begin, size_rows), :]), mix_w[...])
 
     def branch_send(i, unused):
         part = rows_of(i * quarter, quarter)
@@ -543,6 +607,7 @@
     other, mine = rows_of((1 - xx) * quarter, quarter), rows_of(xx * quarter, quarter)
     send_x[...] = low(kept[other, :] + wide(recv_c[other, :]))
     to_xx = links.to(send_x, recv_x, **to_x)
+    cot_arrival(3)
     to_xx.wait_recv()
     gain_two = vector_of(scal_ref, width, width)
     hidden = wide(x_ref[rows_of(row_begin, quarter), :]) + (
@@ -572,31 +637,36 @@
         nt_core.append(links.to(block, block, **to_core))
 
     ff_arrival(1)
+    nt_arrival(2)
+    nt_arrival(1)
     nt_on(0)
     cot_on(3)
+    nt_arrival(3)
     ff_arrival(3)
-    nt_arrival(2)
-    nt_arrival(1)
-    nt_arrival(3)
     for d in (2, 1, 3):
         nt_on(d)
     for copy in cot_core + ff_y + nt_core:
         copy.wait_recv()
     links.finish()
     own_copy.wait()
-
-
-def front(starts, scal_in, pack, ff_packs, x_rows, cot_one, cot_two, cosine, sine_term, wide_heads):
+    ff_copy.wait()
+
+
+def front(
+    starts, scal_in, query, keyvalue, mixing_t, expand, shrink_t, x_rows, cot_rows, cosine, sine_term, columns
+):
     rows, width = x_rows.shape
     size = lax.axis_size("seq")
     quarter, half, count = rows // 4, rows // 2, 2 * size
+    block_rows, wide_heads = query.shape
     bf16, f32 = jnp.bfloat16, jnp.float32
     shape = jax.ShapeDtypeStruct
     in_vmem_spec, anywhere = pl.BlockSpec(memory_space=pltpu.VMEM), pl.BlockSpec(memory_space=pl.ANY)
     outs = [
         (shape((count,) + scal_in.shape, f32), in_vmem_spec),
-        (shape((count * pack.shape[0], pack.shape[1]), bf16), in_vmem_spec),
-        (shape((count * pack.shape[0], ff_packs.shape[2]), bf16), anywhere),
+        (shape((count * block_rows, wide_heads + 2 * HD), bf16), in_vmem_spec),
+        (shape((count * block_rows, wide_heads), bf16), in_vmem_spec),
+        (shape((count * block_rows, columns), bf16), anywhere),
         (shape((size * rows, width), bf16), anywhere),
         (shape((rows, width), bf16), in_vmem_spec),
         (shape((rows, wide_heads), bf16), in_vmem_spec),
@@ -610,29 +680,32 @@
     return pl.pallas_call(
         front_kernel,
         out_shape=[o[0] for o in outs],
-        in_specs=[
-            pl.BlockSpec(memory_space=pltpu.SMEM), in_vmem_spec, in_vmem_spec, anywhere,
-            in_vmem_spec, anywhere, anywhere, in_vmem_spec, in_vmem_spec,
-        ],
+        in_specs=[pl.BlockSpec(memory_space=pltpu.SMEM)]
+        + [in_vmem_spec] * 4
+        + [anywhere] * 2
+        + [in_vmem_spec, anywhere, in_vmem_spec, in_vmem_spec],
         out_specs=[o[1] for o in outs],
         scratch_shapes=[
+            pltpu.VMEM(expand.shape, f32),
+            pltpu.VMEM(shrink_t.shape, f32),
+            pltpu.VMEM((size, block_rows, columns), bf16),
             pltpu.VMEM((quarter, width), bf16),
             pltpu.VMEM((half, width), bf16),
             pltpu.VMEM((half, width), bf16),
             pltpu.VMEM((quarter, width), bf16),
             pltpu.VMEM((quarter, width), bf16),
             pltpu.VMEM((half, width), f32),
-            pltpu.SemaphoreType.DMA((56,)),
-            pltpu.SemaphoreType.DMA((56,)),
-            pltpu.SemaphoreType.DMA((1,)),
+            pltpu.SemaphoreType.DMA((64,)),
+            pltpu.SemaphoreType.DMA((64,)),
+            pltpu.SemaphoreType.DMA((3,)),
         ],
         compiler_params=pltpu.CompilerParams(
-            collective_id=1, has_side_effects=True, vmem_limit_bytes=48 * 1024 * 1024
+            collective_id=1, has_side_effects=True, vmem_limit_bytes=62 * 1024 * 1024
         ),
         cost_estimate=pl.CostEstimate(
             flops=6 * 10**9, bytes_accessed=30 * 10**6, transcendentals=10**7
         ),
-    )(starts, scal_in, pack, ff_packs, x_rows, cot_one, cot_two, cosine, sine_term)
+    )(starts, scal_in, query, keyvalue, mixing_t, expand, shrink_t, x_rows, cot_rows, cosine, sine_term)
 
 
 def gated(gate_value, up_value, act_grad):
@@ -643,7 +716,7 @@
 
 
 def ff_kernel(
-    nt_ref, ff_w, ff_packs, cot_all, cot_ref, cot_one, cot_two, hid_ref, scal_ref,
+    nt_ref, ff_w, cot_all, cot_ref, hid_ref, scal_ref,
     hg_ref, bg_ref, gain_ref, gw_ref, out_ref, early_ref,
     nt_all, cot_v, w_v, both_v, act_v, send_c, recv_c, kept, send_x, recv_x, send_z, recv_z, total, grad_v, out_v,
     send_sems, recv_sems, local_sems,
@@ -658,8 +731,8 @@
     main = wide_units // 256 * 128
     owners = [z, z + 1 - 2 * lax.rem(z, 2), lax.rem(z + 2, 4), 3 - z]
     to_x, to_core = {"head": head + 2 - 4 * xx}, {"head": head + 1 - 2 * core}
-    size, block_rows = 4, ff_packs.shape[1]
-    me = y * size + z
+    size = 4
+    block_rows = ff_w.shape[0] // (2 * size)
     loads = []
 
     def load(source, target):
@@ -667,18 +740,10 @@
         copy.start()
         loads.append(copy)
 
-    load(ff_packs.at[z], at_rows(w_v, me, block_rows))
-    for k in range(1, 2 * size):
-        owner = lax.rem(me + k, 2 * size)
-        load(at_rows(ff_w, owner, block_rows), at_rows(w_v, owner, block_rows))
+    load(ff_w, w_v)
     load(cot_ref, at_rows(cot_v, z, rows))
     for d in (1, 2, 3):
-        part = rows_of(owners[d] * rows + row_begin, quarter)
-        load((cot_one, cot_two, cot_all.at[part, :])[d - 1], cot_v.at[part, :])
-        part = rows_of(owners[d] * rows + x_begin, quarter)
-        load(cot_all.at[part, :], cot_v.at[part, :])
-        part = rows_of(owners[d] * rows + (1 - core) * half, half)
-        load(cot_all.at[part, :], cot_v.at[part, :])
+        load(at_rows(cot_all, owners[d], rows), at_rows(cot_v, owners[d], rows))
     first_loads = list(loads)
     load(nt_ref, nt_all)
     to_y = {"dp": 1 - y}
@@ -810,7 +875,7 @@
             copy.wait_send()
 
 
-def feed_forward(nt, ff_w, ff_packs, cot_all, cot, cot_one, cot_two, hidden, scal, units):
+def feed_forward(nt, ff_w, cot_all, cot, hidden, scal, units):
     quarter, width = hidden.shape
     rows, stream, columns = 4 * quarter, cot_all.shape[0], ff_w.shape[1]
     bf16, f32 = jnp.bfloat16, jnp.float32
@@ -822,12 +887,12 @@
         (shape((1, width), f32), in_vmem_spec),
         (shape((width, columns), bf16), anywhere),
         (shape((stream, width), bf16), anywhere),
-        (shape(ff_packs.shape[1:], bf16), anywhere),
+        (shape((width // 8, columns), bf16), anywhere),
     ]
     return pl.pallas_call(
         ff_kernel,
         out_shape=[o[0] for o in outs],
-        in_specs=[anywhere] * 7 + [in_vmem_spec] * 2,
+        in_specs=[anywhere] * 4 + [in_vmem_spec] * 2,
         out_specs=[o[1] for o in outs],
         scratch_shapes=[
             pltpu.VMEM((stream, width), bf16),
@@ -855,16 +920,16 @@
         cost_estimate=pl.CostEstimate(
             flops=33 * 10**9, bytes_accessed=40 * 10**6, transcendentals=10**6
         ),
-    )(nt, ff_w, ff_packs, cot_all, cot, cot_one, cot_two, hidden, scal)
+    )(nt, ff_w, cot_all, cot, hidden, scal)
 
 
 def back_kernel(
-    starts_ref, scal_ref, x_own, hid_ref, hg_ref, gain_two_ref, bg_ref, attn_w, normed_ref, q_ref, k_all, v_all,
+    starts_ref, scal_ref, x_ref, hid_ref, hg_ref, gain_two_ref, bg_ref, attn_w, mix_w, normed_ref, q_ref, k_all, v_all,
     att_ref, lse_ref, cos_ref, sin_ref, gw_ref, part_ref, early_ref,
     layer_ref, input_ref, ff_grads, attn_ref, kv_ref, small_ref,
     ff_y, ff_own, out_c, out_own, out_sx, out_rx, out_sz, out_rz, dk, dv, do, dq, dkv_s, dkv_r, dkv_rz, dkv_own,
     qg, one_sc, one_rc, one_keep, one_sx, one_rx, layer_own, input_own, a_other, a_own, a_y, a_z, a_sz,
-    small, small_y, small_s, small_z, small_h, kv_own,
+    x_own, small, small_y, small_s, small_z, small_h, kv_own,
     send_sems, recv_sems, local_sems,
 ):
     quarter, width = x_own.shape
@@ -904,6 +969,7 @@
 
     ff_start(2)
     ff_early = load(early_ref, ff_y.at[3])
+    x_load = load(x_ref.at[rows_of(row_begin, quarter), :], x_own)
     out_sent, out_load = [], []
     for s in range(4):
         begin = owners[s] * rows
@@ -915,9 +981,9 @@
     for d in order:
         ff_load[d] = load(grad_rows(gw_ref, y, d), ff_own.at[d])
 
-    ff_over_z = {}
-
-    def ff_step(d):
+    ff_over_z = []
+
+    def ff_add(d):
         if d == 3:
             ff_early.wait()
         else:
@@ -930,10 +996,20 @@
             return unused
 
         lax.fori_loop(0, block_rows // 64, add, 0)
+
+    def ff_half(d, i):
+        part = pl.ds(i * (block_rows // 2), block_rows // 2)
+        ff_over_z.append(
+            links.to(ff_own.at[d, part, :], ff_grads.at[z, part, :], seq=owners[d])
+        )
+
+    def ff_step(d):
+        ff_add(d)
         if d == 0:
             load(ff_own.at[d], ff_grads.at[z])
         else:
-            ff_over_z[d] = links.to(ff_own.at[d], ff_grads.at[z], seq=owners[d])
+            ff_half(d, 0)
+            ff_half(d, 1)
 
     out_x, out_z = {}, {}
 
@@ -957,10 +1033,11 @@
 
     def do_rows(i, unused):
         part = rows_of(i * half, half)
-        do[part, :] = low(dot_nn(bg_ref[part, :], attn_w[:, wide_heads : 2 * wide_heads]))
+        do[part, :] = low(dot_nn(bg_ref[part, :], mix_w[...]))
         return unused
 
-    ff_step(3)
+    ff_add(3)
+    ff_half(3, 0)
     lax.fori_loop(0, 2, do_rows, 0)
     attention_backward(starts_ref, q_ref, k_all, v_all, do, att_ref, lse_ref, dq, dk, dv, (0,))
     out_step_c(3)
@@ -982,13 +1059,13 @@
         dkv_own[d] = low(dkv_block(d))
         dkv_z.append(links.to(dkv_own.at[d], dkv_rz.at[d - 1], seq=owners[d]))
     total = dkv_block(0)
-    ff_step(2)
     for d in (1, 2, 3):
         dkv_z[d - 1].wait_recv()
         total = total + wide(dkv_rz[d - 1])
+    ff_half(3, 1)
     turned = turn(total, cos_ref[...], -sin_ref[...])
     dkv_own[0] = low(turned * (1.0 - is_core) + total * is_core)
-    key_columns = pl.ds(pl.multiple_of(2 * wide_heads + core * HD, HD), HD)
+    key_columns = pl.ds(pl.multiple_of(wide_heads + core * HD, HD), HD)
 
     def one_part(begin):
         part = rows_of(begin, quarter)
@@ -1024,6 +1101,7 @@
     attn_sent = {
         d: links.to(at_rows(a_other, owners[d], block_rows), a_y.at[d], **to_y) for d in order
     }
+    ff_step(2)
     out_step_c(1)
     out_step_c(0)
     attn_grads(y, a_own)
@@ -1031,6 +1109,7 @@
 
     one_x.wait_recv()
     norm_one_grad = one_keep[mine, :] + wide(one_rc[mine, :]) + wide(one_rx[...])
+    x_load.wait()
     x_rows = wide(x_own[...])
     gain_one = vector_of(scal_ref, 0, width)
     scale = lax.rsqrt(jnp.mean(x_rows * x_rows, axis=-1, keepdims=True) + norm_eps)
@@ -1103,17 +1182,7 @@
     layer_own[...] = low(layer)
     layer_sent = gather(layer_own, layer_ref)
     ff_step(1)
-    value = small_s[z]
-    for d in (1, 2, 3):
-        small_over_z[d - 1].wait_recv()
-        value = value + small_z[d - 1]
-    small_h[0] = value
-    small_x = links.to(small_h.at[0], small_h.at[1], **to_x)
     block = attn_step(0)
-    small_x.wait_recv()
-    small_h[2] = small_h[0] + small_h[1]
-    small_c = links.to(small_h.at[2], small_h.at[3], **to_core)
-    gather_on(layer_sent, layer_ref)
     for d in (1, 2):
         attn_over_z[d].wait_recv()
         block = block + wide(a_z[d - 1])
@@ -1123,24 +1192,34 @@
     place[...] = kv_own[...]
     kv_x = links.to(kv_own, place, **to_x)
     kv_core = [links.to(kv_own, place, **to_core)]
+    gather_on(layer_sent, layer_ref)
+    value = small_s[z]
+    for d in (1, 2, 3):
+        small_over_z[d - 1].wait_recv()
+        value = value + small_z[d - 1]
+    small_h[0] = value
+    small_x = links.to(small_h.at[0], small_h.at[1], **to_x)
+    small_x.wait_recv()
+    small_h[2] = small_h[0] + small_h[1]
+    small_c = links.to(small_h.at[2], small_h.at[3], **to_core)
     small_c.wait_recv()
     small_ref[...] = small_h[2] + small_h[3]
     kv_x.wait_recv()
     place = kv_ref.at[core * 2 + 1 - xx]
     kv_core.append(links.to(place, place, **to_core))
     ff_step(0)
-    for copy in kv_core + input_sent[1] + layer_sent[1] + [ff_over_z[d] for d in (3, 2, 1)]:
+    for copy in kv_core + input_sent[1] + layer_sent[1] + ff_over_z:
         copy.wait_recv()
     links.finish()
-    for copy in loads[9:]:
+    for copy in loads[10:]:
         copy.wait()
 
 
 def back(
-    starts, scal, x_own, hidden, hidden_grad, gain_two_grad, branch_grad, attn_w, normed, q, k_all, v_all, attended, lse,
+    starts, scal, x_rows, hidden, hidden_grad, gain_two_grad, branch_grad, attn_w, mix_w, normed, q, k_all, v_all, attended, lse,
     cosine, sine_term, gw, out_part, early,
 ):
-    quarter, width = x_own.shape
+    quarter, width = hidden.shape
     half, rows = 2 * quarter, 4 * quarter
     size = lax.axis_size("seq")
     block_rows, columns = gw.shape[0] // (2 * size), gw.shape[1]
@@ -1189,6 +1268,7 @@
         ((4, block_rows, attn_columns), bf16),
         ((3, block_rows, attn_columns), bf16),
         ((3, block_rows, attn_columns), bf16),
+        ((quarter, width), bf16),
         (scal.shape, f32),
         (small, f32),
         (small, f32),
@@ -1199,13 +1279,15 @@
     return pl.pallas_call(
         back_kernel,
         out_shape=[o[0] for o in outs],
-        in_specs=[pl.BlockSpec(memory_space=pltpu.SMEM)] + [in_vmem_spec] * 15 + [anywhere] * 3,
+        in_specs=[pl.BlockSpec(memory_space=pltpu.SMEM), in_vmem_spec, anywhere]
+        + [in_vmem_spec] * 14
+        + [anywhere] * 3,
         out_specs=[o[1] for o in outs],
         scratch_shapes=[pltpu.VMEM(*one) for one in scratch]
         + [
             pltpu.SemaphoreType.DMA((56,)),
             pltpu.SemaphoreType.DMA((56,)),
-            pltpu.SemaphoreType.DMA((12,)),
+            pltpu.SemaphoreType.DMA((14,)),
         ],
         compiler_params=pltpu.CompilerParams(
             collective_id=3, has_side_effects=True, vmem_limit_bytes=62 * 1024 * 1024
@@ -1214,9 +1296,69 @@
             flops=10 * 10**9, bytes_accessed=40 * 10**6, transcendentals=10**6
         ),
     )(
-        starts, scal, x_own, hidden, hidden_grad, gain_two_grad, branch_grad, attn_w, normed, q, k_all, v_all, attended,
+        starts, scal, x_rows, hidden, hidden_grad, gain_two_grad, branch_grad, attn_w, mix_w, normed, q, k_all, v_all, attended,
         lse, cosine, sine_term, gw, out_part, early,
     )
+
+
+def optimizer_kernel(*refs):
+    ff_grads, attn_grads, kv_blocks = refs[:3]
+    held, outs = refs[3:18], refs[18:]
+    size, wide_heads = ff_grads.shape[0], held[0].shape[1]
+    main = 512
+
+    def joined(begin, rest_begin, width):
+        pieces = [ff_grads[j, :, begin : begin + main] for j in range(size)]
+        pieces += [
+            ff_grads[j, :, rest_begin : rest_begin + 64] for j in range((width - size * main) // 64)
+        ]
+        return wide(jnp.concatenate(pieces, axis=1))
+
+    def update(number, grad, at=slice(None)):
+        master, moment, square = (ref[at] for ref in held[3 * number : 3 * number + 3])
+        results = adamw(master, moment, square, grad, learn_rates[number], decay_rates[number])
+        for ref, value in zip(outs[5 * number : 5 * number + 4], results):
+            ref[at] = value
+        if at == slice(None):
+            outs[5 * number + 4][...] = results[4]
+
+    update(0, wide(low(attn_grads[:, :wide_heads])))
+    update(1, wide(jnp.concatenate([kv_blocks[i] for i in range(4)], axis=1)))
+    update(2, wide(low(attn_grads[:, wide_heads : 2 * wide_heads])))
+    every = slice(None)
+    hidden_units = held[9].shape[2]
+    update(3, joined(0, 2 * main, hidden_units), (every, 0, every))
+    update(3, joined(main, 2 * main + 64, hidden_units), (every, 1, every))
+    outs[19][...] = low(outs[18][...])
+    update(4, joined(2 * main + 128, 3 * main + 128, hidden_units))
+
+
+def optimizer(ff_grads, attn_grads, kv_blocks, held):
+    rows, step = attn_grads.shape[0], 16
+
+    def block(array):
+        if array.ndim == 3 and array.shape[0] == 4:
+            return pl.BlockSpec((4, step) + array.shape[2:], lambda i: (0, i, 0))
+        rest = array.shape[1:]
+        return pl.BlockSpec((step,) + rest, lambda i: (i,) + (0,) * len(rest))
+
+    outs, flat = [], []
+    for three in held:
+        flat.extend(three)
+        outs += [jax.ShapeDtypeStruct(three[0].shape, jnp.float32)] * 4
+        outs.append(jax.ShapeDtypeStruct(three[0].shape, jnp.bfloat16))
+    operands = [ff_grads, attn_grads, kv_blocks] + flat
+    return pl.pallas_call(
+        optimizer_kernel,
+        grid=(rows // step,),
+        out_shape=outs,
+        in_specs=[block(one) for one in operands],
+        out_specs=[block(one) for one in outs],
+        compiler_params=pltpu.CompilerParams(vmem_limit_bytes=62 * 1024 * 1024),
+        cost_estimate=pl.CostEstimate(
+            flops=3 * 10**7, bytes_accessed=50 * 10**6, transcendentals=2 * 10**6
+        ),
+    )(*operands)
 
 
 def rope_tables(places):
@@ -1495,53 +1637,12 @@
     scalars_moment,
     scalars_square,
 ):
-    local_rows, width = tokens.shape[1], tokens.shape[2]
+    local_rows = tokens.shape[1]
     seq_count = lax.axis_size("seq")
-    head_count = lax.axis_size("head")
-    head_index = lax.axis_index("head")
     seq_index = lax.axis_index("seq")
-    local_heads = H // head_count
-    wide_heads = local_heads * HD
-    kv_head = head_index * local_heads // (H // KV)
-    core = head_index % 2
-    quarter = local_rows // 4
-    row_begin = (head_index % 2) * (2 * quarter) + (head_index // 2) * quarter
     hidden_units = expand_master.shape[2]
+
     units = 64 * -(-hidden_units // (64 * seq_count))
-
-    cot_own = lax.dynamic_slice_in_dim(cotangent[0], row_begin, quarter, 0)
-    cot_two = lax.ppermute(cot_own, "seq", [(i, i ^ 2) for i in range(seq_count)])
-    cot_one = lax.ppermute(cot_own, "seq", [(i, i ^ 1) for i in range(seq_count)])
-
-    attn_pack = jnp.concatenate(
-        [
-            low(queries_master),
-            low(mixing_master).T,
-            low(lax.dynamic_slice_in_dim(keyvalue_master, kv_head * HD, HD, 1)),
-            low(lax.dynamic_slice_in_dim(keyvalue_master, (KV + kv_head) * HD, HD, 1)),
-        ],
-        axis=1,
-    )
-    main = units // 128 * 128
-    rest = units - main
-    gate_low, up_low = low(expand_master[:, 0]), low(expand_master[:, 1])
-    shrink_low = low(shrink_master).T
-
-    def own_units(values, j):
-        begin = main * seq_count + rest * j
-        last = values[:, begin : begin + rest]
-        last = jnp.pad(last, ((0, 0), (0, rest - last.shape[1])))
-        return values[:, main * j : main * (j + 1)], last
-
-    ff_packs = []
-    for j in range(seq_count):
-        gate_main, gate_rest = own_units(gate_low, j)
-        up_main, up_rest = own_units(up_low, j)
-        shrink_main, shrink_rest = own_units(shrink_low, j)
-        pieces = [gate_main, up_main, gate_rest, up_rest, shrink_main, shrink_rest]
-        pieces.append(jnp.zeros_like(shrink_rest))
-        ff_packs.append(jnp.concatenate(pieces, axis=1))
-    ff_packs = jnp.stack(ff_packs)
     x_low, cot_rows = tokens[0], cotangent[0]
     lengths = doc_lengths[0]
     places = folded_places(
@@ -1553,50 +1654,35 @@
     cosine, sine_term = rope_tables(within)
     scal_in = jnp.broadcast_to(wide(low(scalars_master))[None], (8, scalars_master.shape[0]))
     (
-        scal_all, attn_weight, ff_weight, cot_all, normed, queries, all_keys, all_values,
+        scal_all, attn_weight, mix_weight, ff_weight, cot_all, normed, queries, all_keys, all_values,
         attended, log_total, hidden, normed_all,
     ) = front(
-        half_starts, scal_in, attn_pack, ff_packs, x_low, cot_one, cot_two, cosine, sine_term, wide_heads
+        half_starts, scal_in, queries_master, keyvalue_master, mixing_master.T, expand_master, shrink_master.T,
+        x_low, cot_rows, cosine, sine_term, 3 * units + 64,
     )
     hidden_grad, branch_grad, gain_two_grad, ff_part, out_part, early = feed_forward(
-        normed_all, ff_weight, ff_packs, cot_all, cot_rows, cot_one, cot_two, hidden, scal_all, units
-    )
-    x_own = lax.dynamic_slice_in_dim(x_low, row_begin, quarter, 0)
+        normed_all, ff_weight, cot_all, cot_rows, hidden, scal_all, units
+    )
     layer_out, input_grad, ff_grads, attn_grads, kv_blocks, small = back(
-        half_starts, scal_all, x_own, hidden, hidden_grad, gain_two_grad, branch_grad, attn_weight, normed, queries,
+        half_starts, scal_all, x_low, hidden, hidden_grad, gain_two_grad, branch_grad, attn_weight, mix_weight, normed, queries,
         all_keys, all_values, attended, log_total, cosine, sine_term, ff_part, out_part, early,
     )
-    shared_keyvalue = wide(jnp.concatenate([kv_blocks[i] for i in range(4)], axis=1))
-    shared_scalars = small[0]
-
-    def joined(begin, rest_begin):
-        pieces = [ff_grads[j, :, begin : begin + main] for j in range(seq_count)]
-        for j in range(seq_count):
-            size = min(rest, hidden_units - main * seq_count - rest * j)
-            pieces.append(ff_grads[j, :, rest_begin : rest_begin + size])
-        return jnp.concatenate(pieces, axis=1)
-
-    expand_grad = jnp.stack([joined(0, 2 * main), joined(main, 2 * main + rest)], axis=1)
-    expand_grad = with_layout_constraint(expand_grad, Layout(major_to_minor=(0, 1, 2)))
-    grads = (
-        attn_grads[:, :wide_heads],
-        shared_keyvalue,
-        attn_grads[:, wide_heads : 2 * wide_heads].T,
-        expand_grad,
-        joined(2 * units, 2 * units + main).T,
-        shared_scalars,
-    )
-    masters = (
+    held = (
         (queries_master, queries_moment, queries_square),
         (keyvalue_master, keyvalue_moment, keyvalue_square),
-        (mixing_master, mixing_moment, mixing_square),
+        tuple(one.T for one in (mixing_master, mixing_moment, mixing_square)),
         (expand_master, expand_moment, expand_square),
-        (shrink_master, shrink_moment, shrink_square),
-        (scalars_master, scalars_moment, scalars_square),
-    )
+        tuple(one.T for one in (shrink_master, shrink_moment, shrink_square)),
+    )
+    updated = optimizer(ff_grads, attn_grads, kv_blocks, held)
     results = [layer_out[None], input_grad[None]]
-    for held, grad, rate, decay in zip(masters, grads, learn_rates, decay_rates):
-        results.extend(adamw(*held, wide(low(grad)), rate, decay))
+    for i in range(5):
+        results.extend(one.T if i in (2, 4) else one for one in updated[5 * i : 5 * i + 5])
+    results.extend(
+        adamw(
+            scalars_master, scalars_moment, scalars_square, wide(low(small[0])), learn_rates[5], decay_rates[5]
+        )
+    )
     return tuple(results)
 
 

time: 477 us -> 433 us (0.908)
  the two profiles are of different devices: /device:TPU:0 before, /device:TPU:29 now
where the time goes in v4:
time: 433 us; the launch traced here: 427 us
  Pallas kernels  411 us (95%)
  other arithmetic  7.92 us (2%)
  local copies, waits for them, and re-layouts  5.57 us (1%)
    pallas_call x1, Pallas kernels, front(): pl.pallas_call(front_kernel, out_shape=[o[0] for o in outs], in_specs=[pl...  163 us
    pallas_call x1, Pallas kernels, back(): pl.pallas_call(back_kernel, out_shape=[o[0] for o in outs], in_specs=[pl....  147 us
    pallas_call x1, Pallas kernels, feed_forward(): pl.pallas_call(ff_kernel, out_shape=[o[0] for o in outs], in_specs=[anywh...  76.1 us
    pallas_call x1, Pallas kernels, optimizer(): pl.pallas_call(optimizer_kernel, grid=(rows // step,), out_shape=outs, in...  24.7 us

profile of v4, /device:TPU:29, one launch (start us, length us, event | category | flops | bytes accessed | tf_op | source)
XLA Modules:
  0.0 427.0 jit_solution(16569408479800436245)
XLA Ops:
  0.7 1.3 fusion.12
  3.3 1.3 subtract_convert_fusion
  4.6 0.5 fusion.11
  5.1 1.9 pad_add_fusion.starts_ref
  7.0 0.7 convert_convert_fusion
  7.7 0.6 broadcast_in_dim.23.scal_in
  8.3 1.0 fusion
  9.3 0.8 pad_maximum_fusion.1.sin_ref
  10.2 0.8 pad_maximum_fusion.cos_ref
  11.0 162.9 %shard_map.452 = (f32[8,8,640]{2,1,0:T(8,128)}, bf16[1536,640]{1,0:T(8,128)(2,1)}, bf16[1536,384]{1,0:T(8,128)(2,1)}, bf16[1536,1792]{1,0:T(8,128)(2,1)}, bf16[2...) custom-call(s32[2]{0:T(128)} %pad_add_fusion.starts_ref, ...), custom_call_target="tpu_custom_call" | custom-call | flops 6000000000 | bytes 30000000 | tf_op jit(solution)/shard_map/pallas_call | solution.py:680
  173.9 76.1 %shard_map.453 = (f32[128,1536]{1,0:T(8,128)}, bf16[512,1536]{1,0:T(8,128)(2,1)}, f32[1,1536]{1,0:T(1,128)}, bf16[1536,1792]{1,0:T(8,128)(2,1)}, bf16[2048,1536]{1,0:T(8,128)(2,1)}, /*index=5*/bf16[192,1792]{1,0:T(8,128)(2,1)}) custom-call(bf16[2048,1536]{1,0:T(8,128)(2,1)} %get-tuple-element.84.nt_ref, bf16[1536,1792]{1,0:T(8,128)(2,1)} %get-tuple-element.85.ff_w, ...), custom_call_target="tpu_custom_call" | custom-call | flops 32999999488 | bytes 40000000 | tf_op jit(solution)/shard_map/pallas_call | solution.py:892
  250.0 0.0 copy-start.2
  250.0 0.0 copy-start.4
  250.0 0.0 copy-start.5
  250.1 147.3 %shard_map.454 = (bf16[512,1536]{1,0:T(8,128)(2,1)}, bf16[512,1536]{1,0:T(8,128)(2,1)}, bf16[4,192,1792]{2,1,0:T(8,128)(2,1)}, f32[192,896]{1,0:T(8,128)}, bf16[...) custom-call(s32[2]{0:T(128)} %pad_add_fusion.starts_ref, f32[8,8,640]{2,1,0:T(8,128)} %get-tuple-element.82.scal_ref, ...), custom_call_target="tpu_custom_call" | custom-call | flops 10000000000 | bytes 40000000 | tf_op jit(solution)/shard_map/pallas_call | solution.py:1279
  397.4 0.7 fusion.3
  398.1 0.0 copy-done.2
  398.1 0.0 copy-done.4
  398.1 0.0 copy-done.5
  398.1 0.0 copy-start.3
  398.2 0.6 fusion.9
  398.8 0.0 copy-start.1
  398.8 24.7 %shard_map.455 = (f32[192,384]{1,0:T(8,128)}, f32[192,384]{1,0:T(8,128)}, f32[192,384]{1,0:T(8,128)}, f32[192,384]{1,0:T(8,128)}, bf16[192,384]{1,0:T(8,128)(2,1...) custom-call(bf16[4,192,1792]{2,1,0:T(8,128)(2,1)} %get-tuple-element, ...), custom_call_target="tpu_custom_call" | custom-call | flops 30000000 | bytes 50000000 | tf_op jit(solution)/shard_map/pallas_call | solution.py:1351
  423.5 0.0 copy-done.3
  423.5 0.0 copy-start
  423.5 0.0 copy-done.1
  423.5 1.1 copy.55
  424.7 0.8 copy-done
  425.5 1.1 copy.56
  (1 shorter events, 0.0 us)
Async XLA Ops:
  250.0 148.1 %copy-start.2 = (f32[640]{0:T(1024)S(1)}, f32[640]{0:T(1024)}, u32[]{:S(2)}) copy-start(f32[640]{0:T(1024)} %param.39) | copy-start | bytes 7684
  250.0 148.1 %copy-start.4 = (f32[640]{0:T(1024)S(1)}, f32[640]{0:T(1024)}, u32[]{:S(2)}) copy-start(f32[640]{0:T(1024)} %param.41) | copy-start | bytes 7684
  250.0 148.1 %copy-start.5 = (f32[640]{0:T(1024)S(1)}, f32[640]{0:T(1024)}, u32[]{:S(2)}) copy-start(f32[640]{0:T(1024)} %param.40) | copy-start | bytes 7684
  398.1 25.3 %copy-start.3 = (f32[640]{0:T(1024)}, f32[640]{0:T(1024)S(1)}, u32[]{:S(2)}) copy-start(f32[640]{0:T(1024)S(1)} %fusion.3) | copy-start | bytes 7684
  398.8 24.7 %copy-start.1 = (bf16[512,1536]{1,0:T(8,128)(2,1)S(1)}, bf16[512,1536]{1,0:T(8,128)(2,1)}, u32[]{:S(2)}) copy-start(bf16[512,1536]{1,0:T(8,128)(2,1)} %get-tuple-element.101) | copy-start | bytes 4718596
  423.5 2.0 copy-start

commit v5 on v4

--- a/solution.py
+++ b/solution.py
@@ -201,8 +201,13 @@
     return total if scatter else out
 
 
-def hidden_before(starts_ref, half, block, block_rows):
-    return jnp.where(block * block_rows >= starts_ref[half], 0.0, masked_low)
+def hidden_before(lengths_ref, half, block, block_rows):
+    first_place = last_block(half) * block_rows
+    end, start = jnp.int32(0), jnp.int32(0)
+    for i in range(lengths_ref.shape[1]):
+        end = end + lengths_ref[0, i]
+        start = start + jnp.where(end <= first_place, lengths_ref[0, i], 0)
+    return jnp.where(block * block_rows >= start, 0.0, masked_low)
 
 
 def last_block(half):
@@ -227,7 +232,7 @@
     return jnp.concatenate([ref[rows, i * HD : (i + 1) * HD] for i in range(heads)], axis=0)
 
 
-def attention_forward(starts_ref, q_ref, k_ref, v_ref, o_ref, lse_ref, halves=(0, 1)):
+def attention_forward(lengths_ref, q_ref, k_ref, v_ref, o_ref, lse_ref, halves=(0, 1)):
     local_rows, heads = q_ref.shape[0], q_ref.shape[1] // HD
     block_rows = local_rows // 2
     size = lax.axis_size("seq")
@@ -245,7 +250,7 @@
             if diagonal:
                 scores = scores + seen_bias(block_rows, heads)
             else:
-                scores = scores + hidden_before(starts_ref, half, block, block_rows)
+                scores = scores + hidden_before(lengths_ref, half, block, block_rows)
             new_max = jnp.maximum(running_max, jnp.max(scores, axis=-1, keepdims=True))
             probs = jnp.exp(scores - new_max)
             fade = jnp.exp(running_max - new_max)
@@ -269,7 +274,7 @@
 
 
 def attention_backward(
-    starts_ref, q_ref, k_ref, v_ref, do_ref, o_ref, lse_ref, dq_ref, dk_ref, dv_ref, halves=(0, 1)
+    lengths_ref, q_ref, k_ref, v_ref, do_ref, o_ref, lse_ref, dq_ref, dk_ref, dv_ref, halves=(0, 1)
 ):
     local_rows, heads = q_ref.shape[0], q_ref.shape[1] // HD
     block_rows = local_rows // 2
@@ -293,7 +298,7 @@
             if diagonal:
                 scores = scores + seen_bias(block_rows, heads)
             else:
-                scores = scores + hidden_before(starts_ref, half, block, block_rows)
+                scores = scores + hidden_before(lengths_ref, half, block, block_rows)
             probs = jnp.exp(scores - lse)
             score_grad = low(probs * (dot_nt(do, v) - delta))
             dk_ref[keys, :] += dot_tn(score_grad, q) * scale
@@ -410,9 +415,9 @@
 
 
 def front_kernel(
-    starts_ref, scal_in, query_ref, kv_ref, mixing_ref, expand_ref, shrink_ref, x_ref, cot_ref, cos_ref, sin_ref,
-    scal_ref, attn_w, mix_w, ff_w, cot_all, normed_ref, q_ref, k_all, v_all, att_ref, lse_ref, hid_ref, nt_all,
-    expand_v, shrink_v, ff_packs, nt_ref, send_c, recv_c, send_x, recv_x, kept, send_sems, recv_sems, local_sem,
+    lengths_ref, scal_own, query_ref, kv_ref, mixing_ref, expand_ref, shrink_ref, x_ref, cot_ref, cos_half, sin_half,
+    scal_ref, attn_out, mix_out, ff_w, cot_all, normed_out, q_out, k_out, v_out, att_out, lse_out, hid_out, nt_all,
+    cos_out, sin_out, scal_in, cos_ref, sin_ref, attn_w, mix_w, normed_ref, q_ref, k_all, v_all, att_ref, lse_ref, hid_ref, expand_v, shrink_v, ff_packs, nt_ref, send_c, recv_c, send_x, recv_x, kept, send_sems, recv_sems, local_sem, store_sems,
 ):
     rows, width = x_ref.shape
     quarter, half = rows // 4, rows // 2
@@ -428,7 +433,15 @@
     to_y, to_x, to_core = {"dp": 1 - y}, {"head": head + 2 - 4 * xx}, {"head": head + 1 - 2 * core}
     greet([{"seq": owners[d]} for d in (1, 2, 3)] + [to_y, to_x, to_core])
     links = Links(send_sems, recv_sems)
-
+    stores = []
+
+    def store(source, target):
+        copy = pltpu.make_async_copy(source, target, store_sems.at[len(stores)])
+        copy.start()
+        stores.append(copy)
+
+
+    scal_in[...] = jnp.broadcast_to(wide(low(scal_own[...])), scal_in.shape)
     scal_ref[me] = scal_in[...]
     load_expand = pltpu.make_async_copy(expand_ref, expand_v, local_sem.at[1])
     load_expand.start()
@@ -465,6 +478,10 @@
         return unused
 
     lax.fori_loop(0, 4, norm_rows, 0)
+    cos_ref[...] = jnp.concatenate([cos_half[...], cos_half[...]], axis=1)
+    sin_ref[...] = jnp.concatenate([-sin_half[...], sin_half[...]], axis=1)
+    store(cos_ref, cos_out)
+    store(sin_ref, sin_out)
 
     def attn_arrival(d):
         attn_z[d].wait_recv()
@@ -514,15 +531,21 @@
     ff_copy.start()
     ff_z, ff_y = {}, []
 
-    def ff_start(d):
-        ff_z[d] = links.to(ff_packs.at[owners[d]], ff_own, seq=owners[d])
-
-    def ff_arrival(d):
-        ff_z[d].wait_recv()
-        block = at_rows(ff_w, y * size + owners[d], block_rows)
+    half_block = block_rows // 2
+
+    def ff_start(d, part):
+        rows_there = rows_of(me * block_rows + part * half_block, half_block)
+        source = ff_packs.at[owners[d], pl.ds(part * half_block, half_block), :]
+        ff_z[d, part] = links.to(source, ff_w.at[rows_there, :], seq=owners[d])
+
+    def ff_arrival(d, part):
+        ff_z[d, part].wait_recv()
+        begin = (y * size + owners[d]) * block_rows + part * half_block
+        block = ff_w.at[rows_of(begin, half_block), :]
         ff_y.append(links.to(block, block, **to_y))
 
-    ff_start(2)
+    ff_start(2, 0)
+    ff_start(2, 1)
     attn_arrival(3)
     mix_y.append(links.to(mix_own, mix_own, **to_y))
     mix_arrival(3)
@@ -571,20 +594,31 @@
 
     kv_z = {d: keys_or_values(z, {"seq": owners[d]}) for d in (3, 2, 1)}
     kv_core = []
-    ff_start(1)
-    ff_start(3)
+    ff_start(1, 0)
+    ff_start(1, 1)
+    ff_start(3, 0)
+    ff_start(3, 1)
     for d in (1, 2, 3):
         kv_z[d].wait_recv()
         kv_core.append(keys_or_values(owners[d], to_core))
     for copy in kv_core:
         copy.wait_recv()
-    attention_forward(starts_ref, q_ref, k_all, v_all, att_ref, lse_ref)
-    ff_arrival(2)
+    store(attn_w, attn_out)
+    store(normed_ref, normed_out)
+    store(q_ref, q_out)
+    store(k_all, k_out)
+    store(v_all, v_out)
+    attention_forward(lengths_ref, q_ref, k_all, v_all, att_ref, lse_ref)
+    store(att_ref, att_out)
+    store(lse_ref, lse_out)
+    ff_arrival(2, 0)
+    ff_arrival(2, 1)
     cot_on(2)
     cot_on(1)
 
     for copy in mix_y:
         copy.wait_recv()
+    store(mix_w, mix_out)
 
     def branch_part(begin, size_rows):
         return dot_nt(low(att_ref[rows_of(begin, size_rows), :]), mix_w[...])
@@ -614,6 +648,7 @@
         kept[mine, :] + wide(recv_c[mine, :]) + wide(recv_x[...])
     )
     hid_ref[...] = hidden
+    store(hid_ref, hid_out)
     scale = lax.rsqrt(jnp.mean(hidden * hidden, axis=-1, keepdims=True) + norm_eps)
     nt_ref[...] = low(hidden * scale * gain_two)
     own = quarter_of(nt_all, 0, row_begin)
@@ -636,13 +671,15 @@
         block = quarter_of(nt_all, d, x_begin)
         nt_core.append(links.to(block, block, **to_core))
 
-    ff_arrival(1)
+    ff_arrival(1, 0)
+    ff_arrival(1, 1)
     nt_arrival(2)
     nt_arrival(1)
     nt_on(0)
     cot_on(3)
     nt_arrival(3)
-    ff_arrival(3)
+    ff_arrival(3, 0)
+    ff_arrival(3, 1)
     for d in (2, 1, 3):
         nt_on(d)
     for copy in cot_core + ff_y + nt_core:
@@ -650,10 +687,12 @@
     links.finish()
     own_copy.wait()
     ff_copy.wait()
+    for copy in stores:
+        copy.wait()
 
 
 def front(
-    starts, scal_in, query, keyvalue, mixing_t, expand, shrink_t, x_rows, cot_rows, cosine, sine_term, columns
+    lengths, scal_own, query, keyvalue, mixing_t, expand, shrink_t, x_rows, cot_rows, cosine, sine_term, columns
 ):
     rows, width = x_rows.shape
     size = lax.axis_size("seq")
@@ -662,21 +701,27 @@
     bf16, f32 = jnp.bfloat16, jnp.float32
     shape = jax.ShapeDtypeStruct
     in_vmem_spec, anywhere = pl.BlockSpec(memory_space=pltpu.VMEM), pl.BlockSpec(memory_space=pl.ANY)
-    outs = [
-        (shape((count,) + scal_in.shape, f32), in_vmem_spec),
-        (shape((count * block_rows, wide_heads + 2 * HD), bf16), in_vmem_spec),
-        (shape((count * block_rows, wide_heads), bf16), in_vmem_spec),
+    staged = [
+        shape((count * block_rows, wide_heads + 2 * HD), bf16),
+        shape((count * block_rows, wide_heads), bf16),
+        shape((rows, width), bf16),
+        shape((rows, wide_heads), bf16),
+        shape((size * rows, HD), bf16),
+        shape((size * rows, HD), bf16),
+        shape((rows, wide_heads), f32),
+        shape((rows, wide_heads // HD), f32),
+        shape((quarter, width), f32),
+    ]
+    table = shape((rows, HD), f32)
+    outs = [(shape((count, 8, scal_own.shape[1]), f32), in_vmem_spec)]
+    outs += [(one, anywhere) for one in staged[:2]]
+    outs += [
         (shape((count * block_rows, columns), bf16), anywhere),
         (shape((size * rows, width), bf16), anywhere),
-        (shape((rows, width), bf16), in_vmem_spec),
-        (shape((rows, wide_heads), bf16), in_vmem_spec),
-        (shape((size * rows, HD), bf16), in_vmem_spec),
-        (shape((size * rows, HD), bf16), in_vmem_spec),
-        (shape((rows, wide_heads), f32), in_vmem_spec),
-        (shape((rows, wide_heads // HD), f32), in_vmem_spec),
-        (shape((quarter, width), f32), in_vmem_spec),
-        (shape((size * rows, width), bf16), anywhere),
     ]
+    outs += [(one, anywhere) for one in staged[2:]]
+    outs.append((shape((size * rows, width), bf16), anywhere))
+    outs += [(table, anywhere)] * 2
     return pl.pallas_call(
         front_kernel,
         out_shape=[o[0] for o in outs],
@@ -686,6 +731,12 @@
         + [in_vmem_spec, anywhere, in_vmem_spec, in_vmem_spec],
         out_specs=[o[1] for o in outs],
         scratch_shapes=[
+            pltpu.VMEM((8, scal_own.shape[1]), f32),
+            pltpu.VMEM(table.shape, f32),
+            pltpu.VMEM(table.shape, f32),
+        ]
+        + [pltpu.VMEM(one.shape, one.dtype) for one in staged]
+        + [
             pltpu.VMEM(expand.shape, f32),
             pltpu.VMEM(shrink_t.shape, f32),
             pltpu.VMEM((size, block_rows, columns), bf16),
@@ -695,9 +746,10 @@
             pltpu.VMEM((quarter, width), bf16),
             pltpu.VMEM((quarter, width), bf16),
             pltpu.VMEM((half, width), f32),
-            pltpu.SemaphoreType.DMA((64,)),
-            pltpu.SemaphoreType.DMA((64,)),
+            pltpu.SemaphoreType.DMA((72,)),
+            pltpu.SemaphoreType.DMA((72,)),
             pltpu.SemaphoreType.DMA((3,)),
+            pltpu.SemaphoreType.DMA((11,)),
         ],
         compiler_params=pltpu.CompilerParams(
             collective_id=1, has_side_effects=True, vmem_limit_bytes=62 * 1024 * 1024
@@ -705,7 +757,7 @@
         cost_estimate=pl.CostEstimate(
             flops=6 * 10**9, bytes_accessed=30 * 10**6, transcendentals=10**7
         ),
-    )(starts, scal_in, query, keyvalue, mixing_t, expand, shrink_t, x_rows, cot_rows, cosine, sine_term)
+    )(lengths, scal_own, query, keyvalue, mixing_t, expand, shrink_t, x_rows, cot_rows, cosine, sine_term)
 
 
 def gated(gate_value, up_value, act_grad):
@@ -741,25 +793,21 @@
         loads.append(copy)
 
     load(ff_w, w_v)
-    load(cot_ref, at_rows(cot_v, z, rows))
-    for d in (1, 2, 3):
-        load(at_rows(cot_all, owners[d], rows), at_rows(cot_v, owners[d], rows))
-    first_loads = list(loads)
-    load(nt_ref, nt_all)
+    for d in (3, 2, 1, 0):
+        if d > 0:
+            load(at_rows(cot_all, owners[d], rows), at_rows(cot_v, owners[d], rows))
+        else:
+            load(cot_ref, at_rows(cot_v, z, rows))
+        load(at_rows(nt_ref, owners[d], rows), at_rows(nt_all, owners[d], rows))
     to_y = {"dp": 1 - y}
     greet([{"seq": owners[d]} for d in (1, 2, 3)] + [to_y, to_x, to_core])
     links = Links(send_sems, recv_sems)
 
-    for copy in first_loads:
-        copy.wait()
-
-    def act_grad_rows(i, unused):
-        part = rows_of(i * half, half)
+    loads[0].wait()
+
+    def act_grad_rows(begin):
+        part = rows_of(begin, half)
         act_v[part, :] = low(dot_nn(cot_v[part, :], w_v[:, wide_units:]))
-        return unused
-
-    lax.fori_loop(0, 2 * size, act_grad_rows, 0)
-    loads[-1].wait()
 
     def gates(begin):
         part = rows_of(begin, half)
@@ -800,11 +848,15 @@
 
     for s in sequence:
         base = owners[s] * rows
+        loads[7 - 2 * s].wait()
+        loads[8 - 2 * s].wait()
+        act_grad_rows(base + (1 - core) * half)
         gates(base + (1 - core) * half)
         if s < 2:
             steps_c[s + 2].wait_send()
         send_c[s % 2] = back_part(base + (1 - core) * half)
         steps_c[s] = links.to(send_c.at[s % 2], recv_c.at[s], **to_core)
+        act_grad_rows(base + core * half)
         gates(base + core * half)
         kept[s % 2] = back_part(base + core * half)
         start_step(s)
@@ -924,13 +976,14 @@
 
 
 def back_kernel(
-    starts_ref, scal_ref, x_ref, hid_ref, hg_ref, gain_two_ref, bg_ref, attn_w, mix_w, normed_ref, q_ref, k_all, v_all,
-    att_ref, lse_ref, cos_ref, sin_ref, gw_ref, part_ref, early_ref,
+    lengths_ref, scal_ref, x_ref, gain_two_ref, gw_ref, part_ref, early_ref,
+    bg_in, mix_in, q_in, k_in, v_in, att_in, lse_in, cos_in, sin_in, attn_in, normed_in, hid_in, hg_in,
     layer_ref, input_ref, ff_grads, attn_ref, kv_ref, small_ref,
+    bg_ref, mix_w, q_ref, k_all, v_all, att_ref, lse_ref, cos_ref, sin_ref, attn_w, normed_ref, hid_ref, hg_ref,
     ff_y, ff_own, out_c, out_own, out_sx, out_rx, out_sz, out_rz, dk, dv, do, dq, dkv_s, dkv_r, dkv_rz, dkv_own,
     qg, one_sc, one_rc, one_keep, one_sx, one_rx, layer_own, input_own, a_other, a_own, a_y, a_z, a_sz,
     x_own, small, small_y, small_s, small_z, small_h, kv_own,
-    send_sems, recv_sems, local_sems,
+    send_sems, recv_sems, local_sems, stage_sems,
 ):
     quarter, width = x_own.shape
     half, rows = 2 * quarter, 4 * quarter
@@ -946,6 +999,14 @@
     to_y, to_x, to_core = {"dp": 1 - y}, {"head": head + 2 - 4 * xx}, {"head": head + 1 - 2 * core}
     mine, other = rows_of(xx * quarter, quarter), rows_of((1 - xx) * quarter, quarter)
     is_core = wide(core)
+    staged = {}
+    for name, source, target in (
+        ("bg", bg_in, bg_ref), ("mix", mix_in, mix_w), ("q", q_in, q_ref), ("k", k_in, k_all), ("v", v_in, v_all),
+        ("att", att_in, att_ref), ("lse", lse_in, lse_ref), ("cos", cos_in, cos_ref), ("sin", sin_in, sin_ref),
+        ("attn", attn_in, attn_w), ("normed", normed_in, normed_ref), ("hid", hid_in, hid_ref), ("hg", hg_in, hg_ref),
+    ):
+        staged[name] = pltpu.make_async_copy(source, target, stage_sems.at[len(staged)])
+        staged[name].start()
     loads = []
 
     def load(source, target):
@@ -1038,13 +1099,19 @@
 
     ff_add(3)
     ff_half(3, 0)
+    for name in ("bg", "mix"):
+        staged[name].wait()
     lax.fori_loop(0, 2, do_rows, 0)
-    attention_backward(starts_ref, q_ref, k_all, v_all, do, att_ref, lse_ref, dq, dk, dv, (0,))
+    for name in ("q", "k", "v", "att", "lse"):
+        staged[name].wait()
+    attention_backward(lengths_ref, q_ref, k_all, v_all, do, att_ref, lse_ref, dq, dk, dv, (0,))
     out_step_c(3)
     out_step_c(2)
-    attention_backward(starts_ref, q_ref, k_all, v_all, do, att_ref, lse_ref, dq, dk, dv, (1,))
+    attention_backward(lengths_ref, q_ref, k_all, v_all, do, att_ref, lse_ref, dq, dk, dv, (1,))
     dkv_s[...] = low(dv[...] * (1.0 - is_core) + dk[...] * is_core)
     dkv_core = links.to(dkv_s, dkv_r, **to_core)
+    for name in ("cos", "sin", "attn", "normed", "hid", "hg"):
+        staged[name].wait()
     for n in range(heads):
         at = slice(n * HD, (n + 1) * HD)
         qg[:, at] = low(turn(dq[:, at], cos_ref[...], -sin_ref[...]))
@@ -1216,7 +1283,7 @@
 
 
 def back(
-    starts, scal, x_rows, hidden, hidden_grad, gain_two_grad, branch_grad, attn_w, mix_w, normed, q, k_all, v_all, attended, lse,
+    lengths, scal, x_rows, hidden, hidden_grad, gain_two_grad, branch_grad, attn_w, mix_w, normed, q, k_all, v_all, attended, lse,
     cosine, sine_term, gw, out_part, early,
 ):
     quarter, width = hidden.shape
@@ -1239,6 +1306,19 @@
     ]
     small = (size,) + scal.shape[1:]
     scratch = [
+        ((rows, width), bf16),
+        (mix_w.shape, bf16),
+        (q.shape, bf16),
+        (k_all.shape, bf16),
+        (v_all.shape, bf16),
+        (attended.shape, f32),
+        (lse.shape, f32),
+        (cosine.shape, f32),
+        (sine_term.shape, f32),
+        (attn_w.shape, bf16),
+        (normed.shape, bf16),
+        (hidden.shape, f32),
+        (hidden.shape, f32),
         ((size, block_rows, columns), bf16),
         ((size, block_rows, columns), bf16),
         ((4, half, width), bf16),
@@ -1279,15 +1359,15 @@
     return pl.pallas_call(
         back_kernel,
         out_shape=[o[0] for o in outs],
-        in_specs=[pl.BlockSpec(memory_space=pltpu.SMEM), in_vmem_spec, anywhere]
-        + [in_vmem_spec] * 14
-        + [anywhere] * 3,
+        in_specs=[pl.BlockSpec(memory_space=pltpu.SMEM), in_vmem_spec, anywhere, in_vmem_spec]
+        + [anywhere] * 16,
         out_specs=[o[1] for o in outs],
         scratch_shapes=[pltpu.VMEM(*one) for one in scratch]
         + [
             pltpu.SemaphoreType.DMA((56,)),
             pltpu.SemaphoreType.DMA((56,)),
             pltpu.SemaphoreType.DMA((14,)),
+            pltpu.SemaphoreType.DMA((13,)),
         ],
         compiler_params=pltpu.CompilerParams(
             collective_id=3, has_side_effects=True, vmem_limit_bytes=62 * 1024 * 1024
@@ -1296,8 +1376,8 @@
             flops=10 * 10**9, bytes_accessed=40 * 10**6, transcendentals=10**6
         ),
     )(
-        starts, scal, x_rows, hidden, hidden_grad, gain_two_grad, branch_grad, attn_w, mix_w, normed, q, k_all, v_all, attended,
-        lse, cosine, sine_term, gw, out_part, early,
+        lengths, scal, x_rows, gain_two_grad, gw, out_part, early, branch_grad, mix_w, q, k_all, v_all, attended, lse,
+        cosine, sine_term, attn_w, normed, hidden, hidden_grad,
     )
 
 
@@ -1334,7 +1414,7 @@
 
 
 def optimizer(ff_grads, attn_grads, kv_blocks, held):
-    rows, step = attn_grads.shape[0], 16
+    rows, step = attn_grads.shape[0], 32
 
     def block(array):
         if array.ndim == 3 and array.shape[0] == 4:
@@ -1366,11 +1446,7 @@
     powers = jnp.arange(halves, dtype=jnp.float32) * (-2.0 / HD)
     frequency = jnp.power(jnp.float32(rope_base), powers)
     angles = places.astype(jnp.float32)[:, None] * frequency[None, :]
-    cosine, sine_term = jnp.cos(angles), jnp.sin(angles)
-    return (
-        jnp.concatenate([cosine, cosine], axis=1),
-        jnp.concatenate([-sine_term, sine_term], axis=1),
-    )
+    return jnp.cos(angles), jnp.sin(angles)
 
 
 def local(
@@ -1460,7 +1536,6 @@
         seq_index * local_rows + jnp.arange(local_rows, dtype=jnp.int32), local_rows, seq_count
     )
     starts = doc_starts(places, lengths)
-    half_starts = jnp.stack([starts[0], starts[local_rows // 2]])
     within = places - starts
     scale_one = lax.rsqrt(jnp.mean(x_rows * x_rows, axis=-1, keepdims=True) + norm_eps)
     normed = low(x_rows * scale_one * gain_one)
@@ -1487,7 +1562,7 @@
             jax.ShapeDtypeStruct((local_rows, wide_heads), jnp.float32),
             jax.ShapeDtypeStruct((local_rows, local_heads), jnp.float32),
         ],
-        half_starts,
+        doc_lengths,
         queries,
         all_keys,
         all_values,
@@ -1535,7 +1610,7 @@
             jax.ShapeDtypeStruct((stream_rows, HD), jnp.float32),
             jax.ShapeDtypeStruct((stream_rows, HD), jnp.float32),
         ],
-        half_starts,
+        doc_lengths,
         queries,
         all_keys,
         all_values,
@@ -1649,22 +1724,20 @@
         seq_index * local_rows + jnp.arange(local_rows, dtype=jnp.int32), local_rows, seq_count
     )
     starts = doc_starts(places, lengths)
-    half_starts = jnp.stack([starts[0], starts[local_rows // 2]])
     within = places - starts
-    cosine, sine_term = rope_tables(within)
-    scal_in = jnp.broadcast_to(wide(low(scalars_master))[None], (8, scalars_master.shape[0]))
+    cos_half, sin_half = rope_tables(within)
     (
         scal_all, attn_weight, mix_weight, ff_weight, cot_all, normed, queries, all_keys, all_values,
-        attended, log_total, hidden, normed_all,
+        attended, log_total, hidden, normed_all, cosine, sine_term,
     ) = front(
-        half_starts, scal_in, queries_master, keyvalue_master, mixing_master.T, expand_master, shrink_master.T,
-        x_low, cot_rows, cosine, sine_term, 3 * units + 64,
+        doc_lengths, scalars_master[None], queries_master, keyvalue_master, mixing_master.T, expand_master, shrink_master.T,
+        x_low, cot_rows, cos_half, sin_half, 3 * units + 64,
     )
     hidden_grad, branch_grad, gain_two_grad, ff_part, out_part, early = feed_forward(
         normed_all, ff_weight, cot_all, cot_rows, hidden, scal_all, units
     )
     layer_out, input_grad, ff_grads, attn_grads, kv_blocks, small = back(
-        half_starts, scal_all, x_low, hidden, hidden_grad, gain_two_grad, branch_grad, attn_weight, mix_weight, normed, queries,
+        doc_lengths, scal_all, x_low, hidden, hidden_grad, gain_two_grad, branch_grad, attn_weight, mix_weight, normed, queries,
         all_keys, all_values, attended, log_total, cosine, sine_term, ff_part, out_part, early,
     )
     held = (

time: 433 us -> 397 us (0.917)
  the two profiles are of different devices: /device:TPU:29 before, /device:TPU:0 now
where the time goes in v5:
time: 397 us; the launch traced here: 392 us
  Pallas kernels  380 us (96%)
  local copies, waits for them, and re-layouts  5.71 us (1%)
  other arithmetic  4.48 us (1%)
    pallas_call x1, Pallas kernels, front(): pl.pallas_call(front_kernel, out_shape=[o[0] for o in outs], in_specs=[pl...  163 us
    pallas_call x1, Pallas kernels, back(): pl.pallas_call(back_kernel, out_shape=[o[0] for o in outs], in_specs=[pl....  122 us
    pallas_call x1, Pallas kernels, feed_forward(): pl.pallas_call(ff_kernel, out_shape=[o[0] for o in outs], in_specs=[anywh...  72.7 us
    pallas_call x1, Pallas kernels, optimizer(): pl.pallas_call(optimizer_kernel, grid=(rows // step,), out_shape=outs, in...  22 us

profile of v5, /device:TPU:0, one launch (start us, length us, event | category | flops | bytes accessed | tf_op | source)
XLA Modules:
  0.0 392.2 jit_solution(8065624165187605453)
XLA Ops:
  0.7 1.3 fusion.10
  3.3 1.3 subtract_convert_fusion
  4.6 1.3 broadcast_in_dim.19.scal_own
  5.9 1.8 multiply_sine_fusion
  7.7 162.7 %shard_map.452 = (f32[8,8,640]{2,1,0:T(8,128)}, bf16[1536,640]{1,0:T(8,128)(2,1)}, bf16[1536,384]{1,0:T(8,128)(2,1)}, bf16[1536,1792]{1,0:T(8,128)(2,1)}, bf16[2...) custom-call(s32[1,2]{1,0:T(1,128)} %lengths_ref.3, ...), custom_call_target="tpu_custom_call" | custom-call | flops 6000000000 | bytes 30000000 | tf_op jit(solution)/shard_map/pallas_call | solution.py:725
  170.4 72.7 %shard_map.453 = (f32[128,1536]{1,0:T(8,128)}, bf16[512,1536]{1,0:T(8,128)(2,1)}, f32[1,1536]{1,0:T(1,128)}, bf16[1536,1792]{1,0:T(8,128)(2,1)}, bf16[2048,1536]{1,0:T(8,128)(2,1)}, /*index=5*/bf16[192,1792]{1,0:T(8,128)(2,1)}) custom-call(bf16[2048,1536]{1,0:T(8,128)(2,1)} %get-tuple-element.85.nt_ref, bf16[1536,1792]{1,0:T(8,128)(2,1)} %get-tuple-element.86.ff_w, ...), custom_call_target="tpu_custom_call" | custom-call | flops 32999999488 | bytes 40000000 | tf_op jit(solution)/shard_map/pallas_call | solution.py:944
  243.2 0.0 copy-start.2
  243.2 0.0 copy-start.4
  243.2 0.0 copy-start.5
  243.2 122.2 %shard_map.454 = (bf16[512,1536]{1,0:T(8,128)(2,1)}, bf16[512,1536]{1,0:T(8,128)(2,1)}, bf16[4,192,1792]{2,1,0:T(8,128)(2,1)}, f32[192,896]{1,0:T(8,128)}, bf16[...) custom-call(s32[1,2]{1,0:T(1,128)} %lengths_ref.3, f32[8,8,640]{2,1,0:T(8,128)} %get-tuple-element.84.scal_ref, ...), custom_call_target="tpu_custom_call" | custom-call | flops 10000000000 | bytes 40000000 | tf_op jit(solution)/shard_map/pallas_call | solution.py:1359
  365.4 0.7 fusion.2
  366.1 0.0 copy-done.2
  366.1 0.0 copy-done.4
  366.2 0.0 copy-done.5
  366.2 0.0 copy-start.3
  366.2 0.6 fusion.8
  366.8 0.0 copy-start.1
  366.8 22.0 %shard_map.455 = (f32[192,384]{1,0:T(8,128)}, f32[192,384]{1,0:T(8,128)}, f32[192,384]{1,0:T(8,128)}, f32[192,384]{1,0:T(8,128)}, bf16[192,384]{1,0:T(8,128)(2,1...) custom-call(bf16[4,192,1792]{2,1,0:T(8,128)(2,1)} %get-tuple-element, ...), custom_call_target="tpu_custom_call" | custom-call | flops 30000000 | bytes 50000000 | tf_op jit(solution)/shard_map/pallas_call | solution.py:1431
  388.8 0.0 copy-done.3
  388.8 0.0 copy-start
  388.9 0.0 copy-done.1
  388.9 1.1 copy.55
  390.0 0.8 copy-done
  390.8 1.1 copy.56
  (1 shorter events, 0.0 us)
Async XLA Ops:
  243.2 123.0 %copy-start.2 = (f32[640]{0:T(1024)S(1)}, f32[640]{0:T(1024)}, u32[]{:S(2)}) copy-start(f32[640]{0:T(1024)} %param.39) | copy-start | bytes 7684
  243.2 123.0 %copy-start.4 = (f32[640]{0:T(1024)S(1)}, f32[640]{0:T(1024)}, u32[]{:S(2)}) copy-start(f32[640]{0:T(1024)} %param.41) | copy-start | bytes 7684
  243.2 123.0 %copy-start.5 = (f32[640]{0:T(1024)S(1)}, f32[640]{0:T(1024)}, u32[]{:S(2)}) copy-start(f32[640]{0:T(1024)} %param.40) | copy-start | bytes 7684
  366.2 22.7 %copy-start.3 = (f32[640]{0:T(1024)}, f32[640]{0:T(1024)S(1)}, u32[]{:S(2)}) copy-start(f32[640]{0:T(1024)S(1)} %fusion.2) | copy-start | bytes 7684
  366.8 22.1 %copy-start.1 = (bf16[512,1536]{1,0:T(8,128)(2,1)S(1)}, bf16[512,1536]{1,0:T(8,128)(2,1)}, u32[]{:S(2)}) copy-start(bf16[512,1536]{1,0:T(8,128)(2,1)} %get-tuple-element.105) | copy-start | bytes 4718596
  388.8 2.0 copy-start

commit v6 on v5

--- a/solution.py
+++ b/solution.py
@@ -450,9 +450,8 @@
     kv_head = lax.div(head * heads, H // KV)
     own_rows = rows_of(me * block_rows, block_rows)
     attn_w[own_rows, :wide_heads] = low(query_ref[...])
-    for i, column in enumerate((kv_head, KV + kv_head)):
-        columns = pl.ds(pl.multiple_of(column * HD, HD), HD)
-        attn_w[own_rows, wide_heads + i * HD : wide_heads + (i + 1) * HD] = low(kv_ref[:, columns])
+    kv_columns = pl.ds(pl.multiple_of((core * KV + kv_head) * HD, HD), HD)
+    attn_w[own_rows, wide_heads:] = low(kv_ref[:, kv_columns])
     mix_w[own_rows, :] = low(mixing_ref[...])
     scal_z = {d: links.to(scal_in, scal_ref.at[me], seq=owners[d]) for d in (1, 2, 3)}
     scal_y = [links.to(scal_in, scal_ref.at[me], **to_y)]
@@ -557,18 +556,23 @@
 
     base = 2 * width + H * HD
     bias_q = vector_of(scal_ref, 2 * width + head * wide_heads, wide_heads)
-    bias_k = vector_of(scal_ref, base + kv_head * HD, HD)
-    bias_v = vector_of(scal_ref, base + (KV + kv_head) * HD, HD)
-    own_k, own_v = at_rows(k_all, z, rows), at_rows(v_all, z, rows)
+    bias_kv = vector_of(scal_ref, base + (core * KV + kv_head) * HD, HD)
 
     def project(i, unused):
         part = rows_of(i * half, half)
         normed = normed_ref[part, :]
         cosine, sine_term = cos_ref[part, :], sin_ref[part, :]
-        pre = dot_nn(normed, attn_w[:, wide_heads:])
+        pre = dot_nn(normed, attn_w[:, wide_heads:]) + bias_kv
         own = rows_of(z * rows + i * half, half)
-        k_all[own, :] = low(turn(pre[:, :HD] + bias_k, cosine, sine_term))
-        v_all[own, :] = low(pre[:, HD:] + bias_v)
+
+        @pl.when(core == 0)
+        def _():
+            k_all[own, :] = low(turn(pre, cosine, sine_term))
+
+        @pl.when(core == 1)
+        def _():
+            v_all[own, :] = low(pre)
+
         pre = dot_nn(normed, attn_w[:, :wide_heads]) + bias_q
         for n in range(heads):
             at = slice(n * HD, (n + 1) * HD)
@@ -593,7 +597,7 @@
         return copy
 
     kv_z = {d: keys_or_values(z, {"seq": owners[d]}) for d in (3, 2, 1)}
-    kv_core = []
+    kv_core = [keys_or_values(z, to_core)]
     ff_start(1, 0)
     ff_start(1, 1)
     ff_start(3, 0)
@@ -702,7 +706,7 @@
     shape = jax.ShapeDtypeStruct
     in_vmem_spec, anywhere = pl.BlockSpec(memory_space=pltpu.VMEM), pl.BlockSpec(memory_space=pl.ANY)
     staged = [
-        shape((count * block_rows, wide_heads + 2 * HD), bf16),
+        shape((count * block_rows, wide_heads + HD), bf16),
         shape((count * block_rows, wide_heads), bf16),
         shape((rows, width), bf16),
         shape((rows, wide_heads), bf16),
@@ -1132,12 +1136,11 @@
     ff_half(3, 1)
     turned = turn(total, cos_ref[...], -sin_ref[...])
     dkv_own[0] = low(turned * (1.0 - is_core) + total * is_core)
-    key_columns = pl.ds(pl.multiple_of(wide_heads + core * HD, HD), HD)
 
     def one_part(begin):
         part = rows_of(begin, quarter)
         return dot_nt(qg[part, :], attn_w[:, :wide_heads]) + dot_nt(
-            dkv_own[0, part, :], attn_w[:, key_columns]
+            dkv_own[0, part, :], attn_w[:, wide_heads:]
         )
 
     def one_send(i, unused):

time: 397 us -> 394 us (level)
  no operation moved by 1% of the time
where the time goes in v6:
time: 394 us; the launch traced here: 389 us
  Pallas kernels  377 us (96%)
  local copies, waits for them, and re-layouts  5.71 us (1%)
  other arithmetic  4.48 us (1%)
    pallas_call x1, Pallas kernels, front(): pl.pallas_call(front_kernel, out_shape=[o[0] for o in outs], in_specs=[pl...  160 us
    pallas_call x1, Pallas kernels, back(): pl.pallas_call(back_kernel, out_shape=[o[0] for o in outs], in_specs=[pl....  122 us
    pallas_call x1, Pallas kernels, feed_forward(): pl.pallas_call(ff_kernel, out_shape=[o[0] for o in outs], in_specs=[anywh...  72.8 us
    pallas_call x1, Pallas kernels, optimizer(): pl.pallas_call(optimizer_kernel, grid=(rows // step,), out_shape=outs, in...  22 us

profile of v6, /device:TPU:0, one launch (start us, length us, event | category | flops | bytes accessed | tf_op | source)
XLA Modules:
  0.0 389.1 jit_solution(1752949471282938692)
XLA Ops:
  0.7 1.3 fusion.10
  3.3 1.3 subtract_convert_fusion
  4.6 1.3 broadcast_in_dim.19.scal_own
  5.9 1.8 multiply_sine_fusion
  7.7 159.7 %shard_map.452 = (f32[8,8,640]{2,1,0:T(8,128)}, bf16[1536,512]{1,0:T(8,128)(2,1)}, bf16[1536,384]{1,0:T(8,128)(2,1)}, bf16[1536,1792]{1,0:T(8,128)(2,1)}, bf16[2...) custom-call(s32[1,2]{1,0:T(1,128)} %lengths_ref.3, ...), custom_call_target="tpu_custom_call" | custom-call | flops 6000000000 | bytes 30000000 | tf_op jit(solution)/shard_map/pallas_call | solution.py:729
  167.4 72.8 %shard_map.453 = (f32[128,1536]{1,0:T(8,128)}, bf16[512,1536]{1,0:T(8,128)(2,1)}, f32[1,1536]{1,0:T(1,128)}, bf16[1536,1792]{1,0:T(8,128)(2,1)}, bf16[2048,1536]{1,0:T(8,128)(2,1)}, /*index=5*/bf16[192,1792]{1,0:T(8,128)(2,1)}) custom-call(bf16[2048,1536]{1,0:T(8,128)(2,1)} %get-tuple-element.85.nt_ref, bf16[1536,1792]{1,0:T(8,128)(2,1)} %get-tuple-element.86.ff_w, ...), custom_call_target="tpu_custom_call" | custom-call | flops 32999999488 | bytes 40000000 | tf_op jit(solution)/shard_map/pallas_call | solution.py:948
  240.2 0.0 copy-start.2
  240.2 0.0 copy-start.4
  240.2 0.0 copy-start.5
  240.2 122.0 %shard_map.454 = (bf16[512,1536]{1,0:T(8,128)(2,1)}, bf16[512,1536]{1,0:T(8,128)(2,1)}, bf16[4,192,1792]{2,1,0:T(8,128)(2,1)}, f32[192,896]{1,0:T(8,128)}, bf16[...) custom-call(s32[1,2]{1,0:T(1,128)} %lengths_ref.3, f32[8,8,640]{2,1,0:T(8,128)} %get-tuple-element.84.scal_ref, ...), custom_call_target="tpu_custom_call" | custom-call | flops 10000000000 | bytes 40000000 | tf_op jit(solution)/shard_map/pallas_call | solution.py:1362
  362.2 0.7 fusion.2
  363.0 0.0 copy-done.2
  363.0 0.0 copy-done.4
  363.0 0.0 copy-done.5
  363.0 0.0 copy-start.3
  363.0 0.6 fusion.8
  363.6 0.0 copy-start.1
  363.6 22.0 %shard_map.455 = (f32[192,384]{1,0:T(8,128)}, f32[192,384]{1,0:T(8,128)}, f32[192,384]{1,0:T(8,128)}, f32[192,384]{1,0:T(8,128)}, bf16[192,384]{1,0:T(8,128)(2,1...) custom-call(bf16[4,192,1792]{2,1,0:T(8,128)(2,1)} %get-tuple-element, ...), custom_call_target="tpu_custom_call" | custom-call | flops 30000000 | bytes 50000000 | tf_op jit(solution)/shard_map/pallas_call | solution.py:1434
  385.7 0.0 copy-done.3
  385.7 0.0 copy-start
  385.7 0.0 copy-done.1
  385.7 1.1 copy.55
  386.8 0.8 copy-done
  387.7 1.1 copy.56
  (1 shorter events, 0.0 us)
Async XLA Ops:
  240.2 122.8 %copy-start.2 = (f32[640]{0:T(1024)S(1)}, f32[640]{0:T(1024)}, u32[]{:S(2)}) copy-start(f32[640]{0:T(1024)} %param.39) | copy-start | bytes 7684
  240.2 122.8 %copy-start.4 = (f32[640]{0:T(1024)S(1)}, f32[640]{0:T(1024)}, u32[]{:S(2)}) copy-start(f32[640]{0:T(1024)} %param.41) | copy-start | bytes 7684
  240.2 122.8 %copy-start.5 = (f32[640]{0:T(1024)S(1)}, f32[640]{0:T(1024)}, u32[]{:S(2)}) copy-start(f32[640]{0:T(1024)} %param.40) | copy-start | bytes 7684
  363.0 22.7 %copy-start.3 = (f32[640]{0:T(1024)}, f32[640]{0:T(1024)S(1)}, u32[]{:S(2)}) copy-start(f32[640]{0:T(1024)S(1)} %fusion.2) | copy-start | bytes 7684
  363.6 22.1 %copy-start.1 = (bf16[512,1536]{1,0:T(8,128)(2,1)S(1)}, bf16[512,1536]{1,0:T(8,128)(2,1)}, u32[]{:S(2)}) copy-start(bf16[512,1536]{1,0:T(8,128)(2,1)} %get-tuple-element.105) | copy-start | bytes 4718596
  385.7 2.0 copy-start
